TPU v7x, 32 devices: a whole 2x2x4 slice. The times are simulated.
32 devices in a mesh: dp: 8 (over z, y), tensor: 4 (over x, core).
Axes of the slice: x: 2, y: 2, z: 4, core: 2. Of those that a mesh axis runs over, the one named last changes fastest.
Arguments:
- layer_input: bfloat16 [16384, 1536], P('dp'), may hold values from -6 to 6
- segments: int32 [16384], P('dp'), may hold values from 0 to 2048, as said below
- routes: int32 [16384, 8], P(('dp', 'tensor')), may hold values from 0 to 31, all different within a row; in each aligned block of 512 rows (0 to 511, 512 to 1023, ...) at most 160 rows name the same one
- norm1_gain: bfloat16 [1536], replicated, may hold values from 0.5 to 1.5
- w_query: bfloat16 [1536, 1536], P(None, 'tensor'), may hold values from -0.15625 to 0.15625
- w_key: bfloat16 [1536, 512], P(None, 'tensor'), may hold values from -0.15625 to 0.15625
- w_value: bfloat16 [1536, 512], P(None, 'tensor'), may hold values from -0.15625 to 0.15625
- w_output: bfloat16 [1536, 1536], P('tensor'), may hold values from -2.5 to 2.5
- norm2_gain: bfloat16 [1536], replicated, may hold values from 0.5 to 1.5
- router: bfloat16 [1536, 32], replicated, may hold values from -0.078125 to 0.078125
- w_gate: bfloat16 [32, 1536, 512], P('dp'), may hold values from -0.15625 to 0.15625
- w_up: bfloat16 [32, 1536, 512], P('dp'), may hold values from -0.15625 to 0.15625
- w_down: bfloat16 [32, 512, 1536], P('dp'), may hold values from -0.75 to 0.75
- cotangent: bfloat16 [16384, 1536], P(('dp', 'tensor')), may hold values from -6 to 6
Outputs:
- layer_out: bfloat16 [16384, 1536], P(('dp', 'tensor'))
- input_grad: float32 [16384, 1536], P(('dp', 'tensor'))
- norm1_grad: float32 [1536], P(('dp', 'tensor'))
- query_grad: float32 [1536, 1536], P('dp', 'tensor')
- key_grad: float32 [1536, 512], P('dp', 'tensor')
- value_grad: float32 [1536, 512], P('dp', 'tensor')
- output_grad: float32 [1536, 1536], P('tensor', 'dp')
- norm2_grad: float32 [1536], P(('dp', 'tensor'))
- router_grad: float32 [1536, 32], P(('dp', 'tensor'))
- gate_grad: float32 [32, 1536, 512], P('dp', 'tensor')
- up_grad: float32 [32, 1536, 512], P('dp', 'tensor')
- down_grad: float32 [32, 512, 1536], P('dp', None, 'tensor')
Inputs may be any that keep to these rules, and one draw needn't show every extreme that they name: `segments`: within each sequence of 2048 tokens the numbers never fall until its last 1 to 256 tokens, which are 0; 0 appears nowhere else. In each sequence the last document before the padding is numbered 2048. `routes`: each token names 8 different experts. Among the 512 tokens of one device (aligned blocks of rows) no expert is named more than 160 times, a bound that some block reaches.
All inputs are finite; a program needn't handle non-finite values.
Results may differ from a plain program's by a relative error of at most 0.025.
Values may be sent and summed in bfloat16 or wider, within the bound.
No kernel may reach another device: no remote copies, remote signals or barrier semaphores. Data moves between devices by JAX's collectives and lax.ppermute only.
A program may use at most 384 MiB of HBM per device.

v0:
```python
import jax
import jax.numpy as jnp
from jax import lax
from jax.sharding import PartitionSpec as P

HD = 64
WINDOW = 1024
SEQ = 2048


epsilon = 1e-05
highest = lax.Precision.HIGHEST


def rotate(values, places, direction):
    half_dim = values.shape[-1] // 2
    frequency = 10000.0 ** (-jnp.arange(half_dim).astype(jnp.float32) / half_dim)
    angles = places.astype(jnp.float32)[:, None] * frequency[None, :]
    cos_table = jnp.cos(angles)[:, None, :]
    sin_table = direction * jnp.sin(angles)[:, None, :]
    lower_half = values[..., :half_dim]
    upper_half = values[..., half_dim:]
    return jnp.concatenate(
        [
            lower_half * cos_table - upper_half * sin_table,
            upper_half * cos_table + lower_half * sin_table,
        ],
        axis=-1,
    )


def slot_tables(route_rows, experts, capacity):
    flat_routes = route_rows.reshape(-1)
    slot_count = flat_routes.shape[0]
    one_hot = (flat_routes[:, None] == jnp.arange(experts, dtype=jnp.int32)[None, :]).astype(
        jnp.int32
    )
    earlier = jnp.cumsum(one_hot, axis=0) - one_hot
    slot_rank = jnp.sum(earlier * one_hot, axis=1)
    places = flat_routes * capacity + slot_rank
    filled = (
        jnp.full((experts * capacity,), slot_count, jnp.int32)
        .at[places]
        .set(jnp.arange(slot_count, dtype=jnp.int32))
    )
    return (places, filled)


def per_device(
    layer_input,
    segments,
    routes,
    norm1_gain,
    w_query,
    w_key,
    w_value,
    w_output,
    norm2_gain,
    router,
    w_gate,
    w_up,
    w_down,
    cotangent,
):
    tokens_dev = layer_input.shape[0]
    model_width = layer_input.shape[1]
    quarter = routes.shape[0]
    top_count = routes.shape[1]
    tensor_rank = lax.axis_index("tensor")
    kv_local = w_key.shape[1] // HD
    q_local = w_query.shape[1] // HD
    group_size = q_local // kv_local
    experts = router.shape[1]
    local_experts = w_gate.shape[0]
    owners = experts // local_experts
    capacity = quarter * top_count * 5 // (4 * experts)
    hidden_width = w_gate.shape[2]
    block_rows = min(512, tokens_dev)
    block_count = tokens_dev // block_rows
    key_rows = block_rows + WINDOW
    scaling = HD ** (-0.5)
    f32 = jnp.float32
    bf16 = jnp.bfloat16
    input_f32 = layer_input.astype(f32)
    inv_rms1 = lax.rsqrt(jnp.mean(input_f32 * input_f32, axis=-1, keepdims=True) + epsilon)
    gain_one = norm1_gain.astype(f32)
    normed1 = (input_f32 * inv_rms1 * gain_one).astype(bf16)
    q_pre = jnp.dot(normed1, w_query, preferred_element_type=f32).reshape(tokens_dev, q_local, HD)
    k_pre = jnp.dot(normed1, w_key, preferred_element_type=f32).reshape(tokens_dev, kv_local, HD)
    v_pre = jnp.dot(normed1, w_value, preferred_element_type=f32).reshape(tokens_dev, kv_local, HD)
    places = jnp.arange(tokens_dev, dtype=jnp.int32) % SEQ
    q_rot = rotate(q_pre, places, 1.0).astype(bf16)
    k_rot = rotate(k_pre, places, 1.0).astype(bf16)
    v_low = v_pre.astype(bf16)
    pad_keys = jnp.zeros((WINDOW, kv_local, HD), bf16)
    k_padded = jnp.concatenate([pad_keys, k_rot], axis=0)
    v_padded = jnp.concatenate([pad_keys, v_low], axis=0)
    seg_padded = jnp.concatenate([jnp.zeros((WINDOW,), jnp.int32), segments], axis=0)

    def block_scores(offset):
        row_ids = offset + jnp.arange(block_rows, dtype=jnp.int32)
        key_ids = offset - WINDOW + jnp.arange(key_rows, dtype=jnp.int32)
        row_seg = lax.dynamic_slice_in_dim(segments, offset, block_rows)
        key_seg = lax.dynamic_slice_in_dim(seg_padded, offset, key_rows)
        allowed = (
            (key_ids[None, :] >= 0)
            & (key_ids[None, :] <= row_ids[:, None])
            & (row_ids[:, None] - key_ids[None, :] < WINDOW)
        )
        allowed = allowed & (key_ids[None, :] // SEQ == row_ids[:, None] // SEQ)
        allowed = allowed & (key_seg[None, :] == row_seg[:, None]) & (row_seg[:, None] != 0)
        allowed = allowed | (key_ids[None, :] == row_ids[:, None])
        q_block = lax.dynamic_slice_in_dim(q_rot, offset, block_rows).reshape(
            block_rows, kv_local, group_size, HD
        )
        k_block = lax.dynamic_slice_in_dim(k_padded, offset, key_rows)
        v_block = lax.dynamic_slice_in_dim(v_padded, offset, key_rows)
        raw_scores = (
            jnp.einsum("qgjd,kgd->gjqk", q_block, k_block, preferred_element_type=f32) * scaling
        )
        return (jnp.where(allowed[None, None], raw_scores, -jnp.inf), q_block, k_block, v_block)

    def forward_block(running, offset):
        scores, q_block, k_block, v_block = block_scores(offset)
        row_max = jnp.max(scores, axis=-1, keepdims=True)
        row_total = jnp.sum(jnp.exp(scores - row_max), axis=-1, keepdims=True)
        log_total = row_max + jnp.log(row_total)
        prob_low = jnp.exp(scores - log_total).astype(bf16)
        head_out = jnp.einsum("gjqk,kgd->qgjd", prob_low, v_block, preferred_element_type=f32)
        return (running, (head_out.astype(bf16), log_total))

    offsets = jnp.arange(block_count, dtype=jnp.int32) * block_rows
    _, (head_blocks, log_totals) = lax.scan(forward_block, jnp.int32(0), offsets)
    heads_low = head_blocks.reshape(tokens_dev, q_local * HD)
    branch = lax.psum_scatter(
        jnp.dot(heads_low, w_output, preferred_element_type=f32).astype(jnp.bfloat16),
        "tensor",
        scatter_dimension=0,
        tiled=True,
    ).astype(jnp.float32)
    row_start = tensor_rank * quarter
    own_input = lax.dynamic_slice_in_dim(input_f32, row_start, quarter)
    middle = own_input + branch
    inv_rms2 = lax.rsqrt(jnp.mean(middle * middle, axis=-1, keepdims=True) + epsilon)
    gain_two = norm2_gain.astype(f32)
    normed2 = (middle * inv_rms2 * gain_two).astype(bf16)
    logits = jnp.dot(normed2, router, preferred_element_type=f32)
    route_hot = (routes[:, :, None] == jnp.arange(experts, dtype=jnp.int32)[None, None, :]).astype(
        f32
    )
    chosen = jnp.einsum("tke,te->tk", route_hot, logits, precision=highest)
    mixing = jax.nn.softmax(chosen, axis=-1)
    places_slot, filled = slot_tables(routes, experts, capacity)
    padded_rows = jnp.concatenate([normed2, jnp.zeros((1, model_width), bf16)], axis=0)
    send_rows = jnp.take(padded_rows, filled // top_count, axis=0).reshape(
        owners, local_experts, capacity, model_width
    )
    out_grad = cotangent.astype(f32)
    d_slots = (
        (mixing[:, :, None] * out_grad[:, None, :])
        .astype(bf16)
        .reshape(quarter * top_count, model_width)
    )
    padded_grads = jnp.concatenate([d_slots, jnp.zeros((1, model_width), bf16)], axis=0)
    send_grads = jnp.take(padded_grads, filled, axis=0).reshape(
        owners, local_experts, capacity, model_width
    )
    arrived_part = lax.all_to_all(send_rows, "dp", split_axis=0, concat_axis=0, tiled=True)
    gate_in = jnp.einsum("secd,edh->sech", arrived_part, w_gate, preferred_element_type=f32)
    up_in = jnp.einsum("secd,edh->sech", arrived_part, w_up, preferred_element_type=f32)
    act_rows = (jax.nn.silu(gate_in) * up_in).astype(bf16)
    result_rows = jnp.einsum("sech,ehd->secd", act_rows, w_down, preferred_element_type=f32).astype(
        bf16
    )
    gate_in, up_in, act_rows, result_rows = (gate_in, up_in, act_rows, result_rows)
    returned = lax.all_to_all(result_rows, "dp", split_axis=0, concat_axis=0, tiled=True)
    arrived_grads = lax.all_to_all(send_grads, "dp", split_axis=0, concat_axis=0, tiled=True)
    d_act = jnp.einsum("secd,ehd->sech", arrived_grads, w_down, preferred_element_type=f32)
    gate_sig = jax.nn.sigmoid(gate_in)
    up_back = (d_act * jax.nn.silu(gate_in)).astype(bf16)
    gate_back = (d_act * up_in * gate_sig * (1.0 + gate_in * (1.0 - gate_sig))).astype(bf16)
    rows_back = (
        jnp.einsum("sech,edh->secd", gate_back, w_gate, preferred_element_type=f32)
        + jnp.einsum("sech,edh->secd", up_back, w_up, preferred_element_type=f32)
    ).astype(bf16)
    back_rows = lax.all_to_all(rows_back, "dp", split_axis=0, concat_axis=0, tiled=True)
    returned = returned.reshape(experts * capacity, model_width)
    back_rows = back_rows.reshape(experts * capacity, model_width)
    picked = (
        jnp.take(returned, places_slot, axis=0).reshape(quarter, top_count, model_width).astype(f32)
    )
    layer_out = (middle + jnp.einsum("tk,tkd->td", mixing, picked, precision=highest)).astype(bf16)
    d_mix = jnp.einsum("tkd,td->tk", picked, out_grad, precision=highest)
    d_chosen = mixing * (d_mix - jnp.sum(mixing * d_mix, axis=-1, keepdims=True))
    d_logits = jnp.einsum("tke,tk->te", route_hot, d_chosen, precision=highest).astype(bf16)
    router_part = jnp.einsum("td,te->de", normed2, d_logits, preferred_element_type=f32)
    routed = jnp.sum(
        jnp.take(back_rows, places_slot, axis=0)
        .reshape(quarter, top_count, model_width)
        .astype(f32),
        axis=1,
    )
    gate_full = jnp.einsum("secd,sech->edh", arrived_part, gate_back, preferred_element_type=f32)
    up_full = jnp.einsum("secd,sech->edh", arrived_part, up_back, preferred_element_type=f32)
    down_full = jnp.einsum("secd,sech->edh", arrived_grads, act_rows, preferred_element_type=f32)
    packed_experts = jnp.concatenate([gate_full, up_full, down_full], axis=2)
    summed_experts = lax.psum_scatter(
        packed_experts.astype(jnp.bfloat16), "tensor", scatter_dimension=1, tiled=True
    ).astype(jnp.float32)
    gate_grad = summed_experts[:, :, :hidden_width]
    up_grad = summed_experts[:, :, hidden_width : 2 * hidden_width]
    down_grad = jnp.transpose(summed_experts[:, :, 2 * hidden_width :], (0, 2, 1))
    d_normed2 = routed + jnp.einsum("te,de->td", d_logits, router, preferred_element_type=f32)
    second_gain_part = jnp.sum(d_normed2 * middle * inv_rms2, axis=0)
    scaled_two = d_normed2 * gain_two
    d_middle = (
        out_grad
        + inv_rms2 * scaled_two
        - middle * inv_rms2**3 * jnp.mean(scaled_two * middle, axis=-1, keepdims=True)
    )
    d_branch = d_middle.astype(bf16)
    part_rows = lax.all_gather(d_branch, "tensor", axis=0, tiled=True)
    head_grads = jnp.einsum("td,hd->th", part_rows, w_output, preferred_element_type=f32)
    wo_acc = jnp.einsum("td,th->dh", part_rows, heads_low, preferred_element_type=f32)
    d_heads_low = head_grads.astype(bf16).reshape(tokens_dev, kv_local, group_size, HD)

    def backward_block(running, inputs):
        dk_padded, dv_padded = running
        offset, log_total = inputs
        scores, q_block, k_block, v_block = block_scores(offset)
        prob_rows = jnp.exp(scores - log_total)
        prob_low = prob_rows.astype(bf16)
        do_block = lax.dynamic_slice_in_dim(d_heads_low, offset, block_rows)
        d_probs = jnp.einsum("qgjd,kgd->gjqk", do_block, v_block, preferred_element_type=f32)
        row_delta = jnp.sum(prob_rows * d_probs, axis=-1, keepdims=True)
        d_scores = (prob_rows * (d_probs - row_delta)).astype(bf16)
        dq_block = (
            jnp.einsum("gjqk,kgd->qgjd", d_scores, k_block, preferred_element_type=f32) * scaling
        )
        dk_block = (
            jnp.einsum("gjqk,qgjd->kgd", d_scores, q_block, preferred_element_type=f32) * scaling
        )
        dv_block = jnp.einsum("gjqk,qgjd->kgd", prob_low, do_block, preferred_element_type=f32)
        dk_padded = lax.dynamic_update_slice_in_dim(
            dk_padded, lax.dynamic_slice_in_dim(dk_padded, offset, key_rows) + dk_block, offset, 0
        )
        dv_padded = lax.dynamic_update_slice_in_dim(
            dv_padded, lax.dynamic_slice_in_dim(dv_padded, offset, key_rows) + dv_block, offset, 0
        )
        return ((dk_padded, dv_padded), dq_block)

    zero_keys = jnp.zeros((WINDOW + tokens_dev, kv_local, HD), f32)
    (dk_padded, dv_padded), dq_blocks = lax.scan(
        backward_block, (zero_keys, zero_keys), (offsets, log_totals)
    )
    dq_low = (
        rotate(dq_blocks.reshape(tokens_dev, q_local, HD), places, -1.0)
        .astype(bf16)
        .reshape(tokens_dev, q_local * HD)
    )
    dk_low = (
        rotate(dk_padded[WINDOW:], places, -1.0).astype(bf16).reshape(tokens_dev, kv_local * HD)
    )
    dv_low = dv_padded[WINDOW:].astype(bf16).reshape(tokens_dev, kv_local * HD)
    query_part = jnp.einsum("td,th->dh", normed1, dq_low, preferred_element_type=f32)
    key_part = jnp.einsum("td,th->dh", normed1, dk_low, preferred_element_type=f32)
    value_part = jnp.einsum("td,th->dh", normed1, dv_low, preferred_element_type=f32)
    total_rows = jnp.einsum("th,dh->td", dq_low, w_query, preferred_element_type=f32)
    total_rows = total_rows + jnp.einsum("th,dh->td", dk_low, w_key, preferred_element_type=f32)
    d_normed1 = lax.psum_scatter(
        (total_rows + jnp.einsum("th,dh->td", dv_low, w_value, preferred_element_type=f32)).astype(
            jnp.bfloat16
        ),
        "tensor",
        scatter_dimension=0,
        tiled=True,
    ).astype(jnp.float32)
    own_rms = lax.dynamic_slice_in_dim(inv_rms1, row_start, quarter)
    scaled_one = d_normed1 * gain_one
    first_gain_part = jnp.sum(d_normed1 * own_input * own_rms, axis=0)
    input_grad = (
        d_middle
        + own_rms * scaled_one
        - own_input * own_rms**3 * jnp.mean(scaled_one * own_input, axis=-1, keepdims=True)
    )
    q_cols = q_local * HD
    kv_cols = kv_local * HD
    packed_dense = jnp.concatenate([query_part, key_part, value_part, wo_acc], axis=1)
    dense_sum = lax.psum_scatter(
        packed_dense.astype(jnp.bfloat16), "dp", scatter_dimension=0, tiled=True
    ).astype(jnp.float32)
    query_grad = dense_sum[:, :q_cols]
    key_grad = dense_sum[:, q_cols : q_cols + kv_cols]
    value_grad = dense_sum[:, q_cols + kv_cols : q_cols + 2 * kv_cols]
    output_grad = jnp.transpose(dense_sum[:, q_cols + 2 * kv_cols :])
    gain_pair = jnp.stack([first_gain_part, second_gain_part], axis=1)
    router_grad, gain_sums = (
        lax.psum_scatter(router_part, ("dp", "tensor"), scatter_dimension=0, tiled=True),
        lax.psum_scatter(gain_pair, ("dp", "tensor"), scatter_dimension=0, tiled=True),
    )
    return (
        layer_out,
        input_grad,
        gain_sums[:, 0],
        query_grad,
        key_grad,
        value_grad,
        output_grad,
        gain_sums[:, 1],
        router_grad,
        gate_grad,
        up_grad,
        down_grad,
    )


def solution(mesh):
    placed = (
        P("dp", None),
        P("dp"),
        P(("dp", "tensor"), None),
        P(),
        P(None, "tensor"),
        P(None, "tensor"),
        P(None, "tensor"),
        P("tensor", None),
        P(),
        P(),
        P("dp", None, None),
        P("dp", None, None),
        P("dp", None, None),
        P(("dp", "tensor"), None),
    )
    return jax.shard_map(
        per_device,
        mesh=mesh,
        in_specs=placed,
        out_specs=(
            P(("dp", "tensor"), None),
            P(("dp", "tensor"), None),
            P(("dp", "tensor")),
            P("dp", "tensor"),
            P("dp", "tensor"),
            P("dp", "tensor"),
            P("tensor", "dp"),
            P(("dp", "tensor")),
            P(("dp", "tensor"), None),
            P("dp", "tensor", None),
            P("dp", "tensor", None),
            P("dp", None, "tensor"),
        ),
        check_vma=False,
    )
```

profile of v0, /device:TPU:0, one launch (start us, length us, event | category | flops | bytes accessed | tf_op | source)
XLA Modules:
  0.0 2766.5 jit_solution(11273178910138510963)
XLA Ops:
  26.9 167.3 %while.32 = (s32[]{:T(128)}, bf16[4,512,2,3,64]{1,4,3,2,0:T(8,128)(2,1)}, f32[4,2,3,512,1]{3,2,1,4,0:T(4,128)}, s32[4]{0:T(128)}, bf16[3072,2,64]{0,2,1:T(8,128)...) while((s32[]{:T(128)}, ...), condition=%wide.region_4.5_spmd, body=%wide.region_1.4_spmd.sunk | while | flops 1269531136 | bytes 62300424 | solution.py:133
  46.9 10.8 exponential_reduce_fusion.2
  59.0 9.7 fusion.210
  80.5 8.1 fusion.209
  88.6 10.8 exponential_reduce_fusion.2
  100.8 9.7 fusion.210
  130.3 10.8 exponential_reduce_fusion.2
  142.5 9.7 fusion.210
  172.1 10.8 exponential_reduce_fusion.2
  184.2 9.7 fusion.210
  205.6 10.6 convert_element_type.220
  216.5 9.2 reduce-window.6
  227.4 15.5 scatter_custom_fusion
  243.7 22.0 reduce-scatter.15.cloned.1.call-done
  271.8 23.8 gather_fusion
  295.6 8.2 broadcast_select_fusion.1
  303.8 345.9 %all_to_all.20 = bf16[8,4,160,1536]{3,2,1,0:T(8,128)(2,1)} all-to-all(bf16[8,4,160,1536]{3,2,1,0:T(8,128)(2,1)S(1)} %broadcast_select_fusion.1), channel_id=1, replica_groups=mesh['dp'=8,'tensor'=4] {'dp'}, dimensions={0} | all-to-all | bytes 31457280 | tf_op jit(solution)/shard_map/all_to_all | solution.py:168
  649.7 15.8 fusion.75
  665.4 18.8 fusion.85
  684.3 15.2 convert_bitcast_fusion
  699.5 13.1 copy.93
  723.3 334.8 %all-to-all-done.1 = bf16[8,4,160,1536]{3,2,1,0:T(8,128)(2,1)} async-done(((bf16[8,4,160,1536]{3,2,1,0:T(8,128)(2,1)}), bf16[8,4,160,1536]{3,2,1,0:T(8,128)(2,1)}, u32[]{:S(2)}, u32[]{:S(2)}) %all-to-all-start.1) | async-done | bytes 15728672 | tf_op jit(solution)/shard_map/all_to_all | solution.py:176
  1058.1 33.0 %gather_fusion.2 = bf16[4096,1536]{1,0:T(8,128)(2,1)} fusion(bf16[5120,1536]{1,0:T(8,128)(2,1)} %bitcast.47, s32[4096]{0:T(1024)S(1)} %broadcast_clamp_fusion.1), kind=kCustom, calls=%fused_computation.clone | custom fusion | bytes 25182208 | tf_op jit(solution)/shard_map/jit(_take)/gather | solution.py:190
  1091.1 12.5 fusion.77
  1115.2 37.5 %gather_fusion.1 = bf16[5120,1536]{1,0:T(8,128)(2,1)} fusion(bf16[4097,1536]{1,0:T(8,128)(2,1)} %concatenate.45, s32[5120]{0:T(1024)S(1)} %copy-done.42), kind=kCustom, calls=%fused_computation.3 | custom fusion | bytes 31477760 | tf_op jit(solution)/shard_map/jit(_take)/gather | solution.py:165
  1152.7 8.2 broadcast_select_fusion
  1160.9 344.5 %all_to_all.21 = bf16[8,4,160,1536]{3,2,1,0:T(8,128)(2,1)} all-to-all(bf16[8,4,160,1536]{3,2,1,0:T(8,128)(2,1)S(1)} %broadcast_select_fusion), channel_id=1, replica_groups=mesh['dp'=8,'tensor'=4] {'dp'}, dimensions={0} | all-to-all | bytes 31457280 | tf_op jit(solution)/shard_map/all_to_all | solution.py:177
  1505.4 23.0 fusion.84
  1528.3 18.1 fusion.93
  1546.4 22.9 fusion.90
  1569.3 13.2 copy.95
  1591.6 14.4 fusion.79
  1606.0 321.8 %all-to-all-done.3 = bf16[8,4,160,1536]{3,2,1,0:T(8,128)(2,1)} async-done(((bf16[8,4,160,1536]{3,2,1,0:T(8,128)(2,1)}), bf16[8,4,160,1536]{3,2,1,0:T(8,128)(2,1)}, u32[]{:S(2)}, u32[]{:S(2)}) %all-to-all-start.3) | async-done | bytes 15728672 | tf_op jit(solution)/shard_map/all_to_all | solution.py:186
  1927.8 32.8 %gather_fusion.3 = bf16[4096,1536]{1,0:T(8,128)(2,1)} fusion(bf16[5120,1536]{1,0:T(8,128)(2,1)} %bitcast.57, s32[4096]{0:T(1024)S(1)} %copy-done.37), kind=kCustom, calls=%fused_computation.1.clone | custom fusion | bytes 25182208 | tf_op jit(solution)/shard_map/jit(_take)/gather | solution.py:198
  1960.6 28.9 %convert_reduce_fusion = f32[512,1536]{1,0:T(8,128)S(1)} fusion(bf16[4096,1536]{1,0:T(8,128)(2,1)} %gather_fusion.3, pred[4096]{0:T(1024)(128)(4,1)S(1)} %compare_and_fusion.2), kind=kLoop, calls=%fused_computation.114 | loop fusion | flops 18087936 | bytes 15732736 | tf_op jit(solution)/shard_map/reduce_sum | solution.py:197
  1996.9 16.5 bitcast_convert_fusion
  2013.4 15.3 bitcast_convert_fusion.1
  2028.7 15.7 bitcast_convert_fusion.2
  2044.3 14.9 pad_maximum_fusion
  2059.2 32.1 %copy.138 = bf16[4,1536,1536]{2,0,1:T(4,128)(2,1)} copy(bf16[4,1536,1536]{1,2,0:T(8,128)(2,1)} %pad_maximum_fusion) | data formatting | bytes 37748736
  2091.3 19.9 copy.157
  2122.1 375.5 %while.33 = (s32[]{:T(128)}, f32[3072,2,64]{0,2,1:T(8,128)}, f32[3072,2,64]{0,2,1:T(8,128)}, f32[4,512,2,3,64]{1,0,4,3,2:T(4,128)}, s32[4]{0:T(128)}, /*index=5*...) while((s32[]{:T(128)}, f32[3072,2,64]{0,2,1:T(8,128)}, ...), condition=%wide.region_18.20_spmd, body=%wide.region_16.19_spmd.sunk | while | flops 3100934656 | bytes 171196752 | solution.py:253
  2142.7 13.1 fusion.224
  2161.9 17.0 fusion.221
  2179.0 13.6 fusion.222
  2203.7 16.1 dynamic_update_slice.49
  2232.3 8.2 fusion.219
  2240.5 12.7 fusion.224
  2258.9 13.8 fusion.221
  2272.6 13.7 fusion.222
  2297.3 16.0 dynamic_update_slice.49
  2333.7 12.4 fusion.224
  2351.7 13.8 fusion.221
  2365.4 13.5 fusion.222
  2389.9 16.0 dynamic_update_slice.49
  2426.2 12.3 fusion.224
  2443.7 13.7 fusion.221
  2457.4 13.5 fusion.222
  2481.4 16.0 dynamic_update_slice.49
  2535.7 12.4 add_convert_fusion.1
  2550.4 8.6 reshape.937
  2558.9 9.0 copy.139
  2600.4 55.4 %reduce-scatter.17.cloned.1.call-done = bf16[512,1536]{1,0:T(8,128)(2,1)} async-done(((bf16[2048,1536]{1,0:T(8,128)(2,1)}), bf16[512,1536]{1,0:T(8,128)(2,1)}) %reduce-scatter.17.cloned.1.call-update) | async-done | bytes 1572880 | tf_op jit(solution)/shard_map/reduce_scatter | solution.py:270
  2665.8 91.3 %reduce-scatter.19.cloned.1.call-done = f32[48,2]{1,0:T(8,128)} async-done(((f32[1536,2]{1,0:T(8,128)}), f32[48,2]{1,0:T(8,128)}) %reduce-scatter.19.cloned.1.call-update) | async-done | bytes 400
  (347 shorter events, 358.6 us)
Async XLA Ops:
  7.2 191.9 %copy-start = (bf16[384,1536]{1,0:T(8,128)(2,1)S(1)}, bf16[384,1536]{1,0:T(8,128)(2,1)}, u32[]{:S(2)}) copy-start(bf16[384,1536]{1,0:T(8,128)(2,1)} %param.27) | copy-start | bytes 3538948
  7.2 258.5 %reduce-scatter.15.cloned.1.call-start = ((), (), s32[]{:S(2)}) async-start(), calls=%async_computation.10 | async-start | bytes 7864320 | tf_op jit(solution)/shard_map/reduce_scatter | solution.py:135
  7.8 6.4 copy-start.4
  8.6 7.0 copy-start.38
  12.9 2.8 copy-start.43
  15.7 4.4 copy-start.1
  15.7 2.2 copy-start.27
  17.9 2.2 copy-start.30
  24.9 2.0 copy-start.15
  194.3 10.1 copy-start.2
  194.3 10.1 copy-start.14
  205.6 10.6 copy-start.48
  216.2 53.0 %copy-start.40 = (f32[1536]{0:T(1024)}, f32[1536]{0:T(1024)S(1)}, u32[]{:S(2)}) copy-start(f32[1536]{0:T(1024)S(1)} %convert_element_type.229) | copy-start | bytes 18436
  268.5 1.7 copy-start.6
  269.2 26.4 copy-start.44
  712.6 9.6 copy-start.11
  712.6 9.6 copy-start.32
  712.6 345.5 %all-to-all-start.1 = ((bf16[8,4,160,1536]{3,2,1,0:T(8,128)(2,1)}), bf16[8,4,160,1536]{3,2,1,0:T(8,128)(2,1)}, u32[]{:S(2)}, u32[]{:S(2)}) async-start(bf16[8,4,160,1536]{3,2,1,0:T(8,128)(2,1)} %copy.93), calls=%async_computation.2 | async-start | bytes 31457280 | tf_op jit(solution)/shard_map/all_to_all | solution.py:176
  722.2 368.8 %copy-start.36 = (s32[4096]{0:T(1024)}, s32[4096]{0:T(1024)S(1)}, u32[]{:S(2)}) copy-start(s32[4096]{0:T(1024)S(1)} %broadcast_clamp_fusion.1) | copy-start | bytes 49156
  1058.1 33.0 %copy-start.17 = (bf16[512,1536]{1,0:T(8,128)(2,1)S(1)}, bf16[512,1536]{1,0:T(8,128)(2,1)}, u32[]{:S(2)}) copy-start(bf16[512,1536]{1,0:T(8,128)(2,1)} %param.33) | copy-start | bytes 4718596
  1109.6 5.6 copy-start.42
  1582.5 6.0 copy-start.35
  1582.5 345.3 %all-to-all-start.3 = ((bf16[8,4,160,1536]{3,2,1,0:T(8,128)(2,1)}), bf16[8,4,160,1536]{3,2,1,0:T(8,128)(2,1)}, u32[]{:S(2)}, u32[]{:S(2)}) async-start(bf16[8,4,160,1536]{3,2,1,0:T(8,128)(2,1)} %copy.95), calls=%async_computation.4 | async-start | bytes 31457280 | tf_op jit(solution)/shard_map/all_to_all | solution.py:186
  1588.3 523.1 %all-gather.2.cloned.1.call-start = ((), (), s32[]{:S(2)}) async-start(), calls=%async_computation.11 | async-start | bytes 7864320 | tf_op jit(solution)/shard_map/all_gather | solution.py:222
  1591.5 336.2 %copy-start.37 = (s32[4096]{0:T(1024)S(1)}, s32[4096]{0:T(1024)}, u32[]{:S(2)}) copy-start(s32[4096]{0:T(1024)} %copy-done.36) | copy-start | bytes 49156
  1960.6 29.0 %copy-start.7 = (f32[512,1536]{1,0:T(8,128)S(1)}, f32[512,1536]{1,0:T(8,128)}, u32[]{:S(2)}) copy-start(f32[512,1536]{1,0:T(8,128)} %copy-done.6) | copy-start | bytes 9437188
  1960.6 29.0 %copy-start.33 = (bf16[1536,32]{0,1:T(8,128)(2,1)S(1)}, bf16[1536,32]{0,1:T(8,128)(2,1)}, u32[]{:S(2)}) copy-start(bf16[1536,32]{0,1:T(8,128)(2,1)} %param.29) | copy-start | bytes 294916
  1960.6 29.0 %copy-start.41 = (f32[1536]{0:T(1024)S(1)}, f32[1536]{0:T(1024)}, u32[]{:S(2)}) copy-start(f32[1536]{0:T(1024)} %copy-done.40) | copy-start | bytes 18436
  1960.6 29.0 %copy-start.45 = (f32[512]{0:T(512)S(1)}, f32[512]{0:T(512)}, u32[]{:S(2)}) copy-start(f32[512]{0:T(512)} %copy-done.44) | copy-start | bytes 6148
  1989.5 1.6 copy-start.18
  1989.5 2.4 copy-start.22
  1989.6 2.4 copy-start.47
  1991.9 3.4 copy-start.12
  1995.2 553.7 %reduce-scatter.23.cloned.1.call-start = ((), (), s32[]{:S(2)}) async-start(), calls=%async_computation.15 | async-start | bytes 811008
  1996.8 553.5 %reduce-scatter.25.cloned.1.call-start = ((), (), s32[]{:S(2)}) async-start(), calls=%async_computation.16 | async-start | bytes 23592960
  2111.3 10.9 copy-start.3
  2111.3 484.5 %reduce-scatter.21.cloned.1.call-start = ((), (), s32[]{:S(2)}) async-start(), calls=%async_computation.14 | async-start | bytes 3538944
  2134.8 7.9 copy-start.23
  2179.0 13.6 copy-start.8
  2232.3 8.2 copy-start.23
  2272.6 13.7 copy-start.8
  2325.9 7.9 copy-start.23
  2365.4 13.5 copy-start.8
  2418.3 7.9 copy-start.23
  2457.4 13.5 copy-start.8
  2497.6 6.9 copy-start.9
  2497.6 6.9 copy-start.16
  2497.6 6.9 copy-start.24
  2503.1 2.2 copy-start.13
  2503.1 4.2 slice-start
  2504.5 4.1 copy-start.20
  2505.3 2.3 slice-start.1
  2508.6 3.7 slice-start.2
  2509.7 2.7 copy-start.29
  2509.7 2.7 slice-start.3
  2521.5 134.3 %reduce-scatter.17.cloned.1.call-start = ((), (), s32[]{:S(2)}) async-start(), calls=%async_computation.12 | async-start | bytes 7864320 | tf_op jit(solution)/shard_map/reduce_scatter | solution.py:270
  2521.5 7.5 copy-start.31
  2529.0 6.6 copy-start.21
  2529.1 6.6 copy-start.26
  2548.1 2.3 copy-start.46
  2548.1 209.1 %reduce-scatter.19.cloned.1.call-start = ((), (), s32[]{:S(2)}) async-start(), calls=%async_computation.13 | async-start | bytes 811008
  2567.9 6.8 copy-start.5
  2585.1 70.6 %copy-start.39 = (f32[1536]{0:T(1024)S(1)}, f32[1536]{0:T(1024)}, u32[]{:S(2)}) copy-start(f32[1536]{0:T(1024)} %copy-done.38) | copy-start | bytes 18436
  2655.7 4.7 copy-start.19
  (4 other events, 4.6 us)
Sparse Core Ops, SparseCore 0:
  204.6 61.0 reduce-scatter.14
  1995.4 44.5 all-gather.1
  2045.9 95.5 reduce-scatter.22
  2144.1 138.4 reduce-scatter.24
  2521.6 74.1 reduce-scatter.20
  2598.2 57.5 reduce-scatter.16
  2661.7 95.4 reduce-scatter.18
where the time goes:
time: 2780 us; the launch traced here: 2770 us
  waiting for transfers between devices  832 us (30%)
  blocking collectives  690 us (25%)
  matrix products  479 us (17%)
  local copies, waits for them, and re-layouts  436 us (16%)
  other arithmetic  269 us (10%)
  loops' own time  32.2 us (1%)
    all_to_all x1, blocking collectives, per_device(): lax.all_to_all(send_rows, 'dp', split_axis=0, concat_axis=0, tiled=True)  346 us
    all_to_all x1, blocking collectives, per_device(): lax.all_to_all(send_grads, 'dp', split_axis=0, concat_axis=0, tiled=True)  344 us
    all_to_all x1, waiting for transfers between devices, per_device(): lax.all_to_all(result_rows, 'dp', split_axis=0, concat_axis=0, tiled=True)  335 us
    all_to_all x1, waiting for transfers between devices, per_device(): lax.all_to_all(rows_back, 'dp', split_axis=0, concat_axis=0, tiled=True)  322 us
    unnamed x11, waiting for transfers between devices  98.3 us
    unnamed x120, local copies, waits for them, and re-layouts  96.1 us
    dynamic_update_slice x8, local copies, waits for them, and re-layouts, per_device(): lax.scan(backward_block, (zero_keys, zero_keys), (offsets, log_totals))  67.5 us
    dot_general x8, matrix products, block_scores(): jnp.einsum('qgjd,kgd->gjqk', q_block, k_block, preferred_element_type=f32)  64.4 us
  transfers between devices with their start and end apart: 9, of which 6 were waited for; matrix products, arithmetic and copies ran while one was open for 23% of the time, Pallas kernels for 0%

commit v1 on v0

v1 whole, which is shorter than its diff:
```python
import functools

import jax
import jax.numpy as jnp
import numpy as np
from jax import lax
from jax.experimental import pallas as pl
from jax.experimental.pallas import tpu as pltpu
from jax.sharding import PartitionSpec as P

HD = 64
WINDOW = 1024
SEQ = 2048
QB = 256
EPS = 1e-05
NEG = -1e30
MIB = 1 << 20
f32 = jnp.float32
bf16 = jnp.bfloat16
i32 = jnp.int32

NT = (((1,), (1,)), ((), ()))
TN = (((0,), (0,)), ((), ()))
NN = (((1,), (0,)), ((), ()))


def mm(a, b, dims=NN):
    return lax.dot_general(a, b, dims, preferred_element_type=f32)


def params(mib, n=1):
    return pltpu.CompilerParams(
        vmem_limit_bytes=mib * MIB, dimension_semantics=("arbitrary",) * n
    )


def cost(gflop, mb):
    return pl.CostEstimate(
        flops=int(gflop * 1e9), bytes_accessed=int(mb * 1e6), transcendentals=0
    )


def rope_tables():
    half = HD // 2
    freq = (10000.0 ** (-np.arange(half, dtype=np.float32) / half)).astype(np.float32)
    angles = (np.arange(SEQ, dtype=np.float32)[:, None] * freq[None, :]).astype(np.float32)
    cos, sin = np.cos(angles), np.sin(angles)
    return (
        np.concatenate([cos] * 4, axis=1).astype(np.float32),
        np.concatenate([-sin, sin] * 2, axis=1).astype(np.float32),
    )


def swap_halves(u):
    lane = lax.broadcasted_iota(i32, u.shape, 1) % HD
    return jnp.where(lane < HD // 2, pltpu.roll(u, 2 * HD - HD // 2, 1), pltpu.roll(u, HD // 2, 1))


def qkv_kernel(x_ref, gain_ref, wq_ref, wk_ref, wv_ref, cos_ref, sin_ref,
               n_ref, q_ref, k_ref, v_ref, kt_ref):
    x = x_ref[...].astype(f32)
    inv = lax.rsqrt(jnp.mean(x * x, axis=-1, keepdims=True) + EPS)
    normed = (x * inv * gain_ref[...].astype(f32)).astype(bf16)
    n_ref[...] = normed
    cos, sin = cos_ref[...], sin_ref[...]
    q = mm(normed, wq_ref[...])
    for c in range(q.shape[1] // 128):
        u = q[:, 128 * c:128 * (c + 1)]
        r = ((u * cos + swap_halves(u) * sin) * HD ** (-0.5)).astype(bf16)
        q_ref[2 * c] = r[:, :HD]
        q_ref[2 * c + 1] = r[:, HD:]
    k = mm(normed, wk_ref[...])
    v = mm(normed, wv_ref[...])
    for c in range(k.shape[1] // 128):
        u = k[:, 128 * c:128 * (c + 1)]
        r = u * cos + swap_halves(u) * sin
        rb = r.astype(bf16)
        k_ref[2 * c] = rb[:, :HD]
        k_ref[2 * c + 1] = rb[:, HD:]
        rt = jnp.transpose(r).astype(bf16)
        kt_ref[2 * c] = rt[:HD]
        kt_ref[2 * c + 1] = rt[HD:]
        vb = v[:, 128 * c:128 * (c + 1)].astype(bf16)
        v_ref[2 * c] = vb[:, :HD]
        v_ref[2 * c + 1] = vb[:, HD:]


def qkv_call(x, gain, wq, wk, wv, cos, sin):
    rows, width = x.shape
    rb = 512
    qc, kc = wq.shape[1], wk.shape[1]
    qh, kh = qc // HD, kc // HD
    per_seq = SEQ // rb
    whole = lambda shape: pl.BlockSpec(shape, lambda i: (0,) * len(shape))
    return pl.pallas_call(
        qkv_kernel,
        grid=(rows // rb,),
        in_specs=[
            pl.BlockSpec((rb, width), lambda i: (i, 0)),
            whole((1, width)), whole((width, qc)), whole((width, kc)), whole((width, kc)),
            pl.BlockSpec((rb, 128), lambda i: (i % per_seq, 0)),
            pl.BlockSpec((rb, 128), lambda i: (i % per_seq, 0)),
        ],
        out_specs=[
            pl.BlockSpec((rb, width), lambda i: (i, 0)),
            pl.BlockSpec((qh, rb, HD), lambda i: (0, i, 0)),
            pl.BlockSpec((kh, rb, HD), lambda i: (0, i, 0)),
            pl.BlockSpec((kh, rb, HD), lambda i: (0, i, 0)),
            pl.BlockSpec((kh, HD, rb), lambda i: (0, 0, i)),
        ],
        out_shape=[
            jax.ShapeDtypeStruct((rows, width), bf16),
            jax.ShapeDtypeStruct((qh, rows, HD), bf16),
            jax.ShapeDtypeStruct((kh, rows, HD), bf16),
            jax.ShapeDtypeStruct((kh, rows, HD), bf16),
            jax.ShapeDtypeStruct((kh, HD, rows), bf16),
        ],
        compiler_params=params(48),
        cost_estimate=cost(13, 20),
        name="norm_qkv",
    )(x, gain, wq, wk, wv, cos, sin)


def window_blocks():
    return WINDOW // QB + 1


def on_block(i, body):
    most = window_blocks()
    for j in range(most - 1):
        pl.when(i == j)(functools.partial(body, j + 1, 0))
    pl.when(i >= most - 1)(
        lambda: body(most, pl.multiple_of((i - (most - 1)) * QB, QB))
    )


def attend_kernel(order_ref, q_ref, k_ref, v_ref, segq_ref, segk_ref, wo_ref, *rest):
    heads_ref, lse_ref, send_ref, keep_ref, bias_ref = rest[-5:]
    step = pl.program_id(0)
    i = order_ref[step]
    qh, kh = q_ref.shape[0], k_ref.shape[0]
    group = qh // kh

    def body(blocks, start):
        span = blocks * QB
        segq = segq_ref[...]
        segq = jnp.where(segq == 0, -1, segq)
        row = lax.broadcasted_iota(i32, (QB, QB), 0)
        col = lax.broadcasted_iota(i32, (QB, QB), 1)
        for j in range(blocks):
            same = segk_ref[:, pl.ds(start + j * QB, QB)] == segq
            if j == blocks - 1:
                same = (same & (col <= row)) | (col == row)
            elif blocks == window_blocks() and j == 0:
                same = same & (row < col)
            bias_ref[:, j * QB:(j + 1) * QB] = jnp.where(same, 0.0, NEG)
        lane = lax.broadcasted_iota(i32, (QB, 128), 1)
        logs = jnp.zeros((QB, 128), f32)
        outs = []
        for g in range(kh):
            q = q_ref[g * group:(g + 1) * group].reshape(group * QB, HD)
            k = k_ref[g, pl.ds(start, span), :]
            v = v_ref[g, pl.ds(start, span), :]
            s = mm(q, k, NT).reshape(group, QB, span) + bias_ref[:, :span][None]
            top = jnp.max(s, axis=-1, keepdims=True)
            p = jnp.exp(s - top)
            total = jnp.sum(p, axis=-1, keepdims=True)
            o = mm(p.astype(bf16).reshape(group * QB, span), v).reshape(group, QB, HD)
            o = (o * (1.0 / total)).astype(bf16)
            log = top + jnp.log(total)
            for h in range(group):
                outs.append(o[h])
                logs = jnp.where(lane == g * group + h, log[h], logs)
        heads = jnp.concatenate(outs, axis=1)
        heads_ref[...] = heads
        lse_ref[...] = jnp.transpose(logs)[:lse_ref.shape[0]]
        part = mm(heads, wo_ref[...]).astype(bf16)

        @pl.when(step < 2)
        def _():
            send_ref[...] = part

        @pl.when(step >= 2)
        def _():
            keep_ref[...] = part

    on_block(i, body)


def attend_call(order, q, k, v, seg_col, seg_row, wo, held=None):
    qh, rows, _ = q.shape
    kh = k.shape[0]
    width = wo.shape[1]
    lse_rows = -(-qh // 8) * 8
    in_specs = [
        pl.BlockSpec((qh, QB, HD), lambda s, o: (0, o[s], 0)),
        pl.BlockSpec((kh, rows, HD), lambda s, o: (0, 0, 0)),
        pl.BlockSpec((kh, rows, HD), lambda s, o: (0, 0, 0)),
        pl.BlockSpec((QB, 1), lambda s, o: (o[s], 0)),
        pl.BlockSpec((1, rows), lambda s, o: (0, 0)),
        pl.BlockSpec((qh * HD, width), lambda s, o: (0, 0)),
    ]
    args = [q, k, v, seg_col, seg_row, wo]
    aliases = {}
    if held is not None:
        aliases = {1 + len(args): 0, 2 + len(args): 1}
        args += list(held)
        in_specs += [pl.BlockSpec(memory_space=pl.ANY)] * 2
    return pl.pallas_call(
        attend_kernel,
        grid_spec=pltpu.PrefetchScalarGridSpec(
            num_scalar_prefetch=1,
            grid=(4,),
            in_specs=in_specs,
            out_specs=[
                pl.BlockSpec((QB, qh * HD), lambda s, o: (o[s], 0)),
                pl.BlockSpec((lse_rows, QB), lambda s, o: (0, o[s])),
                pl.BlockSpec((QB, width), lambda s, o: (jnp.minimum(s, 1), 0)),
                pl.BlockSpec((QB, width), lambda s, o: (jnp.maximum(s - 2, 0), 0)),
            ],
            scratch_shapes=[pltpu.VMEM((QB, window_blocks() * QB), f32)],
        ),
        out_shape=[
            jax.ShapeDtypeStruct((rows, qh * HD), bf16),
            jax.ShapeDtypeStruct((lse_rows, rows), f32),
            jax.ShapeDtypeStruct((2 * QB, width), bf16),
            jax.ShapeDtypeStruct((2 * QB, width), bf16),
        ],
        input_output_aliases=aliases,
        compiler_params=params(56),
        cost_estimate=cost(17, 10),
        name="attend",
    )(order, *args)


def attend_back_kernel(last, order_ref, q_ref, k_ref, v_ref, kt_ref, segq_ref, segk_ref,
                       heads_ref, lse_ref, dba_ref, dbb_ref, wo_ref, cos_ref, sin_ref, *rest):
    if last:
        (cosk_ref, sink_ref, dk_in, dv_in, _, dq_ref, dkv_ref,
         bias_ref, dk_ref, dv_ref, p_ref, ds_ref) = rest
    else:
        dq_ref, dk_ref, dv_ref, bias_ref, p_ref, ds_ref = rest
    step = pl.program_id(0)
    i = order_ref[step]
    qh, kh = q_ref.shape[0], k_ref.shape[0]
    group = qh // kh

    @pl.when(step == 0)
    def _():
        dk_ref[...] = dk_in[...] if last else jnp.zeros_like(dk_ref)
        dv_ref[...] = dv_in[...] if last else jnp.zeros_like(dv_ref)

    def body(blocks, start):
        span = blocks * QB
        segq = segq_ref[...]
        segq = jnp.where(segq == 0, -1, segq)
        row = lax.broadcasted_iota(i32, (QB, QB), 1)
        col = lax.broadcasted_iota(i32, (QB, QB), 0)
        for j in range(blocks):
            same = segk_ref[pl.ds(start + j * QB, QB), :] == segq
            if j == blocks - 1:
                same = (same & (col <= row)) | (col == row)
            elif blocks == window_blocks() and j == 0:
                same = same & (row < col)
            bias_ref[j * QB:(j + 1) * QB, :] = jnp.where(same, 0.0, NEG)
        db = jnp.where(step < 2, dba_ref[...], dbb_ref[...])
        heads = heads_ref[...]
        dh = mm(db, wo_ref[...], NT).astype(bf16)
        prod = jnp.transpose(dh.astype(f32) * heads.astype(f32))
        dqs = []
        for g in range(kh):
            k = k_ref[g, pl.ds(start, span), :]
            v = v_ref[g, pl.ds(start, span), :]
            dos = []
            for h in range(group):
                at = g * group + h
                do = dh[:, at * HD:(at + 1) * HD]
                dos.append(do)
                delta = jnp.sum(prod[at * HD:(at + 1) * HD], axis=0, keepdims=True)
                s = mm(k, q_ref[at], NT) + bias_ref[:span]
                p = jnp.exp(s - lse_ref[at:at + 1, :])
                dp = mm(v, do, NT)
                p_ref[:span, h * QB:(h + 1) * QB] = p.astype(bf16)
                ds_ref[:span, h * QB:(h + 1) * QB] = (p * (dp - delta)).astype(bf16)
            q = q_ref[g * group:(g + 1) * group].reshape(group * QB, HD)
            dk_ref[g, pl.ds(start, span), :] += mm(ds_ref[:span], q)
            dv_ref[g, pl.ds(start, span), :] += mm(p_ref[:span], jnp.concatenate(dos, axis=0))
            dq = mm(kt_ref[g, :, pl.ds(start, span)], ds_ref[:span]) * HD ** (-0.5)
            for h in range(group):
                dqs.append(dq[:, h * QB:(h + 1) * QB])
        dq = jnp.transpose(jnp.concatenate(dqs, axis=0))
        cos, sin = cos_ref[...], sin_ref[...]
        for c in range(dq.shape[1] // 128):
            u = dq[:, 128 * c:128 * (c + 1)]
            dq_ref[:, 128 * c:128 * (c + 1)] = (u * cos - swap_halves(u) * sin).astype(bf16)

    on_block(i, body)

    if last:
        @pl.when(step == pl.num_programs(0) - 1)
        def _():
            for c in range(kh // 2):
                u = jnp.concatenate([dk_ref[2 * c], dk_ref[2 * c + 1]], axis=1)
                u = u * cosk_ref[...] - swap_halves(u) * sink_ref[...]
                dkv_ref[:, 128 * c:128 * (c + 1)] = u.astype(bf16)
                w = jnp.concatenate([dv_ref[2 * c], dv_ref[2 * c + 1]], axis=1)
                dkv_ref[:, (kh // 2 + c) * 128:(kh // 2 + c + 1) * 128] = w.astype(bf16)


def attend_back_call(order, q, k, v, kt, seg_row, seg_col, heads, lse, db_a, db_b, wo, cos, sin,
                     held=None):
    qh, rows, _ = q.shape
    kh = k.shape[0]
    width = wo.shape[1]
    span = window_blocks() * QB
    group = qh // kh
    last = held is not None
    whole = lambda shape: pl.BlockSpec(shape, lambda s, o: (0,) * len(shape))
    in_specs = [
        pl.BlockSpec((qh, QB, HD), lambda s, o: (0, o[s], 0)),
        whole((kh, rows, HD)), whole((kh, rows, HD)), whole((kh, HD, rows)),
        pl.BlockSpec((1, QB), lambda s, o: (0, o[s])),
        whole((rows, 1)),
        pl.BlockSpec((QB, qh * HD), lambda s, o: (o[s], 0)),
        pl.BlockSpec((lse.shape[0], QB), lambda s, o: (0, o[s])),
        pl.BlockSpec((QB, width), lambda s, o: (jnp.minimum(s, 1), 0)),
        pl.BlockSpec((QB, width), lambda s, o: (jnp.maximum(s - 2, 0), 0)),
        whole((qh * HD, width)),
        pl.BlockSpec((QB, 128), lambda s, o: (o[s], 0)),
        pl.BlockSpec((QB, 128), lambda s, o: (o[s], 0)),
    ]
    args = [q, k, v, kt, seg_row, seg_col, heads, lse, db_a, db_b, wo, cos, sin]
    out_specs = [pl.BlockSpec((QB, qh * HD), lambda s, o: (o[s], 0))]
    out_shape = [jax.ShapeDtypeStruct((rows, qh * HD), bf16)]
    scratch = [pltpu.VMEM((span, QB), f32)]
    aliases = {}
    if last:
        dq, dk, dv = held
        aliases = {1 + len(args) + 4: 0}
        args += [cos, sin, dk, dv, dq]
        in_specs += [whole((rows, 128)), whole((rows, 128)), whole((kh, rows, HD)),
                     whole((kh, rows, HD)), pl.BlockSpec(memory_space=pl.ANY)]
        out_specs += [whole((rows, 2 * kh * HD))]
        out_shape += [jax.ShapeDtypeStruct((rows, 2 * kh * HD), bf16)]
        scratch += [pltpu.VMEM((kh, rows, HD), f32)] * 2
    else:
        out_specs += [whole((kh, rows, HD))] * 2
        out_shape += [jax.ShapeDtypeStruct((kh, rows, HD), f32)] * 2
    scratch += [pltpu.VMEM((span, group * QB), bf16)] * 2
    return pl.pallas_call(
        functools.partial(attend_back_kernel, last),
        grid_spec=pltpu.PrefetchScalarGridSpec(
            num_scalar_prefetch=1, grid=(4,),
            in_specs=in_specs, out_specs=out_specs, scratch_shapes=scratch,
        ),
        out_shape=out_shape,
        input_output_aliases=aliases,
        compiler_params=params(58),
        cost_estimate=cost(22, 20),
        name="attend_back",
    )(order, *args)


def qkv_back_kernel(order_ref, dq_ref, dkv_ref, x_ref, wq_ref, wk_ref, wv_ref,
                    send_ref, keep_ref, gain_ref):
    step = pl.program_id(0)
    half = pl.num_programs(0) // 2
    kc = wk_ref.shape[1]
    total = (
        mm(dq_ref[...], wq_ref[...], NT)
        + mm(dkv_ref[:, :kc], wk_ref[...], NT)
        + mm(dkv_ref[:, kc:], wv_ref[...], NT)
    )

    @pl.when(step < half)
    def _():
        send_ref[...] = total.astype(bf16)

    @pl.when(step >= half)
    def _():
        keep_ref[...] = total.astype(bf16)

    x = x_ref[...].astype(f32)
    inv = lax.rsqrt(jnp.mean(x * x, axis=-1, keepdims=True) + EPS)
    gain = jnp.sum(total * (x * inv), axis=0, keepdims=True)
    gain_ref[...] = jnp.where(step == 0, gain, gain_ref[...] + gain)


def qkv_back_call(order, dq, dkv, x, wq, wk, wv):
    rows, width = x.shape
    steps = order.shape[0]
    rb = rows // steps
    half = steps // 2
    whole = lambda shape: pl.BlockSpec(shape, lambda s, o: (0,) * len(shape))
    return pl.pallas_call(
        qkv_back_kernel,
        grid_spec=pltpu.PrefetchScalarGridSpec(
            num_scalar_prefetch=1, grid=(steps,),
            in_specs=[
                pl.BlockSpec((rb, dq.shape[1]), lambda s, o: (o[s], 0)),
                pl.BlockSpec((rb, dkv.shape[1]), lambda s, o: (o[s], 0)),
                pl.BlockSpec((rb, width), lambda s, o: (o[s], 0)),
                whole(wq.shape), whole(wk.shape), whole(wv.shape),
            ],
            out_specs=[
                pl.BlockSpec((rb, width), lambda s, o: (jnp.minimum(s, half - 1), 0)),
                pl.BlockSpec((rb, width), lambda s, o: (jnp.maximum(s - half, 0), 0)),
                whole((1, width)),
            ],
        ),
        out_shape=[
            jax.ShapeDtypeStruct((rows // 2, width), bf16),
            jax.ShapeDtypeStruct((rows // 2, width), bf16),
            jax.ShapeDtypeStruct((1, width), f32),
        ],
        compiler_params=params(48),
        cost_estimate=cost(6, 20),
        name="qkv_back",
    )(order, dq, dkv, x, wq, wk, wv)


def expert_kernel(sources, cap, experts, base_ref, *refs):
    x_refs, refs = refs[:2 * sources], refs[2 * sources:]
    c_refs, refs = refs[:sources], refs[sources:]
    router_ref, wg_ref, wu_ref, wd_ref = refs[:4]
    refs = refs[-(4 * sources + 6 + 4):]
    out_refs, refs = refs[:2 * sources], refs[2 * sources:]
    back_refs, refs = refs[:2 * sources], refs[2 * sources:]
    (dmix_ref, xs_ref, cs_ref, act_ref, dg_ref, du_ref,
     mix_ref, rank_ref, so_ref, sd_ref) = refs
    e = pl.program_id(0)
    local = pl.num_programs(0)
    half = x_refs[0].shape[0]
    quarter = 2 * half
    extra = c_refs[0].shape[0] - quarter
    slots = so_ref.shape[1]
    base = base_ref[0]

    @pl.when(e == 0)
    def _():
        for s in range(sources):
            tail = c_refs[s][quarter:, :].astype(f32)
            rank = jnp.concatenate(
                [tail[:, j * quarter:(j + 1) * quarter] for j in range(-(-experts // extra))],
                axis=0,
            )[:experts].astype(i32)
            rank_ref[s] = rank
            logits = jnp.concatenate(
                [mm(router_ref[...], x_refs[2 * s + j][...], NT) for j in range(2)], axis=1
            )
            chosen = rank >= 0
            logits = jnp.where(chosen, logits, NEG)
            top = jnp.max(logits, axis=0, keepdims=True)
            ex = jnp.where(chosen, jnp.exp(logits - top), 0.0)
            mix_ref[s] = ex / jnp.sum(ex, axis=0, keepdims=True)

    slot_row = lax.broadcasted_iota(i32, (cap, quarter), 0)
    picks, mixes = [], []
    for s in range(sources):
        hot = slot_row == rank_ref[s, pl.ds(base + e, 1), :]
        pick = jnp.where(hot, 1.0, 0.0)
        picks.append(pick)
        mixes.append(jnp.sum(pick * mix_ref[s, pl.ds(base + e, 1), :], axis=1, keepdims=True))
        pick = pick.astype(bf16)
        xs_ref[0, s * cap:(s + 1) * cap, :] = (
            mm(pick[:, :half], x_refs[2 * s][...]) + mm(pick[:, half:], x_refs[2 * s + 1][...])
        ).astype(bf16)
        cs_ref[0, s * cap:(s + 1) * cap, :] = mm(pick, c_refs[s][:quarter, :]).astype(bf16)
    mix = jnp.concatenate(mixes, axis=0)
    xs, cs = xs_ref[0], cs_ref[0]
    gate, up = mm(xs, wg_ref[0]), mm(xs, wu_ref[0])
    d_act = mm(cs, wd_ref[0], NT)
    sig = jax.nn.sigmoid(gate)
    silu = gate * sig
    act = silu * up
    d_mix = jnp.sum(act * d_act, axis=1, keepdims=True)
    for s in range(sources):
        dmix_ref[s, pl.ds(e, 1), :] = jnp.sum(
            picks[s] * d_mix[s * cap:(s + 1) * cap], axis=0, keepdims=True
        )
    d_act = d_act * mix
    act = (act * mix).astype(bf16)
    du = (d_act * silu).astype(bf16)
    dg = (d_act * up * sig * (1.0 + gate * (1.0 - sig))).astype(bf16)
    act_ref[0], du_ref[0], dg_ref[0] = act, du, dg
    so = mm(act, wd_ref[0]).astype(bf16)
    sd = (mm(dg, wg_ref[0], NT) + mm(du, wu_ref[0], NT)).astype(bf16)
    at = pl.multiple_of(e * cap, 16)
    for s in range(sources):
        so_ref[s, pl.ds(at, cap), :] = so[s * cap:(s + 1) * cap]
        sd_ref[s, pl.ds(at, cap), :] = sd[s * cap:(s + 1) * cap]

    @pl.when(e == local - 1)
    def _():
        count = slots // cap
        col = lax.broadcasted_iota(i32, (quarter, slots), 1)
        for s in range(sources):
            rows = [rank_ref[s, pl.ds(base + j, 1), :] for j in range(count)]
            rows = [jnp.where(r >= 0, r + j * cap, -1) for j, r in enumerate(rows)]
            rows += [jnp.full((1, quarter), -1, i32)] * (-count % 8)
            back = jnp.transpose(jnp.concatenate(rows, axis=0))
            hot = None
            for j in range(count):
                this = back[:, j:j + 1] == col
                hot = this if hot is None else hot | this
            pick = jnp.where(hot, 1.0, 0.0).astype(bf16)
            for j in range(2):
                part = pick[j * half:(j + 1) * half]
                out_refs[2 * s + j][...] = mm(part, so_ref[s]).astype(bf16)
                back_refs[2 * s + j][...] = mm(part, sd_ref[s]).astype(bf16)


def expert_call(base, xs, cs, router_t, wg, wu, wd, cap, at, of, held=None):
    sources = len(cs)
    experts = router_t.shape[0]
    local, width, hidden = wg.shape
    half = xs[0][0].shape[0]
    quarter = 2 * half
    xs = [part for halves in xs for part in halves]
    sizes = (width, width, hidden, hidden, hidden)
    whole = lambda shape: pl.BlockSpec(shape, lambda e, b: (0,) * len(shape))
    slot_spec = lambda n: pl.BlockSpec((1, sources * cap, n), lambda e, b: (e, at, 0))
    args = [*xs, *cs, router_t, wg, wu, wd]
    in_specs = (
        [whole(a.shape) for a in (*xs, *cs, router_t)]
        + [
            pl.BlockSpec((1, width, hidden), lambda e, b: (e, 0, 0)),
            pl.BlockSpec((1, width, hidden), lambda e, b: (e, 0, 0)),
            pl.BlockSpec((1, hidden, width), lambda e, b: (e, 0, 0)),
        ]
    )
    aliases = {}
    if held is not None:
        aliases = {1 + len(args) + j: 4 * sources + 1 + j for j in range(5)}
        args += list(held)
        in_specs += [pl.BlockSpec(memory_space=pl.ANY)] * 5
    outs = pl.pallas_call(
        functools.partial(expert_kernel, sources, cap, experts),
        grid_spec=pltpu.PrefetchScalarGridSpec(
            num_scalar_prefetch=1,
            grid=(local,),
            in_specs=in_specs,
            out_specs=[whole((half, width))] * (4 * sources)
            + [whole((sources, local, quarter))]
            + [slot_spec(n) for n in sizes],
            scratch_shapes=[
                pltpu.VMEM((sources, experts, quarter), f32),
                pltpu.VMEM((sources, experts, quarter), i32),
                pltpu.VMEM((sources, local * cap, width), bf16),
                pltpu.VMEM((sources, local * cap, width), bf16),
            ],
        ),
        out_shape=[jax.ShapeDtypeStruct((half, width), bf16)] * (4 * sources)
        + [jax.ShapeDtypeStruct((sources, local, quarter), f32)]
        + [jax.ShapeDtypeStruct((local, of * cap, n), bf16) for n in sizes],
        input_output_aliases=aliases,
        compiler_params=params(60),
        cost_estimate=cost(14 * sources, 20),
        name="experts",
    )(base, *args)
    halves = lambda a: [(a[2 * s], a[2 * s + 1]) for s in range(sources)]
    return (
        halves(outs[:2 * sources]),
        halves(outs[2 * sources:4 * sources]),
        outs[4 * sources],
        outs[4 * sources + 1:],
    )


def weight_grad_kernel(order_ref, a_ref, b_ref, send_ref, keep_ref):
    part = mm(a_ref[0], b_ref[0], TN).astype(bf16)
    step = pl.program_id(0)

    @pl.when(step < 2)
    def _():
        send_ref[0, 0] = part

    @pl.when(step >= 2)
    def _():
        keep_ref[0, 0] = part


def weight_grad_call(order, a, b):
    local, slots, width = a.shape
    hidden = b.shape[2]
    cut = width // 4
    shape = jax.ShapeDtypeStruct((2, local, cut, hidden), bf16)
    return pl.pallas_call(
        weight_grad_kernel,
        grid_spec=pltpu.PrefetchScalarGridSpec(
            num_scalar_prefetch=1,
            grid=(4, local),
            in_specs=[
                pl.BlockSpec((1, slots, cut), lambda s, e, o: (e, 0, o[s])),
                pl.BlockSpec((1, slots, hidden), lambda s, e, o: (e, 0, 0)),
            ],
            out_specs=[
                pl.BlockSpec(
                    (1, 1, cut, hidden),
                    lambda s, e, o: (jnp.minimum(s, 1), jnp.where(s < 2, e, local - 1), 0, 0),
                ),
                pl.BlockSpec(
                    (1, 1, cut, hidden),
                    lambda s, e, o: (jnp.maximum(s - 2, 0), jnp.where(s < 2, 0, e), 0, 0),
                ),
            ],
        ),
        out_shape=[shape, shape],
        compiler_params=params(40, 2),
        cost_estimate=cost(10, 20),
        name="weight_grad",
    )(order, a, b)


def ring_of(n):
    return list(range(0, n, 2)) + list(range(n - 1, 0, -2))


def ring_moves(n):
    ring = ring_of(n)
    ahead = [(ring[p], ring[(p + 1) % n]) for p in range(n)]
    return ahead, [(b, a) for a, b in ahead]


def add_low(a, b):
    return (a.astype(f32) + b.astype(f32)).astype(bf16)


def ring_gather(own, n, split):
    ahead, behind = ring_moves(n)
    if split:
        cut = own.shape[0] // 2
        own = (own[:cut], own[cut:])
    else:
        cut = own.shape[0] // 32 * 16
        own = (own,)
    a = b = own
    got = []
    for _ in range(n // 2 - 1):
        a = tuple(lax.ppermute(v, "dp", ahead) for v in a)
        b = tuple(lax.ppermute(v, "dp", behind) for v in b)
        got.append([a, b] if split else [a[0], b[0]])
    if split:
        got.append([(lax.ppermute(a[0], "dp", ahead), lax.ppermute(b[1], "dp", behind))])
    else:
        a, b = lax.ppermute(a[0][:cut], "dp", ahead), lax.ppermute(b[0][cut:], "dp", behind)
        got.append([jnp.concatenate([a, b], axis=0)])
    return own, got


def ring_scatter(own, parts, n, between=()):
    ahead, behind = ring_moves(n)
    far = parts[-1][0]
    a, b = [far[0], None], [None, far[1]]
    came, done = [], []
    for step in range(n // 2):
        if step > 0:
            minus, plus = parts[n // 2 - step - 1]
            sums = [add_low(v, t) for v, t in zip(a + b, plus + minus) if v is not None]
            if step <= len(between):
                done.append(between[step - 1](came[step - 2] if step > 1 else None))
                sums = after(done[-1], sums)
            sums = iter(sums)
            a = [t if v is None else next(sums) for v, t in zip(a, plus)]
            b = [t if v is None else next(sums) for v, t in zip(b, minus)]
        a = [None if v is None else lax.ppermute(v, "dp", ahead) for v in a]
        b = [None if v is None else lax.ppermute(v, "dp", behind) for v in b]
        came.append([v for v in a + b if v is not None])
    return [o.astype(f32) + x.astype(f32) + y.astype(f32) for o, x, y in zip(own, a, b)], done


CORE = [(0, 1), (1, 0), (2, 3), (3, 2)]
CHIP = [(0, 2), (2, 0), (1, 3), (3, 1)]


def to_core(a):
    return lax.ppermute(a, "tensor", CORE)


def to_chip(a):
    return lax.ppermute(a, "tensor", CHIP)


def after(first, then):
    return lax.optimization_barrier((then, first))[0]


def per_device(layer_input, segments, routes, norm1_gain, w_query, w_key, w_value, w_output,
               norm2_gain, router, w_gate, w_up, w_down, cotangent, n_dp):
    tokens_dev, width = layer_input.shape
    quarter, top_count = routes.shape
    experts = router.shape[1]
    local = w_gate.shape[0]
    cap = quarter * top_count * 5 // (4 * experts)
    hidden = w_gate.shape[2]
    t_rank = lax.axis_index("tensor")
    d_rank = lax.axis_index("dp")
    place = jnp.where(d_rank % 2 == 0, d_rank // 2, n_dp - 1 - d_rank // 2)
    ringed = n_dp <= 8
    cos, sin = rope_tables()

    hot_t = jnp.any(
        routes.T[:, None, :] == jnp.arange(experts, dtype=i32)[None, :, None], axis=0
    )
    before = (jnp.arange(quarter)[:, None] < jnp.arange(quarter)[None, :]).astype(bf16)
    rank_t = jnp.dot(hot_t.astype(bf16), before, preferred_element_type=f32)
    rank_t = jnp.where(hot_t, rank_t, -1.0).astype(bf16)
    per_row = width // quarter
    extra = 16 * -(-experts // (16 * per_row))
    rank_rows = jnp.concatenate(
        [rank_t, jnp.full((extra * per_row - experts, quarter), -1.0, bf16)], axis=0
    ).reshape(per_row, extra, quarter)
    rank_rows = jnp.concatenate([rank_rows[j] for j in range(per_row)], axis=1)
    payload = jnp.concatenate([cotangent, rank_rows], axis=0)
    router_t = router.T
    ahead, behind = ring_moves(n_dp)

    normed1, q, k, v, kt = qkv_call(
        layer_input, norm1_gain[None, :], w_query, w_key, w_value, cos, sin
    )
    if ringed:
        _, grads_from = ring_gather(payload, n_dp, False)
        stage = [after(g, jnp.zeros((), i32)) for g in grads_from]
    else:
        stage = [jnp.zeros((), i32)] * 2
    seg_col, seg_row = segments[:, None], segments[None, :]
    pair = lambda t: jnp.stack([2 * t, 2 * t + 1])
    mate, other, cross = t_rank ^ 1, t_rank ^ 2, t_rank ^ 3
    quarters = jnp.stack([cross, mate, other, t_rank]).astype(i32)
    first = jnp.concatenate([pair(cross), pair(other)]).astype(i32)
    second = jnp.concatenate([pair(mate), pair(t_rank)]).astype(i32)
    heads, lse, send_a, keep_a = attend_call(first, q, k, v, seg_col, seg_row, w_output)
    far = to_chip(add_low(keep_a, to_core(send_a)))
    heads, lse, send_b, keep_b = attend_call(
        second + stage[0], q, k, v, seg_col, seg_row, w_output, held=(heads, lse)
    )
    far = far + stage[1].astype(bf16)
    branch = keep_b.astype(f32) + to_core(send_b).astype(f32) + far.astype(f32)

    row_start = t_rank * quarter
    own_input = lax.dynamic_slice_in_dim(layer_input, row_start, quarter).astype(f32)
    middle = own_input + branch
    inv_rms2 = lax.rsqrt(jnp.mean(middle * middle, axis=-1, keepdims=True) + EPS)
    gain_two = norm2_gain.astype(f32)
    normed2 = (middle * inv_rms2 * gain_two).astype(bf16)

    base = (d_rank * local).astype(i32)[None]
    run = lambda xs, cs, at, of, held: expert_call(
        base, xs, cs, router_t, w_gate, w_up, w_down, cap, at, of, held
    )
    if ringed:
        own, rows_from = ring_gather(normed2, n_dp, True)
        (out_own,), (back_own,), dmix_own, held = run([own], [payload], n_dp - 1, n_dp, None)
        outs, backs, dmix_minus, dmix_plus = [], [], [], []
        for j, (xs, cs) in enumerate(zip(rows_from, grads_from)):
            at = j if len(xs) == 2 else n_dp - 2
            o, b, m, held = run(xs, cs, at, n_dp, held)
            outs.append(o)
            backs.append(b)
            dmix_minus.append(m[0])
            dmix_plus.append(m[-1])
        by_step = jnp.stack([dmix_own[0]] + dmix_plus + dmix_minus[-2::-1])
        where = jnp.asarray(
            [d // 2 if d % 2 == 0 else n_dp - 1 - d // 2 for d in range(n_dp)], i32
        )
        dmix_part = jnp.take(by_step, (where - place) % n_dp, axis=0)
        grad_of = lambda i, j: lambda came: weight_grad_call(
            quarters if came is None else quarters + after(came, jnp.zeros((), i32)),
            held[i], held[j],
        )
        routed, expert_parts = ring_scatter(
            back_own, backs, n_dp, (grad_of(0, 3), grad_of(0, 4), grad_of(1, 2))
        )
        routed = jnp.concatenate(routed, axis=0)
    else:
        grads_all = lax.all_gather(payload, "dp", axis=0)
        rows_all = lax.all_gather(normed2, "dp", axis=0)
        halves = lambda a: (a[:quarter // 2], a[quarter // 2:])

        def two(sums, pair_rows):
            x, c = pair_rows
            o, b, m, held = run([halves(x[0]), halves(x[1])], [c[0], c[1]], 0, 2, None)
            grads = [
                list(weight_grad_call(quarters, held[i], held[j])) for i, j in ((0, 3), (0, 4), (1, 2))
            ]
            sums = jax.tree.map(lambda t, g: t + g.astype(f32), sums, grads)
            join = lambda a: jnp.stack([jnp.concatenate(h, axis=0) for h in a])
            return sums, (join(o), join(b), m)

        pairs = lambda a: a.reshape((n_dp // 2, 2) + a.shape[1:])
        zero = jnp.zeros((2, local, width // 4, hidden), f32)
        expert_parts, (outs, backs, dmix_part) = lax.scan(
            two, [[zero, zero]] * 3, (pairs(rows_all), pairs(grads_all))
        )
        expert_parts = jax.tree.map(lambda a: a.astype(bf16), expert_parts)
        dmix_part = dmix_part.reshape(n_dp, local, quarter)
        scatter = lambda a: lax.psum_scatter(
            a.reshape(n_dp * quarter, width), "dp", scatter_dimension=0, tiled=True
        ).astype(f32)
        routed = scatter(backs)
    d_mix = lax.all_to_all(dmix_part, "dp", split_axis=0, concat_axis=0, tiled=True)
    d_mix = d_mix.reshape(experts, quarter)

    logits_t = mm(router_t, normed2, NT)
    logits_t = jnp.where(hot_t, logits_t, -jnp.inf)
    mix_t = jax.nn.softmax(logits_t, axis=0)
    d_logits_t = mix_t * (d_mix - jnp.sum(mix_t * d_mix, axis=0, keepdims=True))
    d_logits = jnp.where(hot_t, d_logits_t, 0.0).astype(bf16).T
    router_part = mm(normed2, d_logits, TN)

    out_grad = cotangent.astype(f32)
    d_normed2 = routed + mm(d_logits, router, NT)
    scaled_two = d_normed2 * gain_two
    d_middle = (
        out_grad
        + inv_rms2 * scaled_two
        - middle * inv_rms2**3 * jnp.mean(scaled_two * middle, axis=-1, keepdims=True)
    )

    db_own = d_middle.astype(bf16)
    db_mate = to_core(db_own)
    db_other = to_chip(db_own)
    db_cross = to_core(db_other)
    near = jnp.concatenate([pair(t_rank), pair(mate)]).astype(i32)
    distant = jnp.concatenate([pair(other), pair(cross)]).astype(i32)
    common = (q, k, v, kt, seg_row, seg_col, heads, lse)
    dq, dk, dv = attend_back_call(near, *common, db_own, db_mate, w_output, cos, sin)
    rows_of = lambda t: lax.dynamic_slice_in_dim(heads, t * quarter, quarter)
    wo_near = mm(db_own, rows_of(t_rank), TN) + mm(db_mate, rows_of(mate), TN)
    dq, dkv = attend_back_call(
        distant, *common, db_other, db_cross, w_output, cos, sin, held=(dq, dk, dv)
    )
    send, keep, first_gain_part = qkv_back_call(
        jnp.concatenate([pair(t) for t in (cross, mate, other, t_rank)]).astype(i32),
        dq, dkv, layer_input, w_query, w_key, w_value,
    )
    came = to_core(send)
    far = to_chip(add_low(keep[:quarter], came[:quarter]))
    d_normed1 = keep[quarter:].astype(f32) + came[quarter:].astype(f32) + far.astype(f32)

    second_gain_part = jnp.sum(d_normed2 * middle * inv_rms2, axis=0)

    def over_all(part):
        rows = part.reshape(n_dp * 4, -1)
        rows = lax.all_to_all(rows, ("dp", "tensor"), split_axis=0, concat_axis=0, tiled=True)
        return jnp.sum(rows, axis=0)

    router_gain = jnp.concatenate([router_part, second_gain_part[:, None]], axis=1)
    router_gain = over_all(router_gain).reshape(-1, experts + 1)
    first_gain = over_all(first_gain_part)

    if ringed:
        summed, _ = ring_scatter(out_own, [list(after(db_own, o)) for o in outs], n_dp)
        summed = jnp.concatenate(summed, axis=0)
    else:
        summed = scatter(outs)
    layer_out = (middle + summed).astype(bf16)

    def shared(parts):
        send, keep = parts
        came = to_core(send)
        far = to_chip(add_low(keep[0], came[0]))
        return keep[1].astype(f32) + came[1].astype(f32) + far.astype(f32)

    gate_grad, up_grad, down_grad = [shared(p) for p in expert_parts]
    down_grad = jnp.transpose(down_grad, (0, 2, 1))

    query_part = mm(normed1, dq, TN).astype(bf16)
    kv_part = mm(normed1, dkv, TN).astype(bf16)
    wo_part = wo_near + mm(db_other, rows_of(other), TN) + mm(db_cross, rows_of(cross), TN)
    packed_dense = jnp.concatenate([query_part, kv_part, wo_part.astype(bf16)], axis=1)
    if ringed:
        blocks = packed_dense.reshape(n_dp, width // n_dp, packed_dense.shape[1])
        ring = jnp.asarray(ring_of(n_dp), i32)

        def block(far):
            rows = lax.dynamic_index_in_dim(
                blocks, ring[(place + far) % n_dp], axis=0, keepdims=False
            )
            return rows[:rows.shape[0] // 2], rows[rows.shape[0] // 2:]

        parts = [[block(-j), block(j)] for j in range(1, n_dp // 2)] + [[block(n_dp // 2)]]
        dense_sum, _ = ring_scatter(block(0), parts, n_dp)
        dense_sum = jnp.concatenate(dense_sum, axis=0)
    else:
        dense_sum = lax.psum_scatter(
            packed_dense, "dp", scatter_dimension=0, tiled=True
        ).astype(f32)
    q_cols, kv_cols = w_query.shape[1], w_key.shape[1]
    query_grad = dense_sum[:, :q_cols]
    key_grad = dense_sum[:, q_cols:q_cols + kv_cols]
    value_grad = dense_sum[:, q_cols + kv_cols:q_cols + 2 * kv_cols]
    output_grad = jnp.transpose(dense_sum[:, q_cols + 2 * kv_cols:])

    own_rms = lax.rsqrt(jnp.mean(own_input * own_input, axis=-1, keepdims=True) + EPS)
    scaled_one = d_normed1 * norm1_gain.astype(f32)
    input_grad = (
        d_middle
        + own_rms * scaled_one
        - own_input * own_rms**3 * jnp.mean(scaled_one * own_input, axis=-1, keepdims=True)
    )
    return (
        layer_out,
        input_grad,
        first_gain,
        query_grad,
        key_grad,
        value_grad,
        output_grad,
        router_gain[:, experts],
        router_gain[:, :experts],
        gate_grad,
        up_grad,
        down_grad,
    )


def solution(mesh):
    both = ("dp", "tensor")
    return jax.shard_map(
        functools.partial(per_device, n_dp=mesh.shape["dp"]),
        mesh=mesh,
        in_specs=(
            P("dp", None), P("dp"), P(both, None), P(),
            P(None, "tensor"), P(None, "tensor"), P(None, "tensor"), P("tensor", None),
            P(), P(), P("dp", None, None), P("dp", None, None), P("dp", None, None),
            P(both, None),
        ),
        out_specs=(
            P(both, None), P(both, None), P(both), P("dp", "tensor"), P("dp", "tensor"),
            P("dp", "tensor"), P("tensor", "dp"), P(both), P(both, None),
            P("dp", "tensor", None), P("dp", "tensor", None), P("dp", None, "tensor"),
        ),
        check_vma=False,
    )
```

time: 2780 us -> 804 us (0.29)
  blocking collectives: 690 us -> 0 us
  waiting for transfers between devices: 832 us -> 204 us
  matrix products: 479 us -> 29.2 us
  local copies, waits for them, and re-layouts: 436 us -> 36.3 us
  Pallas kernels: 0 us -> 318 us
  other arithmetic: 269 us -> 97.2 us
  starting transfers between devices: 12.2 us -> 95.8 us
  loops' own time: 32.2 us -> 0 us
    all_to_all x2 -> x0, blocking collectives: 690 us -> none  [the longest x1 346 us: per_device(): lax.all_to_all(send_rows, 'dp', split_axis=0, concat_axis=0, tiled=True)]
    all_to_all x2 -> x3, waiting for transfers between devices: 657 us -> 14.6 us  [the longest x1 14.6 us: per_device(): lax.all_to_all(dmix_part, 'dp', split_axis=0, concat_axis=0, tiled=True)]
    dot_general x54 -> x10, matrix products: 477 us -> 29.2 us  [the longest x9 29 us: mm(): return lax.dot_general(a, b, dims, preferred_element_type=f32)]
    pallas_call x0 -> x14, Pallas kernels: none -> 318 us  [the longest x5 146 us: expert_call(): pl.pallas_call(functools.partial(expert_kernel, sources, cap, experts), g...]
    ppermute x0 -> x78, waiting for transfers between devices: none -> 190 us  [the longest x9 61.6 us: ring_gather(): a = tuple((lax.ppermute(v, 'dp', ahead) for v in a))]
    gather x4 -> x1, local copies, waits for them, and re-layouts: 127 us -> 0.59 us  [per_device(): dmix_part = jnp.take(by_step, (where - place) % n_dp, axis=0)]
    dynamic_update_slice x16 -> x0, local copies, waits for them, and re-layouts: 111 us -> none  [the longest x8 67.5 us: per_device(): lax.scan(backward_block, (zero_keys, zero_keys), (offsets, log_totals))]
    unnamed x11 -> x0, waiting for transfers between devices: 98.3 us -> none
  transfers between devices with their start and end apart: 9 -> 81, of which waited for: 6 -> 30; matrix products, arithmetic and copies ran while one was open for 23% -> 16% of each run, Pallas kernels for 0% -> 35%
where the time goes in v1:
time: 804 us; the launch traced here: 798 us
  Pallas kernels  318 us (40%)
  waiting for transfers between devices  204 us (25%)
  other arithmetic  97.2 us (12%)
  starting transfers between devices  95.8 us (12%)
  local copies, waits for them, and re-layouts  36.3 us (5%)
  matrix products  29.2 us (4%)
  between operations  17.4 us (2%)
    pallas_call x5, Pallas kernels, expert_call(): pl.pallas_call(functools.partial(expert_kernel, sources, cap, experts), g...  146 us
    ppermute x9, waiting for transfers between devices, ring_gather(): a = tuple((lax.ppermute(v, 'dp', ahead) for v in a))  61.6 us
    ppermute x21, waiting for transfers between devices, ring_scatter(): a = [None if v is None else lax.ppermute(v, 'dp', ahead) for v in a]  56.7 us
    pallas_call x2, Pallas kernels, attend_back_call(): pl.pallas_call(functools.partial(attend_back_kernel, last), grid_spec=plt...  52.8 us
    pallas_call x3, Pallas kernels, weight_grad_call(): pl.pallas_call(weight_grad_kernel, grid_spec=pltpu.PrefetchScalarGridSpec...  52.5 us
    convert_element_type x28, other arithmetic, add_low(): return (a.astype(f32) + b.astype(f32)).astype(bf16)  43.3 us
    pallas_call x2, Pallas kernels, attend_call(): pl.pallas_call(attend_kernel, grid_spec=pltpu.PrefetchScalarGridSpec(num_...  39.4 us
    ppermute x21, waiting for transfers between devices, ring_scatter(): b = [None if v is None else lax.ppermute(v, 'dp', behind) for v in b]  31.4 us
  transfers between devices with their start and end apart: 81, of which 30 were waited for; matrix products, arithmetic and copies ran while one was open for 16% of the time, Pallas kernels for 35%

profile of v1, /device:TPU:0, one launch (start us, length us, event | category | flops | bytes accessed | tf_op | source)
XLA Modules:
  0.0 798.4 jit_solution(7056844969637172288)
XLA Ops:
  1.7 2.8 maximum_maximum_fusion.refs_2_
  4.6 3.0 collective-permute-start
  9.0 13.0 %norm_qkv.1 = (bf16[2048,1536]{1,0:T(8,128)(2,1)}, bf16[6,2048,64]{2,1,0:T(8,128)(2,1)}, bf16[2,2048,64]{2,1,0:T(8,128)(2,1)S(1)}, bf16[2,2048,64]{2,1,0:T(8,128)(2,1)S(1)}, bf16[2,64,2048]{2,1,0:T(8,128)(2,1)S(1)}) custom-call(bf16[2048,1536]{1,0:T(8,128)(2,1)} %x_ref.3, bf16[1,1536]{1,0:T(2,128)(2,1)S(1)} %broadcast_in_dim.53.gain_ref, ...), custom_call_target="tpu_custom_call" | custom-call | flops 12999999488 | bytes 20000000 | tf_op jit(solution)/shard_map/norm_qkv/pallas_call | solution.py:95
  24.8 18.5 %collective-permute-done.refs_4_ = bf16[528,1536]{1,0:T(8,128)(2,1)} collective-permute-done((bf16[528,1536]{1,0:T(8,128)(2,1)}, bf16[528,1536]{1,0:T(8,128)(2,1)}, u32[]{:S(2)}, u32[]{:S(2)}) %collective-permute-start) | collective-permute-done | bytes 1622048 | tf_op jit(solution)/shard_map/ppermute | solution.py:640
  45.5 23.1 %attend.2 = (bf16[2048,384]{1,0:T(8,128)(2,1)}, f32[8,2048]{1,0:T(8,128)}, bf16[512,1536]{1,0:T(8,128)(2,1)}, bf16[512,1536]{1,0:T(8,128)(2,1)}) custom-call(s32[4]{0:T(128)} %get-tuple-element.356.order_ref, bf16[6,2048,64]{2,1,0:T(8,128)(2,1)} %get-tuple-element.130.q_ref, bf16[2,2048,64]{2,1,0:T(8,128)(2,1)} %copy-done.18, ...), custom_call_target="tpu_custom_call" | custom-call | flops 16999999488 | bytes 10000000 | tf_op jit(solution)/shard_map/attend/pallas_call | solution.py:209
  68.5 16.4 %attend.3 = (bf16[2048,384]{1,0:T(8,128)(2,1)}, f32[8,2048]{1,0:T(8,128)}, bf16[512,1536]{1,0:T(8,128)(2,1)}, bf16[512,1536]{1,0:T(8,128)(2,1)}) custom-call(s32[4]{0:T(128)} %get-tuple-element.355.order_ref, bf16[6,2048,64]{2,1,0:T(8,128)(2,1)} %get-tuple-element.130.q_ref, ...), custom_call_target="tpu_custom_call", output_to_operand_aliasing={{0}: (7, {}), {1}: (8, {})} | custom-call | flops 16999999488 | bytes 10000000 | tf_op jit(solution)/shard_map/attend/pallas_call | solution.py:209
  107.8 15.4 %collective-permute-done.5.refs_4_ = bf16[528,1536]{1,0:T(8,128)(2,1)} collective-permute-done((bf16[528,1536]{1,0:T(8,128)(2,1)}, bf16[528,1536]{1,0:T(8,128)(2,1)}, u32[]{:S(2)}, u32[]{:S(2)}) %collective-permute-start.5) | collective-permute-done | bytes 1622048 | tf_op jit(solution)/shard_map/ppermute | solution.py:640
  126.5 3.4 multiply_reduce_fusion.2
  135.5 27.6 %collective-permute-done.15.refs_4_ = bf16[528,1536]{1,0:T(8,128)(2,1)S(1)} collective-permute-done((bf16[528,1536]{1,0:T(8,128)(2,1)}, bf16[528,1536]{1,0:T(8,128)(2,1)S(1)}, u32[]{:S(2)}, u32[]{:S(2)}) %collective-permute-start.15) | collective-permute-done | bytes 1622048 | tf_op jit(solution)/shard_map/ppermute | solution.py:640
  166.3 22.9 %experts.5 = (bf16[256,1536]{1,0:T(8,128)(2,1)}, bf16[256,1536]{1,0:T(8,128)(2,1)}, bf16[256,1536]{1,0:T(8,128)(2,1)}, bf16[256,1536]{1,0:T(8,128)(2,1)}, f32[1,...) custom-call(s32[1]{0:T(128)} %bitcast.11.base_ref, ...), custom_call_target="tpu_custom_call" | custom-call | flops 14000000000 | bytes 20000000 | tf_op jit(solution)/shard_map/experts/pallas_call | solution.py:537
  192.8 5.7 collective-permute-done.22.refs_2_
  200.5 13.1 %collective-permute-done.16 = bf16[256,1536]{1,0:T(8,128)(2,1)S(1)} collective-permute-done((bf16[256,1536]{1,0:T(8,128)(2,1)S(1)}, bf16[256,1536]{1,0:T(8,128)(2,1)S(1)}, u32[]{:S(2)}, u32[]{:S(2)}) %collective-permute-start.16) | collective-permute-done | bytes 786464 | tf_op jit(solution)/shard_map/ppermute | solution.py:646
  215.2 33.6 %experts.6 = (bf16[256,1536]{1,0:T(8,128)(2,1)}, bf16[256,1536]{1,0:T(8,128)(2,1)}, bf16[256,1536]{1,0:T(8,128)(2,1)}, bf16[256,1536]{1,0:T(8,128)(2,1)}, bf16[2...) custom-call(s32[1]{0:T(128)} %bitcast.11.base_ref, ...), custom_call_target="tpu_custom_call", output_to_operand_aliasing={{9}: (11, {}), {10}: (12, {}), {11}: (13, {}), {12}: (14, {... | custom-call | flops 28000000000 | bytes 20000000 | tf_op jit(solution)/shard_map/experts/pallas_call | solution.py:537
  254.9 33.8 %experts.7 = (bf16[256,1536]{1,0:T(8,128)(2,1)}, bf16[256,1536]{1,0:T(8,128)(2,1)}, bf16[256,1536]{1,0:T(8,128)(2,1)}, bf16[256,1536]{1,0:T(8,128)(2,1)}, bf16[2...) custom-call(s32[1]{0:T(128)} %bitcast.11.base_ref, ...), custom_call_target="tpu_custom_call", output_to_operand_aliasing={{9}: (11, {}), {10}: (12, {}), {11}: (13, {}), {12}: (14, {... | custom-call | flops 28000000000 | bytes 20000000 | tf_op jit(solution)/shard_map/experts/pallas_call | solution.py:537
  291.8 33.5 %experts.8 = (bf16[256,1536]{1,0:T(8,128)(2,1)}, bf16[256,1536]{1,0:T(8,128)(2,1)}, bf16[256,1536]{1,0:T(8,128)(2,1)}, bf16[256,1536]{1,0:T(8,128)(2,1)}, bf16[2...) custom-call(s32[1]{0:T(128)} %bitcast.11.base_ref, ...), custom_call_target="tpu_custom_call", output_to_operand_aliasing={{9}: (11, {}), {10}: (12, {}), {11}: (13, {}), {12}: (14, {... | custom-call | flops 28000000000 | bytes 20000000 | tf_op jit(solution)/shard_map/experts/pallas_call | solution.py:537
  329.3 22.5 %experts.9 = (bf16[256,1536]{1,0:T(8,128)(2,1)}, bf16[256,1536]{1,0:T(8,128)(2,1)}, bf16[256,1536]{1,0:T(8,128)(2,1)}, bf16[256,1536]{1,0:T(8,128)(2,1)}, f32[1,...) custom-call(s32[1]{0:T(128)} %bitcast.11.base_ref, ...), custom_call_target="tpu_custom_call", output_to_operand_aliasing={{5}: (8, {}), {6}: (9, {}), {7}: (10, {}), {8}: (11, {}), {... | custom-call | flops 14000000000 | bytes 20000000 | tf_op jit(solution)/shard_map/experts/pallas_call | solution.py:537
  358.3 7.1 collective-permute-done.25
  366.1 2.5 copy-done
  368.6 17.6 %weight_grad.3 = (bf16[2,4,384,512]{3,2,1,0:T(8,128)(2,1)S(1)}, bf16[2,4,384,512]{3,2,1,0:T(8,128)(2,1)S(1)}) custom-call(s32[4]{0:T(128)S(1)} %get-tuple-element.313.order_ref, bf16[4,1280,1536]{2,1,0:T(8,128)(2,1)} %get-tuple-element.168.a_ref, bf16[4,1280,512]{2,1,0:T(8,128)(2,1)S(1)} %copy-done), custom_call_target="tpu_custom_call" | custom-call | flops 10000000000 | bytes 20000000 | tf_op jit(solution)/shard_map/weight_grad/pallas_call | solution.py:588
  392.4 17.4 %weight_grad.4 = (bf16[2,4,384,512]{3,2,1,0:T(8,128)(2,1)S(1)}, bf16[2,4,384,512]{3,2,1,0:T(8,128)(2,1)S(1)}) custom-call(s32[4]{0:T(128)S(1)} %get-tuple-element.312.order_ref, bf16[4,1280,1536]{2,1,0:T(8,128)(2,1)} %get-tuple-element.168.a_ref, bf16[4,1280,512]{2,1,0:T(8,128)(2,1)S(1)} %bitcast.136), custom_call_target="tpu_custom_call" | custom-call | flops 10000000000 | bytes 20000000 | tf_op jit(solution)/shard_map/weight_grad/pallas_call | solution.py:588
  415.9 17.5 %weight_grad.5 = (bf16[2,4,384,512]{3,2,1,0:T(8,128)(2,1)S(1)}, bf16[2,4,384,512]{3,2,1,0:T(8,128)(2,1)S(1)}) custom-call(s32[4]{0:T(128)S(1)} %broadcast_add_fusion.order_ref, bf16[4,1280,1536]{2,1,0:T(8,128)(2,1)} %get-tuple-element.193.a_ref, bf16[4,1280,512]{2,1,0:T(8,128)(2,1)S(1)} %bitcast.134), custom_call_target="tpu_custom_call" | custom-call | flops 10000000000 | bytes 20000000 | tf_op jit(solution)/shard_map/weight_grad/pallas_call | solution.py:588
  436.1 5.7 collective-permute-done.33
  444.0 2.4 collective-permute-done.31
  450.1 3.5 all-to-all-start
  453.6 14.6 %all-to-all-done = f32[8,4,512]{2,1,0:T(4,128)S(1)} async-done(((f32[8,4,512]{2,1,0:T(4,128)}), f32[8,4,512]{2,1,0:T(4,128)S(1)}, u32[]{:S(2)}, u32[]{:S(2)}) %all-to-all-start) | async-done | bytes 65568 | tf_op jit(solution)/shard_map/all_to_all | solution.py:801
  474.9 5.6 collective-permute-done.37
  482.3 2.7 multiply_reduce_fusion
  486.3 2.5 all_to_all.20
  488.7 3.3 all-to-all-start.2
  492.1 7.5 fusion.43
  502.8 3.7 fusion.30
  508.2 3.7 fusion.8
  512.5 3.3 fusion.7
  515.8 5.2 collective-permute-done.39
  524.7 7.2 collective-permute-done.43
  533.6 5.8 collective-permute-done.46
  541.0 10.3 %collective-permute-done.49 = bf16[256,1536]{1,0:T(8,128)(2,1)S(1)} collective-permute-done((bf16[256,1536]{1,0:T(8,128)(2,1)S(1)}, bf16[256,1536]{1,0:T(8,128)(2,1)S(1)}, u32[]{:S(2)}, u32[]{:S(2)}) %collective-permute-start.49) | collective-permute-done | bytes 786464 | tf_op jit(solution)/shard_map/ppermute | solution.py:667
  554.4 3.1 fusion.9
  558.7 20.7 %attend_back.2 = (bf16[2048,384]{1,0:T(8,128)(2,1)}, f32[2,2048,64]{2,1,0:T(8,128)}, f32[2,2048,64]{2,1,0:T(8,128)}) custom-call(s32[4]{0:T(128)} %pad_add_fusion.3.order_ref, bf16[6,2048,64]{2,1,0:T(8,128)(2,1)} %get-tuple-element.130.q_ref, bf16[2,2048,64]{2,1,0:T(8,128)(2,1)} %copy-done.18, bf16[2,2048,64]{2,1,0:T(8,128)(2,1)} %copy-done.19, ...), custom_call_target="tpu_custom_call" | custom-call | flops 22000001024 | bytes 20000000 | tf_op jit(solution)/shard_map/attend_back/pallas_call | solution.py:350
  579.4 2.4 fusion.28
  583.4 3.7 fusion.26
  589.0 11.1 %collective-permute-start.77 = (bf16[4,384,512]{2,1,0:T(8,128)(2,1)}, bf16[4,384,512]{2,1,0:T(8,128)(2,1)}, u32[]{:S(2)}, u32[]{:S(2)}) collective-permute-start(bf16[4,384,512]{2,1,0:T(8,128)(2,1)} %fusion.9), channel_id=1, source_target_pairs={{0,2},{2,0},{1,3},{3,1},{4,6},{6,4},{5,7},{7,5},{8,10},{10,8},{9,1... | collective-permute-start | bytes 4718600 | tf_op jit(solution)/shard_map/ppermute | solution.py:681
  608.1 4.4 bitcast_add_fusion.1
  613.0 4.1 bitcast_add_fusion.2
  617.1 6.3 collective-permute-done.41
  626.0 32.1 %attend_back.3 = (bf16[2048,384]{1,0:T(8,128)(2,1)}, bf16[2048,256]{1,0:T(8,128)(2,1)}) custom-call(s32[4]{0:T(128)} %pad_add_fusion.2.order_ref, bf16[6,2048,64]{2,1,0:T(8,128)(2,1)} %get-tuple-element.130.q_ref, bf16[2,2048,64]{2,1,0:T(8,128)(2,1)} %copy-done.18, bf16[2,2048,64]{2,1,0:T(8,128)(2,1)} %copy-done.19, ...), custom_call_target="tpu_custom_call", output_to_operand_aliasing={{0}: (18, {})} | custom-call | flops 22000001024 | bytes 20000000 | tf_op jit(solution)/shard_map/attend_back/pallas_call | solution.py:350
  658.1 7.0 convolution_convert_fusion
  665.1 4.8 convolution_convert_fusion.1
  669.9 14.2 %qkv_back.1 = (bf16[1024,1536]{1,0:T(8,128)(2,1)}, bf16[1024,1536]{1,0:T(8,128)(2,1)}, f32[1,1536]{1,0:T(1,128)S(1)}) custom-call(s32[8]{0:T(128)S(1)} %concatenate.47.order_ref, bf16[2048,384]{1,0:T(8,128)(2,1)S(1)} %copy-done.17, bf16[2048,256]{1,0:T(8,128)(2,1)S(1)} %copy-done.16, bf16[2048,1536]{1,0:T(8,128)(2,1)} %x_ref.3, ...), custom_call_target="tpu_custom_call" | custom-call | flops 6000000000 | bytes 20000000 | tf_op jit(solution)/shard_map/qkv_back/pallas_call | solution.py:395
  684.1 2.4 fusion.6
  688.4 4.6 copy.93
  694.8 2.4 add_convert_fusion.5
  697.3 4.3 collective-permute-done.68
  705.6 3.6 collective-permute-done.58
  710.4 4.1 fusion.5
  714.6 3.7 copy.97
  719.0 3.4 all-to-all-start.1
  734.8 2.8 collective-permute-done.66
  740.3 3.1 add_convert_fusion.3
  743.4 11.0 %collective-permute-done.48 = bf16[256,1536]{1,0:T(8,128)(2,1)S(1)} collective-permute-done((bf16[256,1536]{1,0:T(8,128)(2,1)S(1)}, bf16[256,1536]{1,0:T(8,128)(2,1)S(1)}, u32[]{:S(2)}, u32[]{:S(2)}) %collective-permute-start.48) | collective-permute-done | bytes 786464 | tf_op jit(solution)/shard_map/ppermute | solution.py:666
  758.6 3.1 collective-permute-done.67
  771.9 18.2 %collective-permute-done.57 = bf16[512,1536]{1,0:T(8,128)(2,1)} collective-permute-done((bf16[512,1536]{1,0:T(8,128)(2,1)}, bf16[512,1536]{1,0:T(8,128)(2,1)}, u32[]{:S(2)}, u32[]{:S(2)}) %collective-permute-start.57) | collective-permute-done | bytes 1572896 | tf_op jit(solution)/shard_map/ppermute | solution.py:681
  790.1 3.5 fusion
  793.7 4.2 fusion.2
  (415 shorter events, 154.9 us)
Async XLA Ops:
  4.6 38.7 %collective-permute-start = (bf16[528,1536]{1,0:T(8,128)(2,1)}, bf16[528,1536]{1,0:T(8,128)(2,1)}, u32[]{:S(2)}, u32[]{:S(2)}) collective-permute-start(bf16[528,1536]{1,0:T(8,128)(2,1)} %maximum_maximum_fusion.refs_2_), channel_id=1, source_target_pairs={{0,8},{8,16},{16,24},{24,28},{28,20},{20,12},{12,4},{4,0},{1,9},{9... | collective-permute-start | bytes 4866056 | tf_op jit(solution)/shard_map/ppermute | solution.py:640
  7.6 37.2 %collective-permute-start.1 = (bf16[528,1536]{1,0:T(8,128)(2,1)}, bf16[528,1536]{1,0:T(8,128)(2,1)}, u32[]{:S(2)}, u32[]{:S(2)}) collective-permute-start(bf16[528,1536]{1,0:T(8,128)(2,1)} %maximum_maximum_fusion.refs_2_), channel_id=1, source_target_pairs={{8,0},{16,8},{24,16},{28,24},{20,28},{12,20},{4,12},{0,4},{9,1},{1... | collective-permute-start | bytes 4866056 | tf_op jit(solution)/shard_map/ppermute | solution.py:641
  68.5 19.0 %collective-permute-start.3 = (bf16[512,1536]{1,0:T(8,128)(2,1)}, bf16[512,1536]{1,0:T(8,128)(2,1)S(1)}, u32[]{:S(2)}, u32[]{:S(2)}) collective-permute-start(bf16[512,1536]{1,0:T(8,128)(2,1)} %get-tuple-element.138), channel_id=1, source_target_pairs={{0,1},{1,0},{2,3},{3,2},{4,5},{5,4},{6,7},{7,6},{8,9},{9,8},{10,11... | collective-permute-start | bytes 4718600 | tf_op jit(solution)/shard_map/ppermute | solution.py:677
  84.9 41.6 %collective-permute-start.2 = (bf16[512,1536]{1,0:T(8,128)(2,1)}, bf16[512,1536]{1,0:T(8,128)(2,1)}, u32[]{:S(2)}, u32[]{:S(2)}) collective-permute-start(bf16[512,1536]{1,0:T(8,128)(2,1)} %get-tuple-element.136), channel_id=1, source_target_pairs={{0,1},{1,0},{2,3},{3,2},{4,5},{5,4},{6,7},{7,6},{8,9},{9,8},{10,11... | collective-permute-start | bytes 4718600 | tf_op jit(solution)/shard_map/ppermute | solution.py:677
  85.5 37.7 %collective-permute-start.5 = (bf16[528,1536]{1,0:T(8,128)(2,1)}, bf16[528,1536]{1,0:T(8,128)(2,1)}, u32[]{:S(2)}, u32[]{:S(2)}) collective-permute-start(bf16[528,1536]{1,0:T(8,128)(2,1)} %collective-permute-done.refs_4_), channel_id=1, source_target_pairs={{0,8},{8,16},{16,24},{24,28},{28,20},{20,12},{12,4},{4,0},{1,9},{9... | collective-permute-start | bytes 4866056 | tf_op jit(solution)/shard_map/ppermute | solution.py:640
  87.0 37.5 %collective-permute-start.6 = (bf16[528,1536]{1,0:T(8,128)(2,1)}, bf16[528,1536]{1,0:T(8,128)(2,1)}, u32[]{:S(2)}, u32[]{:S(2)}) collective-permute-start(bf16[528,1536]{1,0:T(8,128)(2,1)} %collective-permute-done.1.refs_5_), channel_id=1, source_target_pairs={{8,0},{16,8},{24,16},{28,24},{20,28},{12,20},{4,12},{0,4},{9,1},{1... | collective-permute-start | bytes 4866056 | tf_op jit(solution)/shard_map/ppermute | solution.py:641
  87.9 38.6 %collective-permute-start.4 = (bf16[512,1536]{1,0:T(8,128)(2,1)S(1)}, bf16[512,1536]{1,0:T(8,128)(2,1)}, u32[]{:S(2)}, u32[]{:S(2)}) collective-permute-start(bf16[512,1536]{1,0:T(8,128)(2,1)S(1)} %add_convert_fusion.4), channel_id=1, source_target_pairs={{0,2},{2,0},{1,3},{3,1},{4,6},{6,4},{5,7},{7,5},{8,10},{10,8},{9,1... | collective-permute-start | bytes 4718600 | tf_op jit(solution)/shard_map/ppermute | solution.py:681
  124.5 38.6 %collective-permute-start.15 = (bf16[528,1536]{1,0:T(8,128)(2,1)}, bf16[528,1536]{1,0:T(8,128)(2,1)S(1)}, u32[]{:S(2)}, u32[]{:S(2)}) collective-permute-start(bf16[528,1536]{1,0:T(8,128)(2,1)} %collective-permute-done.5.refs_4_), channel_id=1, source_target_pairs={{0,8},{8,16},{16,24},{24,28},{28,20},{20,12},{12,4},{4,0},{1,9},{9... | collective-permute-start | bytes 4866056 | tf_op jit(solution)/shard_map/ppermute | solution.py:640
  126.1 38.7 %collective-permute-start.17 = (bf16[528,1536]{1,0:T(8,128)(2,1)}, bf16[528,1536]{1,0:T(8,128)(2,1)S(1)}, u32[]{:S(2)}, u32[]{:S(2)}) collective-permute-start(bf16[528,1536]{1,0:T(8,128)(2,1)} %collective-permute-done.6.refs_5_), channel_id=1, source_target_pairs={{8,0},{16,8},{24,16},{28,24},{20,28},{12,20},{4,12},{0,4},{9,1},{1... | collective-permute-start | bytes 4866056 | tf_op jit(solution)/shard_map/ppermute | solution.py:641
  133.0 58.8 %collective-permute-start.11 = (bf16[256,1536]{1,0:T(8,128)(2,1)}, bf16[256,1536]{1,0:T(8,128)(2,1)}, u32[]{:S(2)}, u32[]{:S(2)}) collective-permute-start(bf16[256,1536]{1,0:T(8,128)(2,1)} %get-tuple-element.332.refs_1_), channel_id=1, source_target_pairs={{8,0},{16,8},{24,16},{28,24},{20,28},{12,20},{4,12},{0,4},{9,1},{1... | collective-permute-start | bytes 2359304 | tf_op jit(solution)/shard_map/ppermute | solution.py:641
  133.4 58.9 %collective-permute-start.19 = (bf16[256,1536]{1,0:T(8,128)(2,1)}, bf16[256,1536]{1,0:T(8,128)(2,1)}, u32[]{:S(2)}, u32[]{:S(2)}) collective-permute-start(bf16[256,1536]{1,0:T(8,128)(2,1)} %get-tuple-element.332.refs_1_), channel_id=1, source_target_pairs={{0,8},{8,16},{16,24},{24,28},{28,20},{20,12},{12,4},{4,0},{1,9},{9... | collective-permute-start | bytes 2359304 | tf_op jit(solution)/shard_map/ppermute | solution.py:640
  135.0 63.5 %collective-permute-start.22 = (bf16[256,1536]{1,0:T(8,128)(2,1)}, bf16[256,1536]{1,0:T(8,128)(2,1)}, u32[]{:S(2)}, u32[]{:S(2)}) collective-permute-start(bf16[256,1536]{1,0:T(8,128)(2,1)} %get-tuple-element.333.refs_0_), channel_id=1, source_target_pairs={{8,0},{16,8},{24,16},{28,24},{20,28},{12,20},{4,12},{0,4},{9,1},{1... | collective-permute-start | bytes 2359304 | tf_op jit(solution)/shard_map/ppermute | solution.py:641
  163.1 36.9 %collective-permute-start.7 = (bf16[256,1536]{1,0:T(8,128)(2,1)}, bf16[256,1536]{1,0:T(8,128)(2,1)}, u32[]{:S(2)}, u32[]{:S(2)}) collective-permute-start(bf16[256,1536]{1,0:T(8,128)(2,1)} %get-tuple-element.333.refs_0_), channel_id=1, source_target_pairs={{0,8},{8,16},{16,24},{24,28},{28,20},{20,12},{12,4},{4,0},{1,9},{9... | collective-permute-start | bytes 2359304 | tf_op jit(solution)/shard_map/ppermute | solution.py:640
  164.8 48.9 %collective-permute-start.16 = (bf16[256,1536]{1,0:T(8,128)(2,1)S(1)}, bf16[256,1536]{1,0:T(8,128)(2,1)S(1)}, u32[]{:S(2)}, u32[]{:S(2)}) collective-permute-start(bf16[256,1536]{1,0:T(8,128)(2,1)S(1)} %slice.243), channel_id=1, source_target_pairs={{0,8},{8,16},{16,24},{24,28},{28,20},{20,12},{12,4},{4,0},{1,9},{9... | collective-permute-start | bytes 2359304 | tf_op jit(solution)/shard_map/ppermute | solution.py:646
  191.8 57.8 %collective-permute-start.18 = (bf16[272,1536]{1,0:T(8,128)(2,1)S(1)}, bf16[272,1536]{1,0:T(8,128)(2,1)S(1)}, u32[]{:S(2)}, u32[]{:S(2)}) collective-permute-start(bf16[272,1536]{1,0:T(8,128)(2,1)S(1)} %slice.244), channel_id=1, source_target_pairs={{8,0},{16,8},{24,16},{28,24},{20,28},{12,20},{4,12},{0,4},{9,1},{1... | collective-permute-start | bytes 2506760 | tf_op jit(solution)/shard_map/ppermute | solution.py:646
  192.3 58.5 %collective-permute-start.12 = (bf16[256,1536]{1,0:T(8,128)(2,1)}, bf16[256,1536]{1,0:T(8,128)(2,1)}, u32[]{:S(2)}, u32[]{:S(2)}) collective-permute-start(bf16[256,1536]{1,0:T(8,128)(2,1)} %collective-permute-done.11.refs_3_), channel_id=1, source_target_pairs={{8,0},{16,8},{24,16},{28,24},{20,28},{12,20},{4,12},{0,4},{9,1},{1... | collective-permute-start | bytes 2359304 | tf_op jit(solution)/shard_map/ppermute | solution.py:641
  198.5 52.8 %collective-permute-start.20 = (bf16[256,1536]{1,0:T(8,128)(2,1)}, bf16[256,1536]{1,0:T(8,128)(2,1)}, u32[]{:S(2)}, u32[]{:S(2)}) collective-permute-start(bf16[256,1536]{1,0:T(8,128)(2,1)} %collective-permute-done.19.refs_1_), channel_id=1, source_target_pairs={{0,8},{8,16},{16,24},{24,28},{28,20},{20,12},{12,4},{4,0},{1,9},{9... | collective-permute-start | bytes 2359304 | tf_op jit(solution)/shard_map/ppermute | solution.py:640
  200.0 52.9 %collective-permute-start.23 = (bf16[256,1536]{1,0:T(8,128)(2,1)}, bf16[256,1536]{1,0:T(8,128)(2,1)}, u32[]{:S(2)}, u32[]{:S(2)}) collective-permute-start(bf16[256,1536]{1,0:T(8,128)(2,1)} %collective-permute-done.22.refs_2_), channel_id=1, source_target_pairs={{8,0},{16,8},{24,16},{28,24},{20,28},{12,20},{4,12},{0,4},{9,1},{1... | collective-permute-start | bytes 2359304 | tf_op jit(solution)/shard_map/ppermute | solution.py:641
  213.7 39.7 %collective-permute-start.8 = (bf16[256,1536]{1,0:T(8,128)(2,1)}, bf16[256,1536]{1,0:T(8,128)(2,1)}, u32[]{:S(2)}, u32[]{:S(2)}) collective-permute-start(bf16[256,1536]{1,0:T(8,128)(2,1)} %collective-permute-done.7.refs_0_), channel_id=1, source_target_pairs={{0,8},{8,16},{16,24},{24,28},{28,20},{20,12},{12,4},{4,0},{1,9},{9... | collective-permute-start | bytes 2359304 | tf_op jit(solution)/shard_map/ppermute | solution.py:640
  250.8 40.1 %collective-permute-start.13 = (bf16[256,1536]{1,0:T(8,128)(2,1)}, bf16[256,1536]{1,0:T(8,128)(2,1)S(1)}, u32[]{:S(2)}, u32[]{:S(2)}) collective-permute-start(bf16[256,1536]{1,0:T(8,128)(2,1)} %collective-permute-done.12.refs_3_), channel_id=1, source_target_pairs={{8,0},{16,8},{24,16},{28,24},{20,28},{12,20},{4,12},{0,4},{9,1},{1... | collective-permute-start | bytes 2359304 | tf_op jit(solution)/shard_map/ppermute | solution.py:641
  251.3 40.1 %collective-permute-start.21 = (bf16[256,1536]{1,0:T(8,128)(2,1)}, bf16[256,1536]{1,0:T(8,128)(2,1)}, u32[]{:S(2)}, u32[]{:S(2)}) collective-permute-start(bf16[256,1536]{1,0:T(8,128)(2,1)} %collective-permute-done.20.refs_1_), channel_id=1, source_target_pairs={{0,8},{8,16},{16,24},{24,28},{28,20},{20,12},{12,4},{4,0},{1,9},{9... | collective-permute-start | bytes 2359304 | tf_op jit(solution)/shard_map/ppermute | solution.py:640
  252.9 38.6 %collective-permute-start.24 = (bf16[256,1536]{1,0:T(8,128)(2,1)}, bf16[256,1536]{1,0:T(8,128)(2,1)}, u32[]{:S(2)}, u32[]{:S(2)}) collective-permute-start(bf16[256,1536]{1,0:T(8,128)(2,1)} %collective-permute-done.23.refs_2_), channel_id=1, source_target_pairs={{8,0},{16,8},{24,16},{28,24},{20,28},{12,20},{4,12},{0,4},{9,1},{1... | collective-permute-start | bytes 2359304 | tf_op jit(solution)/shard_map/ppermute | solution.py:641
  253.3 36.1 %collective-permute-start.9 = (bf16[256,1536]{1,0:T(8,128)(2,1)}, bf16[256,1536]{1,0:T(8,128)(2,1)S(1)}, u32[]{:S(2)}, u32[]{:S(2)}) collective-permute-start(bf16[256,1536]{1,0:T(8,128)(2,1)} %collective-permute-done.8.refs_0_), channel_id=1, source_target_pairs={{0,8},{8,16},{16,24},{24,28},{28,20},{20,12},{12,4},{4,0},{1,9},{9... | collective-permute-start | bytes 2359304 | tf_op jit(solution)/shard_map/ppermute | solution.py:640
  289.4 38.8 %collective-permute-start.10 = (bf16[256,1536]{1,0:T(8,128)(2,1)S(1)}, bf16[256,1536]{1,0:T(8,128)(2,1)S(1)}, u32[]{:S(2)}, u32[]{:S(2)}) collective-permute-start(bf16[256,1536]{1,0:T(8,128)(2,1)S(1)} %collective-permute-done.9.refs_0_), channel_id=1, source_target_pairs={{0,8},{8,16},{16,24},{24,28},{28,20},{20,12},{12,4},{4,0},{1,9},{9... | collective-permute-start | bytes 2359304 | tf_op jit(solution)/shard_map/ppermute | solution.py:644
  290.9 37.2 %collective-permute-start.14 = (bf16[256,1536]{1,0:T(8,128)(2,1)S(1)}, bf16[256,1536]{1,0:T(8,128)(2,1)S(1)}, u32[]{:S(2)}, u32[]{:S(2)}) collective-permute-start(bf16[256,1536]{1,0:T(8,128)(2,1)S(1)} %collective-permute-done.13.refs_3_), channel_id=1, source_target_pairs={{8,0},{16,8},{24,16},{28,24},{20,28},{12,20},{4,12},{0,4},{9,1},{1... | collective-permute-start | bytes 2359304 | tf_op jit(solution)/shard_map/ppermute | solution.py:644
  325.4 31.6 %collective-permute-start.28 = (bf16[256,1536]{1,0:T(8,128)(2,1)}, bf16[256,1536]{1,0:T(8,128)(2,1)}, u32[]{:S(2)}, u32[]{:S(2)}) collective-permute-start(bf16[256,1536]{1,0:T(8,128)(2,1)} %get-tuple-element.174), channel_id=1, source_target_pairs={{0,8},{8,16},{16,24},{24,28},{28,20},{20,12},{12,4},{4,0},{1,9},{9... | collective-permute-start | bytes 2359304 | tf_op jit(solution)/shard_map/ppermute | solution.py:666
  326.6 27.3 %collective-permute-start.29 = (bf16[256,1536]{1,0:T(8,128)(2,1)}, bf16[256,1536]{1,0:T(8,128)(2,1)}, u32[]{:S(2)}, u32[]{:S(2)}) collective-permute-start(bf16[256,1536]{1,0:T(8,128)(2,1)} %get-tuple-element.176), channel_id=1, source_target_pairs={{8,0},{16,8},{24,16},{28,24},{20,28},{12,20},{4,12},{0,4},{9,1},{1... | collective-permute-start | bytes 2359304 | tf_op jit(solution)/shard_map/ppermute | solution.py:667
  390.3 19.6 %collective-permute-start.27 = (bf16[256,1536]{1,0:T(8,128)(2,1)S(1)}, bf16[256,1536]{1,0:T(8,128)(2,1)S(1)}, u32[]{:S(2)}, u32[]{:S(2)}) collective-permute-start(bf16[256,1536]{1,0:T(8,128)(2,1)S(1)} %add_convert_fusion.24), channel_id=1, source_target_pairs={{0,8},{8,16},{16,24},{24,28},{28,20},{20,12},{12,4},{4,0},{1,9},{9... | collective-permute-start | bytes 2359304 | tf_op jit(solution)/shard_map/ppermute | solution.py:666
  391.1 18.8 %collective-permute-start.30 = (bf16[256,1536]{1,0:T(8,128)(2,1)S(1)}, bf16[256,1536]{1,0:T(8,128)(2,1)S(1)}, u32[]{:S(2)}, u32[]{:S(2)}) collective-permute-start(bf16[256,1536]{1,0:T(8,128)(2,1)S(1)} %add_convert_fusion.23), channel_id=1, source_target_pairs={{8,0},{16,8},{24,16},{28,24},{20,28},{12,20},{4,12},{0,4},{9,1},{1... | collective-permute-start | bytes 2359304 | tf_op jit(solution)/shard_map/ppermute | solution.py:667
  411.8 23.3 %collective-permute-start.34 = (bf16[256,1536]{1,0:T(8,128)(2,1)S(1)}, bf16[256,1536]{1,0:T(8,128)(2,1)S(1)}, u32[]{:S(2)}, u32[]{:S(2)}) collective-permute-start(bf16[256,1536]{1,0:T(8,128)(2,1)S(1)} %add_convert_fusion.19), channel_id=1, source_target_pairs={{8,0},{16,8},{24,16},{28,24},{20,28},{12,20},{4,12},{0,4},{9,1},{1... | collective-permute-start | bytes 2359304 | tf_op jit(solution)/shard_map/ppermute | solution.py:667
  412.9 28.9 %collective-permute-start.33 = (bf16[256,1536]{1,0:T(8,128)(2,1)S(1)}, bf16[256,1536]{1,0:T(8,128)(2,1)S(1)}, u32[]{:S(2)}, u32[]{:S(2)}) collective-permute-start(bf16[256,1536]{1,0:T(8,128)(2,1)S(1)} %copy-done.61), channel_id=1, source_target_pairs={{8,0},{16,8},{24,16},{28,24},{20,28},{12,20},{4,12},{0,4},{9,1},{1... | collective-permute-start | bytes 2359304 | tf_op jit(solution)/shard_map/ppermute | solution.py:667
  413.5 29.4 %collective-permute-start.32 = (bf16[256,1536]{1,0:T(8,128)(2,1)S(1)}, bf16[256,1536]{1,0:T(8,128)(2,1)S(1)}, u32[]{:S(2)}, u32[]{:S(2)}) collective-permute-start(bf16[256,1536]{1,0:T(8,128)(2,1)S(1)} %add_convert_fusion.21), channel_id=1, source_target_pairs={{0,8},{8,16},{16,24},{24,28},{28,20},{20,12},{12,4},{4,0},{1,9},{9... | collective-permute-start | bytes 2359304 | tf_op jit(solution)/shard_map/ppermute | solution.py:666
  414.9 31.4 %collective-permute-start.31 = (bf16[256,1536]{1,0:T(8,128)(2,1)S(1)}, bf16[256,1536]{1,0:T(8,128)(2,1)S(1)}, u32[]{:S(2)}, u32[]{:S(2)}) collective-permute-start(bf16[256,1536]{1,0:T(8,128)(2,1)S(1)} %add_convert_fusion.22), channel_id=1, source_target_pairs={{0,8},{8,16},{16,24},{24,28},{28,20},{20,12},{12,4},{4,0},{1,9},{9... | collective-permute-start | bytes 2359304 | tf_op jit(solution)/shard_map/ppermute | solution.py:666
  447.4 25.3 %collective-permute-start.35 = (bf16[256,1536]{1,0:T(8,128)(2,1)}, bf16[256,1536]{1,0:T(8,128)(2,1)}, u32[]{:S(2)}, u32[]{:S(2)}) collective-permute-start(bf16[256,1536]{1,0:T(8,128)(2,1)} %add_convert_fusion.18), channel_id=1, source_target_pairs={{0,8},{8,16},{16,24},{24,28},{28,20},{20,12},{12,4},{4,0},{1,9},{9... | collective-permute-start | bytes 2359304 | tf_op jit(solution)/shard_map/ppermute | solution.py:666
  448.3 24.8 %collective-permute-start.36 = (bf16[256,1536]{1,0:T(8,128)(2,1)}, bf16[256,1536]{1,0:T(8,128)(2,1)}, u32[]{:S(2)}, u32[]{:S(2)}) collective-permute-start(bf16[256,1536]{1,0:T(8,128)(2,1)} %add_convert_fusion.16), channel_id=1, source_target_pairs={{8,0},{16,8},{24,16},{28,24},{20,28},{12,20},{4,12},{0,4},{9,1},{1... | collective-permute-start | bytes 2359304 | tf_op jit(solution)/shard_map/ppermute | solution.py:667
  450.1 18.1 %all-to-all-start = ((f32[8,4,512]{2,1,0:T(4,128)}), f32[8,4,512]{2,1,0:T(4,128)S(1)}, u32[]{:S(2)}, u32[]{:S(2)}) async-start(f32[8,4,512]{2,1,0:T(4,128)} %broadcast_select_fusion), calls=%async_computation | async-start | bytes 131072 | tf_op jit(solution)/shard_map/all_to_all | solution.py:801
  472.6 35.5 %collective-permute-start.74 = (bf16[2,4,384,512]{3,2,1,0:T(8,128)(2,1)}, bf16[2,4,384,512]{3,2,1,0:T(8,128)(2,1)}, u32[]{:S(2)}, u32[]{:S(2)}) collective-permute-start(bf16[2,4,384,512]{3,2,1,0:T(8,128)(2,1)} %copy-done.8), channel_id=1, source_target_pairs={{0,1},{1,0},{2,3},{3,2},{4,5},{5,4},{6,7},{7,6},{8,9},{9,8},{10,11... | collective-permute-start | bytes 9437192 | tf_op jit(solution)/shard_map/ppermute | solution.py:677
  472.7 39.2 %collective-permute-start.72 = (bf16[2,4,384,512]{3,2,1,0:T(8,128)(2,1)}, bf16[2,4,384,512]{3,2,1,0:T(8,128)(2,1)}, u32[]{:S(2)}, u32[]{:S(2)}) collective-permute-start(bf16[2,4,384,512]{3,2,1,0:T(8,128)(2,1)} %copy-done.6), channel_id=1, source_target_pairs={{0,1},{1,0},{2,3},{3,2},{4,5},{5,4},{6,7},{7,6},{8,9},{9,8},{10,11... | collective-permute-start | bytes 9437192 | tf_op jit(solution)/shard_map/ppermute | solution.py:677
  473.2 79.8 %collective-permute-start.76 = (bf16[2,4,384,512]{3,2,1,0:T(8,128)(2,1)}, bf16[2,4,384,512]{3,2,1,0:T(8,128)(2,1)}, u32[]{:S(2)}, u32[]{:S(2)}) collective-permute-start(bf16[2,4,384,512]{3,2,1,0:T(8,128)(2,1)} %copy-done.7), channel_id=1, source_target_pairs={{0,1},{1,0},{2,3},{3,2},{4,5},{5,4},{6,7},{7,6},{8,9},{9,8},{10,11... | collective-permute-start | bytes 9437192 | tf_op jit(solution)/shard_map/ppermute | solution.py:677
  499.6 82.2 %collective-permute-start.53 = (bf16[512,1536]{1,0:T(8,128)(2,1)}, bf16[512,1536]{1,0:T(8,128)(2,1)}, u32[]{:S(2)}, u32[]{:S(2)}) collective-permute-start(bf16[512,1536]{1,0:T(8,128)(2,1)} %get-tuple-element.310.dba_ref), channel_id=1, source_target_pairs={{0,2},{2,0},{1,3},{3,1},{4,6},{6,4},{5,7},{7,5},{8,10},{10,8},{9,1... | collective-permute-start | bytes 4718600 | tf_op jit(solution)/shard_map/ppermute | solution.py:681
  501.4 19.6 %collective-permute-start.39 = (bf16[256,1536]{1,0:T(8,128)(2,1)}, bf16[256,1536]{1,0:T(8,128)(2,1)}, u32[]{:S(2)}, u32[]{:S(2)}) collective-permute-start(bf16[256,1536]{1,0:T(8,128)(2,1)} %get-tuple-element.207), channel_id=1, source_target_pairs={{0,8},{8,16},{16,24},{24,28},{28,20},{20,12},{12,4},{4,0},{1,9},{9... | collective-permute-start | bytes 2359304 | tf_op jit(solution)/shard_map/ppermute | solution.py:666
  508.2 49.4 %collective-permute-start.55 = (bf16[512,1536]{1,0:T(8,128)(2,1)}, bf16[512,1536]{1,0:T(8,128)(2,1)S(1)}, u32[]{:S(2)}, u32[]{:S(2)}) collective-permute-start(bf16[512,1536]{1,0:T(8,128)(2,1)} %get-tuple-element.310.dba_ref), channel_id=1, source_target_pairs={{0,1},{1,0},{2,3},{3,2},{4,5},{5,4},{6,7},{7,6},{8,9},{9,8},{10,11... | collective-permute-start | bytes 4718600 | tf_op jit(solution)/shard_map/ppermute | solution.py:677
  511.9 20.1 %collective-permute-start.43 = (bf16[256,1536]{1,0:T(8,128)(2,1)S(1)}, bf16[256,1536]{1,0:T(8,128)(2,1)S(1)}, u32[]{:S(2)}, u32[]{:S(2)}) collective-permute-start(bf16[256,1536]{1,0:T(8,128)(2,1)S(1)} %copy-done.88), channel_id=1, source_target_pairs={{8,0},{16,8},{24,16},{28,24},{20,28},{12,20},{4,12},{0,4},{9,1},{1... | collective-permute-start | bytes 2359304 | tf_op jit(solution)/shard_map/ppermute | solution.py:667
  521.0 18.4 %collective-permute-start.46 = (bf16[256,1536]{1,0:T(8,128)(2,1)S(1)}, bf16[256,1536]{1,0:T(8,128)(2,1)S(1)}, u32[]{:S(2)}, u32[]{:S(2)}) collective-permute-start(bf16[256,1536]{1,0:T(8,128)(2,1)S(1)} %copy-done.87), channel_id=1, source_target_pairs={{0,8},{8,16},{16,24},{24,28},{28,20},{20,12},{12,4},{4,0},{1,9},{9... | collective-permute-start | bytes 2359304 | tf_op jit(solution)/shard_map/ppermute | solution.py:666
  532.0 19.4 %collective-permute-start.49 = (bf16[256,1536]{1,0:T(8,128)(2,1)S(1)}, bf16[256,1536]{1,0:T(8,128)(2,1)S(1)}, u32[]{:S(2)}, u32[]{:S(2)}) collective-permute-start(bf16[256,1536]{1,0:T(8,128)(2,1)S(1)} %copy-done.89), channel_id=1, source_target_pairs={{8,0},{16,8},{24,16},{28,24},{20,28},{12,20},{4,12},{0,4},{9,1},{1... | collective-permute-start | bytes 2359304 | tf_op jit(solution)/shard_map/ppermute | solution.py:667
  539.5 68.1 %collective-permute-start.75 = (bf16[4,384,512]{2,1,0:T(8,128)(2,1)}, bf16[4,384,512]{2,1,0:T(8,128)(2,1)}, u32[]{:S(2)}, u32[]{:S(2)}) collective-permute-start(bf16[4,384,512]{2,1,0:T(8,128)(2,1)} %fusion.8), channel_id=1, source_target_pairs={{0,2},{2,0},{1,3},{3,1},{4,6},{6,4},{5,7},{7,5},{8,10},{10,8},{9,1... | collective-permute-start | bytes 4718600 | tf_op jit(solution)/shard_map/ppermute | solution.py:681
  551.3 61.1 %collective-permute-start.73 = (bf16[4,384,512]{2,1,0:T(8,128)(2,1)}, bf16[4,384,512]{2,1,0:T(8,128)(2,1)}, u32[]{:S(2)}, u32[]{:S(2)}) collective-permute-start(bf16[4,384,512]{2,1,0:T(8,128)(2,1)} %fusion.7), channel_id=1, source_target_pairs={{0,2},{2,0},{1,3},{3,1},{4,6},{6,4},{5,7},{7,5},{8,10},{10,8},{9,1... | collective-permute-start | bytes 4718600 | tf_op jit(solution)/shard_map/ppermute | solution.py:681
  553.0 34.1 %collective-permute-start.40 = (bf16[256,1536]{1,0:T(8,128)(2,1)}, bf16[256,1536]{1,0:T(8,128)(2,1)}, u32[]{:S(2)}, u32[]{:S(2)}) collective-permute-start(bf16[256,1536]{1,0:T(8,128)(2,1)} %add_convert_fusion.14), channel_id=1, source_target_pairs={{0,8},{8,16},{16,24},{24,28},{28,20},{20,12},{12,4},{4,0},{1,9},{9... | collective-permute-start | bytes 2359304 | tf_op jit(solution)/shard_map/ppermute | solution.py:666
  557.5 31.5 %collective-permute-start.44 = (bf16[256,1536]{1,0:T(8,128)(2,1)}, bf16[256,1536]{1,0:T(8,128)(2,1)}, u32[]{:S(2)}, u32[]{:S(2)}) collective-permute-start(bf16[256,1536]{1,0:T(8,128)(2,1)} %add_convert_fusion.11), channel_id=1, source_target_pairs={{8,0},{16,8},{24,16},{28,24},{20,28},{12,20},{4,12},{0,4},{9,1},{1... | collective-permute-start | bytes 2359304 | tf_op jit(solution)/shard_map/ppermute | solution.py:667
  581.8 20.5 %collective-permute-start.47 = (bf16[256,1536]{1,0:T(8,128)(2,1)S(1)}, bf16[256,1536]{1,0:T(8,128)(2,1)S(1)}, u32[]{:S(2)}, u32[]{:S(2)}) collective-permute-start(bf16[256,1536]{1,0:T(8,128)(2,1)S(1)} %copy-done.63), channel_id=1, source_target_pairs={{0,8},{8,16},{16,24},{24,28},{28,20},{20,12},{12,4},{4,0},{1,9},{9... | collective-permute-start | bytes 2359304 | tf_op jit(solution)/shard_map/ppermute | solution.py:666
  589.0 115.7 %collective-permute-start.77 = (bf16[4,384,512]{2,1,0:T(8,128)(2,1)}, bf16[4,384,512]{2,1,0:T(8,128)(2,1)}, u32[]{:S(2)}, u32[]{:S(2)}) collective-permute-start(bf16[4,384,512]{2,1,0:T(8,128)(2,1)} %fusion.9), channel_id=1, source_target_pairs={{0,2},{2,0},{1,3},{3,1},{4,6},{6,4},{5,7},{7,5},{8,10},{10,8},{9,1... | collective-permute-start | bytes 4718600 | tf_op jit(solution)/shard_map/ppermute | solution.py:681
  602.3 23.7 %collective-permute-start.54 = (bf16[512,1536]{1,0:T(8,128)(2,1)}, bf16[512,1536]{1,0:T(8,128)(2,1)}, u32[]{:S(2)}, u32[]{:S(2)}) collective-permute-start(bf16[512,1536]{1,0:T(8,128)(2,1)} %collective-permute-done.53.dba_ref), channel_id=1, source_target_pairs={{0,1},{1,0},{2,3},{3,2},{4,5},{5,4},{6,7},{7,6},{8,9},{9,8},{10,11... | collective-permute-start | bytes 4718600 | tf_op jit(solution)/shard_map/ppermute | solution.py:677
  604.9 18.5 %collective-permute-start.41 = (bf16[256,1536]{1,0:T(8,128)(2,1)S(1)}, bf16[256,1536]{1,0:T(8,128)(2,1)S(1)}, u32[]{:S(2)}, u32[]{:S(2)}) collective-permute-start(bf16[256,1536]{1,0:T(8,128)(2,1)S(1)} %add_convert_fusion.13), channel_id=1, source_target_pairs={{0,8},{8,16},{16,24},{24,28},{28,20},{20,12},{12,4},{4,0},{1,9},{9... | collective-permute-start | bytes 2359304 | tf_op jit(solution)/shard_map/ppermute | solution.py:666
  607.5 118.4 %collective-permute-start.45 = (bf16[256,1536]{1,0:T(8,128)(2,1)}, bf16[256,1536]{1,0:T(8,128)(2,1)}, u32[]{:S(2)}, u32[]{:S(2)}) collective-permute-start(bf16[256,1536]{1,0:T(8,128)(2,1)} %add_convert_fusion.10), channel_id=1, source_target_pairs={{8,0},{16,8},{24,16},{28,24},{20,28},{12,20},{4,12},{0,4},{9,1},{1... | collective-permute-start | bytes 2359304 | tf_op jit(solution)/shard_map/ppermute | solution.py:667
  612.5 81.8 %collective-permute-start.51 = (bf16[256,1536]{1,0:T(8,128)(2,1)}, bf16[256,1536]{1,0:T(8,128)(2,1)}, u32[]{:S(2)}, u32[]{:S(2)}) collective-permute-start(bf16[256,1536]{1,0:T(8,128)(2,1)} %add_convert_fusion.6), channel_id=1, source_target_pairs={{8,0},{16,8},{24,16},{28,24},{20,28},{12,20},{4,12},{0,4},{9,1},{1... | collective-permute-start | bytes 2359304 | tf_op jit(solution)/shard_map/ppermute | solution.py:667
  624.5 103.1 %collective-permute-start.42 = (bf16[256,1536]{1,0:T(8,128)(2,1)}, bf16[256,1536]{1,0:T(8,128)(2,1)}, u32[]{:S(2)}, u32[]{:S(2)}) collective-permute-start(bf16[256,1536]{1,0:T(8,128)(2,1)} %add_convert_fusion.12), channel_id=1, source_target_pairs={{0,8},{8,16},{16,24},{24,28},{28,20},{20,12},{12,4},{4,0},{1,9},{9... | collective-permute-start | bytes 2359304 | tf_op jit(solution)/shard_map/ppermute | solution.py:666
  684.1 55.8 %collective-permute-start.56 = (bf16[1024,1536]{1,0:T(8,128)(2,1)}, bf16[1024,1536]{1,0:T(8,128)(2,1)}, u32[]{:S(2)}, u32[]{:S(2)}) collective-permute-start(bf16[1024,1536]{1,0:T(8,128)(2,1)} %get-tuple-element.243), channel_id=1, source_target_pairs={{0,1},{1,0},{2,3},{3,2},{4,5},{5,4},{6,7},{7,6},{8,9},{9,8},{10,11... | collective-permute-start | bytes 9437192 | tf_op jit(solution)/shard_map/ppermute | solution.py:677
  719.0 47.6 %all-to-all-start.1 = ((f32[32,1,48]{2,1,0:T(1,128)}), f32[32,1,48]{2,1,0:T(1,128)}, u32[]{:S(2)}, u32[]{:S(2)}) async-start(f32[32,1,48]{2,1,0:T(1,128)} %bitcast.149), calls=%async_computation.1 | async-start | bytes 32768 | tf_op jit(solution)/shard_map/all_to_all | solution.py:845
  730.0 24.4 %collective-permute-start.48 = (bf16[256,1536]{1,0:T(8,128)(2,1)S(1)}, bf16[256,1536]{1,0:T(8,128)(2,1)S(1)}, u32[]{:S(2)}, u32[]{:S(2)}) collective-permute-start(bf16[256,1536]{1,0:T(8,128)(2,1)S(1)} %copy-done.54), channel_id=1, source_target_pairs={{0,8},{8,16},{16,24},{24,28},{28,20},{20,12},{12,4},{4,0},{1,9},{9... | collective-permute-start | bytes 2359304 | tf_op jit(solution)/shard_map/ppermute | solution.py:666
  733.4 22.5 %collective-permute-start.52 = (bf16[256,1536]{1,0:T(8,128)(2,1)S(1)}, bf16[256,1536]{1,0:T(8,128)(2,1)S(1)}, u32[]{:S(2)}, u32[]{:S(2)}) collective-permute-start(bf16[256,1536]{1,0:T(8,128)(2,1)S(1)} %copy-done.57), channel_id=1, source_target_pairs={{8,0},{16,8},{24,16},{28,24},{20,28},{12,20},{4,12},{0,4},{9,1},{1... | collective-permute-start | bytes 2359304 | tf_op jit(solution)/shard_map/ppermute | solution.py:667
  737.9 20.8 %collective-permute-start.60 = (bf16[96,1024]{1,0:T(8,128)(2,1)S(1)}, bf16[96,1024]{1,0:T(8,128)(2,1)S(1)}, u32[]{:S(2)}, u32[]{:S(2)}) collective-permute-start(bf16[96,1024]{1,0:T(8,128)(2,1)S(1)} %get-tuple-element.323), channel_id=1, source_target_pairs={{0,8},{8,16},{16,24},{24,28},{28,20},{20,12},{12,4},{4,0},{1,9},{9... | collective-permute-start | bytes 589832 | tf_op jit(solution)/shard_map/ppermute | solution.py:666
  738.3 20.4 %collective-permute-start.63 = (bf16[96,1024]{1,0:T(8,128)(2,1)S(1)}, bf16[96,1024]{1,0:T(8,128)(2,1)S(1)}, u32[]{:S(2)}, u32[]{:S(2)}) collective-permute-start(bf16[96,1024]{1,0:T(8,128)(2,1)S(1)} %get-tuple-element.322), channel_id=1, source_target_pairs={{8,0},{16,8},{24,16},{28,24},{20,28},{12,20},{4,12},{0,4},{9,1},{1... | collective-permute-start | bytes 589832 | tf_op jit(solution)/shard_map/ppermute | solution.py:667
  740.0 21.8 %collective-permute-start.67 = (bf16[96,1024]{1,0:T(8,128)(2,1)S(1)}, bf16[96,1024]{1,0:T(8,128)(2,1)S(1)}, u32[]{:S(2)}, u32[]{:S(2)}) collective-permute-start(bf16[96,1024]{1,0:T(8,128)(2,1)S(1)} %get-tuple-element.321), channel_id=1, source_target_pairs={{0,8},{8,16},{16,24},{24,28},{28,20},{20,12},{12,4},{4,0},{1,9},{9... | collective-permute-start | bytes 589832 | tf_op jit(solution)/shard_map/ppermute | solution.py:666
  755.9 34.2 %collective-permute-start.57 = (bf16[512,1536]{1,0:T(8,128)(2,1)}, bf16[512,1536]{1,0:T(8,128)(2,1)}, u32[]{:S(2)}, u32[]{:S(2)}) collective-permute-start(bf16[512,1536]{1,0:T(8,128)(2,1)} %add_convert_fusion.3), channel_id=1, source_target_pairs={{0,2},{2,0},{1,3},{3,1},{4,6},{6,4},{5,7},{7,5},{8,10},{10,8},{9,1... | collective-permute-start | bytes 4718600 | tf_op jit(solution)/shard_map/ppermute | solution.py:681
  (113 other events, 1170.6 us)

commit v2 on v1

--- a/solution.py
+++ b/solution.py
@@ -34,9 +34,12 @@
     )
 
 
-def cost(gflop, mb):
+WEIGHT = 1.0
+
+
+def takes(us):
     return pl.CostEstimate(
-        flops=int(gflop * 1e9), bytes_accessed=int(mb * 1e6), transcendentals=0
+        flops=int(us * WEIGHT * 1.153e9), bytes_accessed=1_000_000, transcendentals=0
     )
 
 
@@ -116,7 +119,7 @@
             jax.ShapeDtypeStruct((kh, HD, rows), bf16),
         ],
         compiler_params=params(48),
-        cost_estimate=cost(13, 20),
+        cost_estimate=takes(99),
         name="norm_qkv",
     )(x, gain, wq, wk, wv, cos, sin)
 
@@ -228,7 +231,7 @@
         ],
         input_output_aliases=aliases,
         compiler_params=params(56),
-        cost_estimate=cost(17, 10),
+        cost_estimate=takes(1),
         name="attend",
     )(order, *args)
 
@@ -355,14 +358,13 @@
         ),
         out_shape=out_shape,
         input_output_aliases=aliases,
-        compiler_params=params(58),
-        cost_estimate=cost(22, 20),
+        compiler_params=params(34),
+        cost_estimate=takes(27),
         name="attend_back",
     )(order, *args)
 
 
-def qkv_back_kernel(order_ref, dq_ref, dkv_ref, x_ref, wq_ref, wk_ref, wv_ref,
-                    send_ref, keep_ref, gain_ref):
+def qkv_back_kernel(order_ref, dq_ref, dkv_ref, wq_ref, wk_ref, wv_ref, send_ref, keep_ref):
     step = pl.program_id(0)
     half = pl.num_programs(0) // 2
     kc = wk_ref.shape[1]
@@ -370,24 +372,19 @@
         mm(dq_ref[...], wq_ref[...], NT)
         + mm(dkv_ref[:, :kc], wk_ref[...], NT)
         + mm(dkv_ref[:, kc:], wv_ref[...], NT)
-    )
+    ).astype(bf16)
 
     @pl.when(step < half)
     def _():
-        send_ref[...] = total.astype(bf16)
+        send_ref[...] = total
 
     @pl.when(step >= half)
     def _():
-        keep_ref[...] = total.astype(bf16)
-
-    x = x_ref[...].astype(f32)
-    inv = lax.rsqrt(jnp.mean(x * x, axis=-1, keepdims=True) + EPS)
-    gain = jnp.sum(total * (x * inv), axis=0, keepdims=True)
-    gain_ref[...] = jnp.where(step == 0, gain, gain_ref[...] + gain)
-
-
-def qkv_back_call(order, dq, dkv, x, wq, wk, wv):
-    rows, width = x.shape
+        keep_ref[...] = total
+
+
+def qkv_back_call(order, dq, dkv, wq, wk, wv):
+    rows, width = dq.shape[0], wq.shape[0]
     steps = order.shape[0]
     rb = rows // steps
     half = steps // 2
@@ -399,35 +396,87 @@
             in_specs=[
                 pl.BlockSpec((rb, dq.shape[1]), lambda s, o: (o[s], 0)),
                 pl.BlockSpec((rb, dkv.shape[1]), lambda s, o: (o[s], 0)),
-                pl.BlockSpec((rb, width), lambda s, o: (o[s], 0)),
                 whole(wq.shape), whole(wk.shape), whole(wv.shape),
             ],
             out_specs=[
                 pl.BlockSpec((rb, width), lambda s, o: (jnp.minimum(s, half - 1), 0)),
                 pl.BlockSpec((rb, width), lambda s, o: (jnp.maximum(s - half, 0), 0)),
-                whole((1, width)),
             ],
         ),
-        out_shape=[
-            jax.ShapeDtypeStruct((rows // 2, width), bf16),
-            jax.ShapeDtypeStruct((rows // 2, width), bf16),
-            jax.ShapeDtypeStruct((1, width), f32),
-        ],
-        compiler_params=params(48),
-        cost_estimate=cost(6, 20),
+        out_shape=[jax.ShapeDtypeStruct((rows // 2, width), bf16)] * 2,
+        compiler_params=params(20),
+        cost_estimate=takes(9),
         name="qkv_back",
-    )(order, dq, dkv, x, wq, wk, wv)
+    )(order, dq, dkv, wq, wk, wv)
+
+
+def dense_grad_kernel(order_ref, n_ref, dq_ref, dkv_ref, db0_ref, db1_ref, db2_ref, db3_ref,
+                      heads_ref, first_ref, second_ref, dlog_ref, gain2_ref, gain_ref,
+                      wq_ref, wk_ref, wv_ref, out_ref):
+    qc, kvc = dq_ref.shape[1], dkv_ref.shape[1]
+    quarter = db0_ref.shape[0]
+    normed = n_ref[...]
+    query, key_value = mm(normed, dq_ref[...], TN), mm(normed, dkv_ref[...], TN)
+    out_ref[:, :qc] = query.astype(bf16)
+    out_ref[:, qc:qc + kvc] = key_value.astype(bf16)
+    first = (
+        jnp.sum(query * wq_ref[...].astype(f32), axis=1, keepdims=True)
+        + jnp.sum(key_value[:, :kvc // 2] * wk_ref[...].astype(f32), axis=1, keepdims=True)
+        + jnp.sum(key_value[:, kvc // 2:] * wv_ref[...].astype(f32), axis=1, keepdims=True)
+    )
+    wo = None
+    for j, db_ref in enumerate((db0_ref, db1_ref, db2_ref, db3_ref)):
+        at = pl.multiple_of(order_ref[j] * quarter, quarter)
+        part = mm(db_ref[...], heads_ref[pl.ds(at, quarter), :], TN)
+        wo = part if wo is None else wo + part
+    out_ref[:, qc + kvc:2 * qc + kvc] = wo.astype(bf16)
+    half = first_ref.shape[0]
+    router = (
+        mm(first_ref[...], dlog_ref[:half, :], TN) + mm(second_ref[...], dlog_ref[half:, :], TN)
+    )
+    cols = router.shape[0]
+    column = lambda row: jnp.transpose(jnp.broadcast_to(row.astype(f32), (8, cols)))[:, :1]
+    pad = out_ref.shape[1] - (2 * qc + kvc) - router.shape[1] - 2
+    out_ref[:, 2 * qc + kvc:] = jnp.concatenate(
+        [router, column(gain2_ref[...]), first / column(gain_ref[...]), jnp.zeros((cols, pad), f32)],
+        axis=1,
+    ).astype(bf16)
+
+
+def dense_grad_call(order, normed1, dq, dkv, dbs, heads, normed2, d_logits, gain2, gain, ws):
+    rows, width = normed1.shape
+    qc, kvc = dq.shape[1], dkv.shape[1]
+    cols = width // 6
+    lanes = 2 * qc + kvc + -(-(d_logits.shape[1] + 2) // 128) * 128
+    whole = lambda a: pl.BlockSpec(a.shape, lambda s, o: (0, 0))
+    block = lambda a: pl.BlockSpec((a.shape[0], cols), lambda s, o: (0, s))
+    lines = lambda a: pl.BlockSpec((cols, a.shape[1]), lambda s, o: (s, 0))
+    return pl.pallas_call(
+        dense_grad_kernel,
+        grid_spec=pltpu.PrefetchScalarGridSpec(
+            num_scalar_prefetch=1,
+            grid=(6,),
+            in_specs=[block(normed1), whole(dq), whole(dkv), *map(block, dbs), whole(heads),
+                      *map(block, normed2), whole(d_logits), block(gain2), block(gain),
+                      *map(lines, ws)],
+            out_specs=pl.BlockSpec((cols, lanes), lambda s, o: (s, 0)),
+        ),
+        out_shape=jax.ShapeDtypeStruct((width, lanes), bf16),
+        compiler_params=params(36),
+        cost_estimate=takes(13),
+        name="dense_grad",
+    )(order, normed1, dq, dkv, *dbs, heads, *normed2, d_logits, gain2, gain, *ws)
 
 
 def expert_kernel(sources, cap, experts, base_ref, *refs):
     x_refs, refs = refs[:2 * sources], refs[2 * sources:]
     c_refs, refs = refs[:sources], refs[sources:]
     router_ref, wg_ref, wu_ref, wd_ref = refs[:4]
-    refs = refs[-(4 * sources + 6 + 4):]
+    refs = refs[-(4 * sources + 5 + 5):]
     out_refs, refs = refs[:2 * sources], refs[2 * sources:]
     back_refs, refs = refs[:2 * sources], refs[2 * sources:]
-    (dmix_ref, xs_ref, cs_ref, act_ref, dg_ref, du_ref,
-     mix_ref, rank_ref, so_ref, sd_ref) = refs
+    (xs_ref, cs_ref, act_ref, dg_ref, du_ref,
+     mix_ref, rank_ref, dmix_ref, so_ref, sd_ref) = refs
     e = pl.program_id(0)
     local = pl.num_programs(0)
     half = x_refs[0].shape[0]
@@ -507,7 +556,17 @@
             for j in range(2):
                 part = pick[j * half:(j + 1) * half]
                 out_refs[2 * s + j][...] = mm(part, so_ref[s]).astype(bf16)
-                back_refs[2 * s + j][...] = mm(part, sd_ref[s]).astype(bf16)
+                back_refs[2 * s + j][:half, :] = mm(part, sd_ref[s]).astype(bf16)
+            row = lax.broadcasted_iota(i32, (extra, quarter), 0)
+            sums = [jnp.zeros((extra, quarter), f32) for _ in range(x_refs[0].shape[1] // quarter)]
+            for j in range(count):
+                line = dmix_ref[s, j:j + 1, :]
+                for piece in range(len(sums)):
+                    sums[piece] = jnp.where(row + piece * extra == base + j, line, sums[piece])
+            sums = jnp.concatenate(sums, axis=1)
+            high = sums.astype(bf16)
+            back_refs[2 * s + 1][half:half + extra, :] = high
+            back_refs[2 * s + 1][half + extra:, :] = (sums - high.astype(f32)).astype(bf16)
 
 
 def expert_call(base, xs, cs, router_t, wg, wu, wd, cap, at, of, held=None):
@@ -517,6 +576,7 @@
     half = xs[0][0].shape[0]
     quarter = 2 * half
     xs = [part for halves in xs for part in halves]
+    rows = [half] * (2 * sources) + [half, half + 2 * (cs[0].shape[0] - quarter)] * sources
     sizes = (width, width, hidden, hidden, hidden)
     whole = lambda shape: pl.BlockSpec(shape, lambda e, b: (0,) * len(shape))
     slot_spec = lambda n: pl.BlockSpec((1, sources * cap, n), lambda e, b: (e, at, 0))
@@ -531,7 +591,7 @@
     )
     aliases = {}
     if held is not None:
-        aliases = {1 + len(args) + j: 4 * sources + 1 + j for j in range(5)}
+        aliases = {1 + len(args) + j: 4 * sources + j for j in range(5)}
         args += list(held)
         in_specs += [pl.BlockSpec(memory_space=pl.ANY)] * 5
     outs = pl.pallas_call(
@@ -540,30 +600,27 @@
             num_scalar_prefetch=1,
             grid=(local,),
             in_specs=in_specs,
-            out_specs=[whole((half, width))] * (4 * sources)
-            + [whole((sources, local, quarter))]
-            + [slot_spec(n) for n in sizes],
+            out_specs=[whole((n, width)) for n in rows] + [slot_spec(n) for n in sizes],
             scratch_shapes=[
                 pltpu.VMEM((sources, experts, quarter), f32),
                 pltpu.VMEM((sources, experts, quarter), i32),
+                pltpu.VMEM((sources, local, quarter), f32),
                 pltpu.VMEM((sources, local * cap, width), bf16),
                 pltpu.VMEM((sources, local * cap, width), bf16),
             ],
         ),
-        out_shape=[jax.ShapeDtypeStruct((half, width), bf16)] * (4 * sources)
-        + [jax.ShapeDtypeStruct((sources, local, quarter), f32)]
+        out_shape=[jax.ShapeDtypeStruct((n, width), bf16) for n in rows]
         + [jax.ShapeDtypeStruct((local, of * cap, n), bf16) for n in sizes],
         input_output_aliases=aliases,
         compiler_params=params(60),
-        cost_estimate=cost(14 * sources, 20),
+        cost_estimate=takes(12 + 11 * sources),
         name="experts",
     )(base, *args)
     halves = lambda a: [(a[2 * s], a[2 * s + 1]) for s in range(sources)]
     return (
         halves(outs[:2 * sources]),
         halves(outs[2 * sources:4 * sources]),
-        outs[4 * sources],
-        outs[4 * sources + 1:],
+        outs[4 * sources:],
     )
 
 
@@ -580,40 +637,261 @@
         keep_ref[0, 0] = part
 
 
-def weight_grad_call(order, a, b):
-    local, slots, width = a.shape
-    hidden = b.shape[2]
+def weight_grad_call(order, a, b, cut_last=False):
+    local, slots, width = (b if cut_last else a).shape
     cut = width // 4
-    shape = jax.ShapeDtypeStruct((2, local, cut, hidden), bf16)
+    part = lambda x: pl.BlockSpec((1, slots, cut), lambda s, e, o: (e, 0, o[s]))
+    full = lambda x: pl.BlockSpec((1, slots, x.shape[2]), lambda s, e, o: (e, 0, 0))
+    dims = (a.shape[2], cut) if cut_last else (cut, b.shape[2])
+    shape = jax.ShapeDtypeStruct((2, local, *dims), bf16)
     return pl.pallas_call(
         weight_grad_kernel,
         grid_spec=pltpu.PrefetchScalarGridSpec(
             num_scalar_prefetch=1,
             grid=(4, local),
-            in_specs=[
-                pl.BlockSpec((1, slots, cut), lambda s, e, o: (e, 0, o[s])),
-                pl.BlockSpec((1, slots, hidden), lambda s, e, o: (e, 0, 0)),
-            ],
+            in_specs=[full(a), part(b)] if cut_last else [part(a), full(b)],
             out_specs=[
                 pl.BlockSpec(
-                    (1, 1, cut, hidden),
+                    (1, 1, *dims),
                     lambda s, e, o: (jnp.minimum(s, 1), jnp.where(s < 2, e, local - 1), 0, 0),
                 ),
                 pl.BlockSpec(
-                    (1, 1, cut, hidden),
+                    (1, 1, *dims),
                     lambda s, e, o: (jnp.maximum(s - 2, 0), jnp.where(s < 2, 0, e), 0, 0),
                 ),
             ],
         ),
         out_shape=[shape, shape],
-        compiler_params=params(40, 2),
-        cost_estimate=cost(10, 20),
+        compiler_params=params(20, 2),
+        cost_estimate=takes(18),
         name="weight_grad",
     )(order, a, b)
 
 
+def norm_two_kernel(at_ref, x_ref, keep_ref, came_ref, far_ref, gain_ref,
+                    middle_ref, first_ref, second_ref):
+    step = pl.program_id(0)
+    branch = keep_ref[...].astype(f32) + came_ref[...].astype(f32) + far_ref[...].astype(f32)
+    middle = x_ref[...].astype(f32) + branch
+    middle_ref[...] = middle
+    inv = lax.rsqrt(jnp.mean(middle * middle, axis=-1, keepdims=True) + EPS)
+    normed = (middle * inv * gain_ref[...].astype(f32)).astype(bf16)
+
+    @pl.when(step < pl.num_programs(0) // 2)
+    def _():
+        first_ref[...] = normed
+
+    @pl.when(step >= pl.num_programs(0) // 2)
+    def _():
+        second_ref[...] = normed
+
+
+def norm_two_call(t_rank, x, keep, came, far, gain):
+    quarter, width = keep.shape
+    rb = quarter // 4
+    row = pl.BlockSpec((rb, width), lambda s, t: (s, 0))
+    return pl.pallas_call(
+        norm_two_kernel,
+        grid_spec=pltpu.PrefetchScalarGridSpec(
+            num_scalar_prefetch=1,
+            grid=(4,),
+            in_specs=[
+                pl.BlockSpec((rb, width), lambda s, t: (4 * t[0] + s, 0)), row, row, row,
+                pl.BlockSpec((1, width), lambda s, t: (0, 0)),
+            ],
+            out_specs=[
+                row,
+                pl.BlockSpec((rb, width), lambda s, t: (jnp.minimum(s, 1), 0)),
+                pl.BlockSpec((rb, width), lambda s, t: (jnp.maximum(s - 2, 0), 0)),
+            ],
+        ),
+        out_shape=[
+            jax.ShapeDtypeStruct((quarter, width), f32),
+            jax.ShapeDtypeStruct((quarter // 2, width), bf16),
+            jax.ShapeDtypeStruct((quarter // 2, width), bf16),
+        ],
+        compiler_params=params(12),
+        cost_estimate=takes(3),
+        name="norm_two",
+    )(t_rank, x, keep, came, far, gain)
+
+
+def middle_back_kernel(*refs):
+    terms, tails, refs = refs[:6], refs[6:9], refs[9:]
+    (mix_ref, router_ref, middle_ref, cot_ref, gain_ref,
+     dmid_ref, db_ref, dlog_ref, gain2_ref, dl_ref) = refs
+    step = pl.program_id(0)
+    rb, width = middle_ref.shape
+    experts, quarter = mix_ref.shape
+
+    @pl.when(step == 0)
+    def _():
+        tail = sum(t[...].astype(f32) for t in tails)
+        extra = tail.shape[0] // 2
+        tail = tail[:extra] + tail[extra:]
+        d_mix = jnp.concatenate(
+            [tail[:, j * quarter:(j + 1) * quarter] for j in range(-(-experts // extra))], axis=0
+        )[:experts]
+        mix = mix_ref[...]
+        d_logits = mix * (d_mix - jnp.sum(mix * d_mix, axis=0, keepdims=True))
+        d_logits = jnp.transpose(d_logits).astype(bf16)
+        dlog_ref[...] = d_logits
+        dl_ref[...] = d_logits
+        gain2_ref[...] = jnp.zeros_like(gain2_ref)
+
+    first = [t[...].astype(f32) for t in terms[:3]]
+    second = [t[...].astype(f32) for t in terms[3:]]
+    routed = jnp.where(step < pl.num_programs(0) // 2, sum(first), sum(second))
+    d_logits = dl_ref[pl.ds(pl.multiple_of(step * rb, rb), rb), :]
+    d_normed = routed + mm(d_logits, router_ref[...])
+    middle = middle_ref[...]
+    inv = lax.rsqrt(jnp.mean(middle * middle, axis=-1, keepdims=True) + EPS)
+    gain2_ref[...] += jnp.sum(d_normed * middle * inv, axis=0, keepdims=True)
+    scaled = d_normed * gain_ref[...].astype(f32)
+    d_middle = (
+        cot_ref[...].astype(f32)
+        + inv * scaled
+        - middle * (inv * inv * inv * jnp.mean(scaled * middle, axis=-1, keepdims=True))
+    )
+    dmid_ref[...] = d_middle
+    db_ref[...] = d_middle.astype(bf16)
+
+
+def middle_back_call(terms, mix_t, router_t, middle, cotangent, gain):
+    quarter, width = middle.shape
+    experts = mix_t.shape[0]
+    half = quarter // 2
+    tail = terms[0][1].shape[0] - half
+    rb = half // 4
+    row = pl.BlockSpec((rb, width), lambda s: (s, 0))
+    low = pl.BlockSpec((rb, width), lambda s: (jnp.minimum(s, 3), 0))
+    high = pl.BlockSpec((rb, width), lambda s: (jnp.maximum(s - 4, 0), 0))
+    end = pl.BlockSpec((tail, width), lambda s: (half // tail, 0))
+    whole = lambda shape: pl.BlockSpec(shape, lambda s: (0,) * len(shape))
+    firsts, seconds = [t[0] for t in terms], [t[1] for t in terms]
+    return pl.pallas_call(
+        middle_back_kernel,
+        grid=(8,),
+        in_specs=[low] * 3 + [high] * 3 + [end] * 3
+        + [whole((experts, quarter)), whole((experts, width)), row, row, whole((1, width))],
+        out_specs=[row, row, whole((quarter, experts)), whole((1, width))],
+        out_shape=[
+            jax.ShapeDtypeStruct((quarter, width), f32),
+            jax.ShapeDtypeStruct((quarter, width), bf16),
+            jax.ShapeDtypeStruct((quarter, experts), bf16),
+            jax.ShapeDtypeStruct((1, width), f32),
+        ],
+        scratch_shapes=[pltpu.VMEM((quarter, experts), bf16)],
+        compiler_params=params(16),
+        cost_estimate=takes(7),
+        name="middle_back",
+    )(*firsts, *seconds, *seconds, mix_t, router_t, middle, cotangent, gain)
+
+
+def in_first_half():
+    return pl.program_id(0) < pl.num_programs(0) // 2
+
+
+def two_sums_kernel(first, wait_ref, a_ref, b_ref, p0_ref, p1_ref, m0_ref, m1_ref, pa_ref, mb_ref):
+    plus = jnp.where(in_first_half(), p0_ref[...], p1_ref[...]).astype(f32)
+    minus = jnp.where(in_first_half(), m0_ref[...], m1_ref[...]).astype(f32)
+    a, b = a_ref[...].astype(f32), b_ref[...].astype(f32)
+    if first:
+        a, b = jnp.where(in_first_half(), a, 0.0), jnp.where(in_first_half(), 0.0, b)
+    pa_ref[...] = (a + plus).astype(bf16)
+    mb_ref[...] = (b + minus).astype(bf16)
+
+
+def half_specs(rb, width):
+    return (
+        pl.BlockSpec((rb, width), lambda s, *_: (s, 0)),
+        pl.BlockSpec((rb, width), lambda s, *_: (jnp.minimum(s, 3), 0)),
+        pl.BlockSpec((rb, width), lambda s, *_: (jnp.maximum(s - 4, 0), 0)),
+    )
+
+
+def two_sums_call(wait, a, b, plus, minus, first):
+    rows, width = 2 * plus[0].shape[0], plus[0].shape[1]
+    row, low, high = half_specs(rows // 8, width)
+    return pl.pallas_call(
+        functools.partial(two_sums_kernel, first),
+        grid_spec=pltpu.PrefetchScalarGridSpec(
+            num_scalar_prefetch=1,
+            grid=(8,),
+            in_specs=[low if first else row, high if first else row, low, high, low, high],
+            out_specs=[row, row],
+        ),
+        out_shape=[jax.ShapeDtypeStruct((rows, width), bf16)] * 2,
+        compiler_params=params(10),
+        cost_estimate=takes(4),
+        name="two_sums",
+    )(wait.astype(i32)[None], a, b, *plus, *minus)
+
+
+def layer_out_kernel(middle_ref, first_ref, second_ref, a_ref, b_ref, out_ref):
+    own = jnp.where(in_first_half(), first_ref[...], second_ref[...]).astype(f32)
+    out_ref[...] = (
+        middle_ref[...] + own + a_ref[...].astype(f32) + b_ref[...].astype(f32)
+    ).astype(bf16)
+
+
+def layer_out_call(middle, own, a, b):
+    quarter, width = middle.shape
+    row, low, high = half_specs(quarter // 8, width)
+    return pl.pallas_call(
+        layer_out_kernel,
+        grid=(8,),
+        in_specs=[row, low, high, row, row],
+        out_specs=row,
+        out_shape=jax.ShapeDtypeStruct((quarter, width), bf16),
+        compiler_params=params(10),
+        cost_estimate=takes(4),
+        name="layer_out",
+    )(middle, *own, a, b)
+
+
+def input_back_kernel(at_ref, keep_ref, came_ref, far_ref, dmid_ref, x_ref, gain_ref, out_ref):
+    d_normed = keep_ref[...].astype(f32) + came_ref[...].astype(f32) + far_ref[...].astype(f32)
+    x = x_ref[...].astype(f32)
+    inv = lax.rsqrt(jnp.mean(x * x, axis=-1, keepdims=True) + EPS)
+    scaled = d_normed * gain_ref[...].astype(f32)
+    out_ref[...] = (
+        dmid_ref[...]
+        + inv * scaled
+        - x * (inv * inv * inv * jnp.mean(scaled * x, axis=-1, keepdims=True))
+    )
+
+
+def input_back_call(t_rank, keep, came, far, d_middle, x, gain):
+    quarter, width = d_middle.shape
+    rb = quarter // 8
+    row = pl.BlockSpec((rb, width), lambda s, t: (s, 0))
+    behind = pl.BlockSpec((rb, width), lambda s, t: (8 + s, 0))
+    return pl.pallas_call(
+        input_back_kernel,
+        grid_spec=pltpu.PrefetchScalarGridSpec(
+            num_scalar_prefetch=1,
+            grid=(8,),
+            in_specs=[
+                behind, behind, row, row,
+                pl.BlockSpec((rb, width), lambda s, t: (8 * t[0] + s, 0)),
+                pl.BlockSpec((1, width), lambda s, t: (0, 0)),
+            ],
+            out_specs=row,
+        ),
+        out_shape=jax.ShapeDtypeStruct((quarter, width), f32),
+        compiler_params=params(10),
+        cost_estimate=takes(6),
+        name="input_back",
+    )(t_rank, keep, came, far, d_middle, x, gain)
+
+
 def ring_of(n):
     return list(range(0, n, 2)) + list(range(n - 1, 0, -2))
+
+
+def index_at(place, n):
+    return jnp.where(place < n // 2, 2 * place, 2 * n - 1 - 2 * place)
 
 
 def ring_moves(n):
@@ -622,51 +900,44 @@
     return ahead, [(b, a) for a, b in ahead]
 
 
-def add_low(a, b):
-    return (a.astype(f32) + b.astype(f32)).astype(bf16)
-
-
-def ring_gather(own, n, split):
-    ahead, behind = ring_moves(n)
-    if split:
-        cut = own.shape[0] // 2
-        own = (own[:cut], own[cut:])
-    else:
-        cut = own.shape[0] // 32 * 16
-        own = (own,)
-    a = b = own
-    got = []
-    for _ in range(n // 2 - 1):
-        a = tuple(lax.ppermute(v, "dp", ahead) for v in a)
-        b = tuple(lax.ppermute(v, "dp", behind) for v in b)
-        got.append([a, b] if split else [a[0], b[0]])
-    if split:
-        got.append([(lax.ppermute(a[0], "dp", ahead), lax.ppermute(b[1], "dp", behind))])
-    else:
-        a, b = lax.ppermute(a[0][:cut], "dp", ahead), lax.ppermute(b[0][cut:], "dp", behind)
-        got.append([jnp.concatenate([a, b], axis=0)])
-    return own, got
-
-
-def ring_scatter(own, parts, n, between=()):
-    ahead, behind = ring_moves(n)
-    far = parts[-1][0]
-    a, b = [far[0], None], [None, far[1]]
-    came, done = [], []
-    for step in range(n // 2):
-        if step > 0:
-            minus, plus = parts[n // 2 - step - 1]
-            sums = [add_low(v, t) for v, t in zip(a + b, plus + minus) if v is not None]
-            if step <= len(between):
-                done.append(between[step - 1](came[step - 2] if step > 1 else None))
-                sums = after(done[-1], sums)
-            sums = iter(sums)
-            a = [t if v is None else next(sums) for v, t in zip(a, plus)]
-            b = [t if v is None else next(sums) for v, t in zip(b, minus)]
-        a = [None if v is None else lax.ppermute(v, "dp", ahead) for v in a]
-        b = [None if v is None else lax.ppermute(v, "dp", behind) for v in b]
-        came.append([v for v in a + b if v is not None])
-    return [o.astype(f32) + x.astype(f32) + y.astype(f32) for o, x, y in zip(own, a, b)], done
+def add_low(a, b, wait=0.0):
+    return (a.astype(f32) + jnp.asarray(b).astype(f32) + wait).astype(bf16)
+
+
+class RingSum:
+
+    def __init__(self, own, parts, n):
+        self.own, self.parts, self.half = own, parts, n // 2
+        self.ways = ring_moves(n)
+        self.long, self.short = [None, None], [None, None]
+        self.rounds = 0
+
+    def term(self, distance, way, half):
+        if distance == self.half:
+            return self.parts[-1][0][half]
+        return self.parts[distance - 1][1 - way][half]
+
+    def round(self, wait=0.0):
+        r = self.rounds
+        self.rounds += 1
+        sums = []
+        for held, hop, distance, turn in (
+            (self.short, r, self.half - 1 - r, 1),
+            (self.long, r - 1, self.half + 1 - r, 0),
+        ):
+            if hop < 0 or distance < 1:
+                continue
+            for way in range(2):
+                t = self.term(distance, way, (way + turn) % 2)
+                if hop > 0:
+                    t = add_low(held[way], t, wait)
+                    sums.append(t)
+                held[way] = lax.ppermute(t, "dp", self.ways[way])
+        return sums
+
+    def terms(self):
+        a, b = self.long, self.short
+        return [tuple(self.own), (a[0], b[0]), (b[1], a[1])]
 
 
 CORE = [(0, 1), (1, 0), (2, 3), (3, 2)]
@@ -679,6 +950,18 @@
 
 def to_chip(a):
     return lax.ppermute(a, "tensor", CHIP)
+
+
+def zero_of(a):
+    while a.ndim > 2:
+        a = a[0]
+    return jnp.minimum(jnp.abs(a[0, 0].astype(f32)), 0.0)
+
+
+def mark(a):
+    while a.ndim > 2:
+        a = a[0]
+    return zero_of(a)
 
 
 def after(first, then):
@@ -696,7 +979,7 @@
     t_rank = lax.axis_index("tensor")
     d_rank = lax.axis_index("dp")
     place = jnp.where(d_rank % 2 == 0, d_rank // 2, n_dp - 1 - d_rank // 2)
-    ringed = n_dp <= 8
+    ringed = n_dp in (4, 6, 8)
     cos, sin = rope_tables()
 
     hot_t = jnp.any(
@@ -714,201 +997,228 @@
     payload = jnp.concatenate([cotangent, rank_rows], axis=0)
     router_t = router.T
     ahead, behind = ring_moves(n_dp)
-
-    normed1, q, k, v, kt = qkv_call(
-        layer_input, norm1_gain[None, :], w_query, w_key, w_value, cos, sin
-    )
-    if ringed:
-        _, grads_from = ring_gather(payload, n_dp, False)
-        stage = [after(g, jnp.zeros((), i32)) for g in grads_from]
-    else:
-        stage = [jnp.zeros((), i32)] * 2
-    seg_col, seg_row = segments[:, None], segments[None, :]
-    pair = lambda t: jnp.stack([2 * t, 2 * t + 1])
+    zero = jnp.zeros((), i32)
+    own_at = t_rank.astype(i32)[None]
     mate, other, cross = t_rank ^ 1, t_rank ^ 2, t_rank ^ 3
     quarters = jnp.stack([cross, mate, other, t_rank]).astype(i32)
-    first = jnp.concatenate([pair(cross), pair(other)]).astype(i32)
-    second = jnp.concatenate([pair(mate), pair(t_rank)]).astype(i32)
-    heads, lse, send_a, keep_a = attend_call(first, q, k, v, seg_col, seg_row, w_output)
-    far = to_chip(add_low(keep_a, to_core(send_a)))
+    pairs_of = lambda *ts: jnp.stack([2 * t + j for t in ts for j in range(2)]).astype(i32)
+
+    if ringed:
+        a = b = payload
+        grads_from = []
+        for _ in range(n_dp // 2 - 1):
+            a, b = lax.ppermute(a, "dp", ahead), lax.ppermute(b, "dp", behind)
+            grads_from.append((a, b))
+        stage = [after(g, zero) for g in grads_from]
+    else:
+        stage = [zero] * 3
+    normed1, q, k, v, kt = qkv_call(
+        layer_input, after(payload, norm1_gain[None, :]), w_query, w_key, w_value, cos, sin
+    )
+    seg_col, seg_row = segments[:, None], segments[None, :]
+    heads, lse, send_a, keep_a = attend_call(
+        pairs_of(cross, other), q, k, v, seg_col, seg_row, w_output
+    )
+    if ringed:
+        send_a, grads_from[0] = lax.optimization_barrier((send_a, grads_from[0]))
+    sum_a = add_low(keep_a, to_core(send_a))
+    far = to_chip(sum_a)
     heads, lse, send_b, keep_b = attend_call(
-        second + stage[0], q, k, v, seg_col, seg_row, w_output, held=(heads, lse)
-    )
-    far = far + stage[1].astype(bf16)
-    branch = keep_b.astype(f32) + to_core(send_b).astype(f32) + far.astype(f32)
-
-    row_start = t_rank * quarter
-    own_input = lax.dynamic_slice_in_dim(layer_input, row_start, quarter).astype(f32)
-    middle = own_input + branch
-    inv_rms2 = lax.rsqrt(jnp.mean(middle * middle, axis=-1, keepdims=True) + EPS)
-    gain_two = norm2_gain.astype(f32)
-    normed2 = (middle * inv_rms2 * gain_two).astype(bf16)
+        after(sum_a, pairs_of(mate, t_rank)),
+        q, k, v, seg_col, seg_row, w_output, held=(heads, lse),
+    )
+    came_b = jnp.concatenate([to_core(send_b[:QB]), to_core(send_b[QB:])], axis=0)
+    middle, *normed2 = norm_two_call(
+        own_at + stage[1], layer_input, keep_b, came_b, far, norm2_gain[None, :]
+    )
 
     base = (d_rank * local).astype(i32)[None]
-    run = lambda xs, cs, at, of, held: expert_call(
+    run = lambda base, xs, cs, at, of, held: expert_call(
         base, xs, cs, router_t, w_gate, w_up, w_down, cap, at, of, held
     )
+
+    def own_mixing(rows):
+        logits = jnp.concatenate([mm(router_t, r, NT) for r in rows], axis=1)
+        return jax.nn.softmax(jnp.where(hot_t, logits, -jnp.inf), axis=0)
+
+    def core_sum(parts, wait):
+        send, keep = parts
+        came = to_core(send)
+        away = add_low(keep[0], came[0], wait)
+        return keep[1], came[1], away
+
+    def chip_sum(sums, wait):
+        keep, came, away = sums
+        return keep.astype(f32) + came.astype(f32) + to_chip(away).astype(f32) + wait
+
     if ringed:
-        own, rows_from = ring_gather(normed2, n_dp, True)
-        (out_own,), (back_own,), dmix_own, held = run([own], [payload], n_dp - 1, n_dp, None)
-        outs, backs, dmix_minus, dmix_plus = [], [], [], []
-        for j, (xs, cs) in enumerate(zip(rows_from, grads_from)):
-            at = j if len(xs) == 2 else n_dp - 2
-            o, b, m, held = run(xs, cs, at, n_dp, held)
+        own = tuple(normed2)
+        step = lambda rows, way: tuple(lax.ppermute(r, "dp", way) for r in rows)
+        xs = [step(own, ahead), step(own, behind)]
+        (out_own,), (back_own,), held = run(base, [own], [payload], n_dp - 1, n_dp, None)
+        outs, backs, last = [], [], out_own
+        cut = payload.shape[0] // 32 * 16
+        for j in range(n_dp // 2):
+            cs = grads_from[j]
+            if j < n_dp // 2 - 1:
+                at = j
+                a, b = after(last, xs)
+                if j < n_dp // 2 - 2:
+                    later = [step(a, ahead), step(b, behind)]
+                else:
+                    later = [step(a[:1], ahead) + step(b[1:], behind)]
+            else:
+                at = n_dp - 2
+            wait = after(grads_from[-1], zero) if j == n_dp // 2 - 2 else zero
+            if j == max(n_dp // 2 - 3, 0):
+                a, b = after(last, grads_from[-1])
+                a, b = lax.ppermute(a[:cut], "dp", ahead), lax.ppermute(b[cut:], "dp", behind)
+                grads_from.append((jnp.concatenate([a, b], axis=0),))
+            o, b, held = run(base + wait, xs, cs, at, n_dp, held)
             outs.append(o)
             backs.append(b)
-            dmix_minus.append(m[0])
-            dmix_plus.append(m[-1])
-        by_step = jnp.stack([dmix_own[0]] + dmix_plus + dmix_minus[-2::-1])
-        where = jnp.asarray(
-            [d // 2 if d % 2 == 0 else n_dp - 1 - d // 2 for d in range(n_dp)], i32
+            last, xs = o, later
+        back = RingSum(back_own, backs, n_dp)
+        back.round()
+        sums = back.round(mark(backs[-1][0][0]))
+        mix_t = own_mixing(after(sums, own))
+        grad_of = lambda i, j: weight_grad_call(
+            quarters + after(sums, zero), held[i], held[j]
         )
-        dmix_part = jnp.take(by_step, (where - place) % n_dp, axis=0)
-        grad_of = lambda i, j: lambda came: weight_grad_call(
-            quarters if came is None else quarters + after(came, jnp.zeros((), i32)),
-            held[i], held[j],
+        gate_parts = grad_of(0, 3)
+        sums = back.round(mark(gate_parts[1]))
+        up_parts = grad_of(0, 4)
+        end = mark(up_parts[1])
+        sums = back.round(end)
+        gate_sum = core_sum(gate_parts, end)
+        down_parts = weight_grad_call(
+            quarters + after(sums, zero) + zero_of(gate_sum[2]).astype(i32), held[2], held[1], True
         )
-        routed, expert_parts = ring_scatter(
-            back_own, backs, n_dp, (grad_of(0, 3), grad_of(0, 4), grad_of(1, 2))
-        )
-        routed = jnp.concatenate(routed, axis=0)
+        end = mark(down_parts[1])
+        sums = back.round(end)
+        gate_grad = chip_sum(gate_sum, end)
+        gate_done = zero_of(gate_grad)
+        routed = back.terms()
     else:
         grads_all = lax.all_gather(payload, "dp", axis=0)
-        rows_all = lax.all_gather(normed2, "dp", axis=0)
+        rows_all = lax.all_gather(jnp.concatenate(normed2, axis=0), "dp", axis=0)
         halves = lambda a: (a[:quarter // 2], a[quarter // 2:])
 
         def two(sums, pair_rows):
             x, c = pair_rows
-            o, b, m, held = run([halves(x[0]), halves(x[1])], [c[0], c[1]], 0, 2, None)
+            o, b, held = run(base, [halves(x[0]), halves(x[1])], [c[0], c[1]], 0, 2, None)
             grads = [
-                list(weight_grad_call(quarters, held[i], held[j])) for i, j in ((0, 3), (0, 4), (1, 2))
+                list(weight_grad_call(quarters, held[i], held[j], i == 2))
+                for i, j in ((0, 3), (0, 4), (2, 1))
             ]
             sums = jax.tree.map(lambda t, g: t + g.astype(f32), sums, grads)
             join = lambda a: jnp.stack([jnp.concatenate(h, axis=0) for h in a])
-            return sums, (join(o), join(b), m)
+            return sums, (join(o), join(b))
 
         pairs = lambda a: a.reshape((n_dp // 2, 2) + a.shape[1:])
-        zero = jnp.zeros((2, local, width // 4, hidden), f32)
-        expert_parts, (outs, backs, dmix_part) = lax.scan(
-            two, [[zero, zero]] * 3, (pairs(rows_all), pairs(grads_all))
+        none = jnp.zeros((2, local, width // 4, hidden), f32)
+        none = [[none] * 2, [none] * 2, [none.transpose(0, 1, 3, 2)] * 2]
+        grads, (outs, backs) = lax.scan(
+            two, none, (pairs(rows_all), pairs(grads_all))
         )
-        expert_parts = jax.tree.map(lambda a: a.astype(bf16), expert_parts)
-        dmix_part = dmix_part.reshape(n_dp, local, quarter)
+        gate_parts, up_parts, down_parts = jax.tree.map(lambda a: a.astype(bf16), grads)
+        gate_grad = chip_sum(core_sum(gate_parts, 0.0), 0.0)
+        gate_done = 0.0
         scatter = lambda a: lax.psum_scatter(
-            a.reshape(n_dp * quarter, width), "dp", scatter_dimension=0, tiled=True
-        ).astype(f32)
-        routed = scatter(backs)
-    d_mix = lax.all_to_all(dmix_part, "dp", split_axis=0, concat_axis=0, tiled=True)
-    d_mix = d_mix.reshape(experts, quarter)
-
-    logits_t = mm(router_t, normed2, NT)
-    logits_t = jnp.where(hot_t, logits_t, -jnp.inf)
-    mix_t = jax.nn.softmax(logits_t, axis=0)
-    d_logits_t = mix_t * (d_mix - jnp.sum(mix_t * d_mix, axis=0, keepdims=True))
-    d_logits = jnp.where(hot_t, d_logits_t, 0.0).astype(bf16).T
-    router_part = mm(normed2, d_logits, TN)
-
-    out_grad = cotangent.astype(f32)
-    d_normed2 = routed + mm(d_logits, router, NT)
-    scaled_two = d_normed2 * gain_two
-    d_middle = (
-        out_grad
-        + inv_rms2 * scaled_two
-        - middle * inv_rms2**3 * jnp.mean(scaled_two * middle, axis=-1, keepdims=True)
-    )
-
-    db_own = d_middle.astype(bf16)
+            a.reshape(-1, width), "dp", scatter_dimension=0, tiled=True
+        )
+        mix_t = own_mixing(normed2)
+        empty = jax.tree.map(jnp.zeros_like, halves(scatter(backs)))
+        routed = [halves(scatter(backs)), empty, empty]
+
+    d_middle, db_own, d_logits, second_gain_part = middle_back_call(
+        routed, mix_t, router_t, middle, cotangent,
+        (norm2_gain.astype(f32) + gate_done).astype(bf16)[None, :],
+    )
+
     db_mate = to_core(db_own)
-    db_other = to_chip(db_own)
+    other_first, other_second = to_chip(db_own[:QB]), to_chip(db_own[QB:])
+    common = (q, k, v, kt, seg_row, seg_col, heads, lse)
+    if ringed:
+        out_a, out_b = after(sums, outs[-1][0])
+        out_a, out_b = lax.ppermute(out_a, "dp", ahead), lax.ppermute(out_b, "dp", behind)
+
+        def out_step(a, b, j, wait):
+            minus, plus = outs[j - 1]
+            a, b = two_sums_call(wait, a, b, plus, minus, j == n_dp // 2 - 1)
+            return lax.ppermute(a, "dp", ahead), lax.ppermute(b, "dp", behind), (a, b)
+
+        steps = list(range(n_dp // 2 - 1, 0, -1))
+    else:
+        out_own = halves(scatter(outs))
+        out_a = out_b = jnp.zeros((quarter, width), bf16)
+        out_step = lambda a, b, j, wait: (a, b, zero)
+        steps = [0, 0, 0]
+    out_a, out_b, sums = out_step(out_a, out_b, steps[0], zero_of(db_own))
+    dq, dk, dv = attend_back_call(
+        pairs_of(t_rank, mate) + after(sums, zero) + zero_of(other_first).astype(i32), *common, db_own, db_mate, w_output, cos, sin
+    )
+    end = mark(dq)
+    db_other = add_low(jnp.concatenate([other_first, other_second], axis=0), end)
+    up_sum = core_sum(up_parts, end)
+    out_a, out_b, sums = out_step(out_a, out_b, steps[1], end)
     db_cross = to_core(db_other)
-    near = jnp.concatenate([pair(t_rank), pair(mate)]).astype(i32)
-    distant = jnp.concatenate([pair(other), pair(cross)]).astype(i32)
-    common = (q, k, v, kt, seg_row, seg_col, heads, lse)
-    dq, dk, dv = attend_back_call(near, *common, db_own, db_mate, w_output, cos, sin)
-    rows_of = lambda t: lax.dynamic_slice_in_dim(heads, t * quarter, quarter)
-    wo_near = mm(db_own, rows_of(t_rank), TN) + mm(db_mate, rows_of(mate), TN)
     dq, dkv = attend_back_call(
-        distant, *common, db_other, db_cross, w_output, cos, sin, held=(dq, dk, dv)
-    )
-    send, keep, first_gain_part = qkv_back_call(
-        jnp.concatenate([pair(t) for t in (cross, mate, other, t_rank)]).astype(i32),
-        dq, dkv, layer_input, w_query, w_key, w_value,
+        pairs_of(other, cross) + after(sums, zero)
+        + zero_of(up_sum[2]).astype(i32),
+        *common, db_other, db_cross, w_output,
+        cos, sin, held=(dq, dk, dv),
+    )
+    sums = zero
+    for j in steps[2:]:
+        out_a, out_b, sums = out_step(out_a, out_b, j, zero_of(dkv))
+    up_grad = chip_sum(up_sum, zero_of(dkv))
+    packed_dense = dense_grad_call(
+        jnp.stack([t_rank, mate, other, cross]).astype(i32) + after(sums, zero)
+        + zero_of(up_grad).astype(i32),
+        normed1, dq, dkv, (db_own, db_mate, db_other, db_cross), heads, normed2, d_logits,
+        second_gain_part, norm1_gain[None, :], (w_query, w_key, w_value),
+    )
+    down_sum = core_sum(down_parts, zero_of(packed_dense))
+    send, keep = qkv_back_call(
+        pairs_of(cross, mate, other, t_rank) + after(packed_dense, zero),
+        dq, dkv, w_query, w_key, w_value,
     )
     came = to_core(send)
-    far = to_chip(add_low(keep[:quarter], came[:quarter]))
-    d_normed1 = keep[quarter:].astype(f32) + came[quarter:].astype(f32) + far.astype(f32)
-
-    second_gain_part = jnp.sum(d_normed2 * middle * inv_rms2, axis=0)
-
-    def over_all(part):
-        rows = part.reshape(n_dp * 4, -1)
-        rows = lax.all_to_all(rows, ("dp", "tensor"), split_axis=0, concat_axis=0, tiled=True)
-        return jnp.sum(rows, axis=0)
-
-    router_gain = jnp.concatenate([router_part, second_gain_part[:, None]], axis=1)
-    router_gain = over_all(router_gain).reshape(-1, experts + 1)
-    first_gain = over_all(first_gain_part)
-
-    if ringed:
-        summed, _ = ring_scatter(out_own, [list(after(db_own, o)) for o in outs], n_dp)
-        summed = jnp.concatenate(summed, axis=0)
-    else:
-        summed = scatter(outs)
-    layer_out = (middle + summed).astype(bf16)
-
-    def shared(parts):
-        send, keep = parts
-        came = to_core(send)
-        far = to_chip(add_low(keep[0], came[0]))
-        return keep[1].astype(f32) + came[1].astype(f32) + far.astype(f32)
-
-    gate_grad, up_grad, down_grad = [shared(p) for p in expert_parts]
-    down_grad = jnp.transpose(down_grad, (0, 2, 1))
-
-    query_part = mm(normed1, dq, TN).astype(bf16)
-    kv_part = mm(normed1, dkv, TN).astype(bf16)
-    wo_part = wo_near + mm(db_other, rows_of(other), TN) + mm(db_cross, rows_of(cross), TN)
-    packed_dense = jnp.concatenate([query_part, kv_part, wo_part.astype(bf16)], axis=1)
-    if ringed:
-        blocks = packed_dense.reshape(n_dp, width // n_dp, packed_dense.shape[1])
-        ring = jnp.asarray(ring_of(n_dp), i32)
-
-        def block(far):
-            rows = lax.dynamic_index_in_dim(
-                blocks, ring[(place + far) % n_dp], axis=0, keepdims=False
-            )
-            return rows[:rows.shape[0] // 2], rows[rows.shape[0] // 2:]
-
-        parts = [[block(-j), block(j)] for j in range(1, n_dp // 2)] + [[block(n_dp // 2)]]
-        dense_sum, _ = ring_scatter(block(0), parts, n_dp)
-        dense_sum = jnp.concatenate(dense_sum, axis=0)
-    else:
-        dense_sum = lax.psum_scatter(
-            packed_dense, "dp", scatter_dimension=0, tiled=True
-        ).astype(f32)
+    sum_in = add_low(keep[:quarter], came[:quarter])
+    far = to_chip(sum_in)
+    down_grad = chip_sum(down_sum, zero_of(sum_in))
+
+    input_grad = input_back_call(
+        own_at, keep, came, far, d_middle, layer_input, norm1_gain[None, :]
+    )
+
+    dense_sum = lax.psum_scatter(
+        packed_dense, "dp", scatter_dimension=0, tiled=True
+    ).astype(f32)
     q_cols, kv_cols = w_query.shape[1], w_key.shape[1]
     query_grad = dense_sum[:, :q_cols]
     key_grad = dense_sum[:, q_cols:q_cols + kv_cols]
     value_grad = dense_sum[:, q_cols + kv_cols:q_cols + 2 * kv_cols]
-    output_grad = jnp.transpose(dense_sum[:, q_cols + 2 * kv_cols:])
-
-    own_rms = lax.rsqrt(jnp.mean(own_input * own_input, axis=-1, keepdims=True) + EPS)
-    scaled_one = d_normed1 * norm1_gain.astype(f32)
-    input_grad = (
-        d_middle
-        + own_rms * scaled_one
-        - own_input * own_rms**3 * jnp.mean(scaled_one * own_input, axis=-1, keepdims=True)
-    )
+    cols = 2 * (q_cols + kv_cols)
+    output_grad = jnp.transpose(dense_sum[:, q_cols + 2 * kv_cols:cols])
+    rows = width // n_dp
+    small = dense_sum[:, cols:cols + experts + 2] + zero_of(input_grad)
+    small = small + to_core(small)
+    small = small + to_chip(small)
+    small = lax.dynamic_slice_in_dim(small, t_rank * (rows // 4), rows // 4)
+
+    layer_out = layer_out_call(middle, out_own, out_a, out_b)
     return (
         layer_out,
         input_grad,
-        first_gain,
+        small[:, experts + 1],
         query_grad,
         key_grad,
         value_grad,
         output_grad,
-        router_gain[:, experts],
-        router_gain[:, :experts],
+        small[:, experts],
+        small[:, :experts],
         gate_grad,
         up_grad,
         down_grad,

time: 804 us -> 745 us (0.927)
  other arithmetic: 97.2 us -> 35.9 us
  Pallas kernels: 318 us -> 364 us
  starting transfers between devices: 95.8 us -> 56.4 us
  local copies, waits for them, and re-layouts: 36.3 us -> 72.4 us
  matrix products: 29.2 us -> 0.79 us
  waiting for transfers between devices: 204 us -> 184 us
  between operations: 17.4 us -> 26.6 us
    pallas_call x0 -> x8, Pallas kernels: none -> 51.5 us  [the longest x3 19.8 us: two_sums_call(): pl.pallas_call(functools.partial(two_sums_kernel, first), grid_spec=pltpu...]
    unnamed x201 -> x256, local copies, waits for them, and re-layouts: 19.9 us -> 51.4 us
    convert_element_type x34 -> x18, other arithmetic: 53.4 us -> 22.8 us  [the longest x16 21.7 us: add_low(): return (a.astype(f32) + jnp.asarray(b).astype(f32) + wait).astype(bf16)]
    dot_general x9 -> x2, matrix products: 29 us -> 0.61 us  [mm(): return lax.dot_general(a, b, dims, preferred_element_type=f32)]
    ppermute x64 -> x44, starting transfers between devices: 67.5 us -> 46.1 us  [the longest x14 14.5 us: round(): held[way] = lax.ppermute(t, 'dp', self.ways[way])]
    all_to_all x3 -> x0, waiting for transfers between devices: 14.6 us -> none  [the longest x1 14.6 us: per_device(): lax.all_to_all(dmix_part, 'dp', split_axis=0, concat_axis=0, tiled=True)]
    slice x5 -> x22, local copies, waits for them, and re-layouts: 4.54 us -> 17 us  [the longest x15 10.6 us: zero_of(): return jnp.minimum(jnp.abs(a[0, 0].astype(f32)), 0.0)]
    all_to_all x3 -> x0, starting transfers between devices: 10.2 us -> none  [the longest x2 6.76 us: over_all(): lax.all_to_all(rows, ('dp', 'tensor'), split_axis=0, concat_axis=0, tiled...]
  transfers between devices with their start and end apart: 81 -> 63, of which waited for: 30 -> 22; matrix products, arithmetic and copies ran while one was open for 16% -> 7% of each run, Pallas kernels for 35% -> 49%
where the time goes in v2:
time: 745 us; the launch traced here: 740 us
  Pallas kernels  364 us (49%)
  waiting for transfers between devices  184 us (25%)
  local copies, waits for them, and re-layouts  72.4 us (10%)
  starting transfers between devices  56.4 us (8%)
  other arithmetic  35.9 us (5%)
  between operations  26.6 us (4%)
    pallas_call x5, Pallas kernels, expert_call(): pl.pallas_call(functools.partial(expert_kernel, sources, cap, experts), g...  149 us
    ppermute x14, waiting for transfers between devices, per_device(): step = lambda rows, way: tuple((lax.ppermute(r, 'dp', way) for r in rows))  57.9 us
    pallas_call x2, Pallas kernels, attend_back_call(): pl.pallas_call(functools.partial(attend_back_kernel, last), grid_spec=plt...  55 us
    ppermute x6, waiting for transfers between devices, out_step(): return (lax.ppermute(a, 'dp', ahead), lax.ppermute(b, 'dp', behind), (a, b))  51.8 us
    unnamed x256, local copies, waits for them, and re-layouts  51.4 us
    pallas_call x3, Pallas kernels, weight_grad_call(): pl.pallas_call(weight_grad_kernel, grid_spec=pltpu.PrefetchScalarGridSpec...  47.8 us
    pallas_call x2, Pallas kernels, attend_call(): pl.pallas_call(attend_kernel, grid_spec=pltpu.PrefetchScalarGridSpec(num_...  39.1 us
    ppermute x14, waiting for transfers between devices, round(): held[way] = lax.ppermute(t, 'dp', self.ways[way])  25.6 us
  transfers between devices with their start and end apart: 63, of which 22 were waited for; matrix products, arithmetic and copies ran while one was open for 7% of the time, Pallas kernels for 49%

profile of v2, /device:TPU:0, one launch (start us, length us, event | category | flops | bytes accessed | tf_op | source)
XLA Modules:
  0.0 740.4 jit_solution(16425043946051259388)
XLA Ops:
  8.6 1.8 maximum_maximum_fusion.refs_2_
  10.4 3.1 collective-permute-start
  13.6 13.0 %norm_qkv.1 = (bf16[2048,1536]{1,0:T(8,128)(2,1)}, bf16[6,2048,64]{2,1,0:T(8,128)(2,1)}, bf16[2,2048,64]{2,1,0:T(8,128)(2,1)S(1)}, bf16[2,2048,64]{2,1,0:T(8,128)(2,1)S(1)}, bf16[2,64,2048]{2,1,0:T(8,128)(2,1)S(1)}) custom-call(bf16[2048,1536]{1,0:T(8,128)(2,1)} %x_ref.5, bf16[1,1536]{1,0:T(2,128)(2,1)S(1)} %broadcast_in_dim.48.gain_ref, ...), custom_call_target="tpu_custom_call" | custom-call | flops 114147000320 | bytes 1000000 | tf_op jit(solution)/shard_map/norm_qkv/pallas_call | solution.py:98
  31.4 23.0 %attend.2 = (bf16[2048,384]{1,0:T(8,128)(2,1)}, f32[8,2048]{1,0:T(8,128)}, bf16[512,1536]{1,0:T(8,128)(2,1)}, bf16[512,1536]{1,0:T(8,128)(2,1)}) custom-call(s32[4]{0:T(128)} %pad_add_fusion.1.order_ref, bf16[6,2048,64]{2,1,0:T(8,128)(2,1)} %get-tuple-element.140.q_ref, bf16[2,2048,64]{2,1,0:T(8,128)(2,1)} %copy-done.5, bf16[2,2048,64]{2,1,0:T(8,128)(2,1)} %copy-done.8, ...), custom_call_target="tpu_custom_call" | custom-call | flops 1152999936 | bytes 1000000 | tf_op jit(solution)/shard_map/attend/pallas_call | solution.py:212
  55.1 2.0 collective-permute-start.1
  58.1 3.0 add_convert_fusion.5
  61.1 16.1 %attend.3 = (bf16[2048,384]{1,0:T(8,128)(2,1)}, f32[8,2048]{1,0:T(8,128)}, bf16[512,1536]{1,0:T(8,128)(2,1)}, bf16[512,1536]{1,0:T(8,128)(2,1)}) custom-call(s32[4]{0:T(128)} %pad_add_fusion.order_ref, bf16[6,2048,64]{2,1,0:T(8,128)(2,1)} %get-tuple-element.140.q_ref, bf16[2,2048,64]{2,1,0:T(8,128)(2,1)} %copy-done.5, ...), custom_call_target="tpu_custom_call", output_to_operand_aliasing={{0}: (7, {}), {1}: (8, {})} | custom-call | flops 1152999936 | bytes 1000000 | tf_op jit(solution)/shard_map/attend/pallas_call | solution.py:212
  77.3 2.4 fusion.13
  80.2 13.3 %collective-permute-done.1.refs_4_ = bf16[528,1536]{1,0:T(8,128)(2,1)} collective-permute-done((bf16[528,1536]{1,0:T(8,128)(2,1)}, bf16[528,1536]{1,0:T(8,128)(2,1)}, u32[]{:S(2)}, u32[]{:S(2)}) %collective-permute-start.1) | collective-permute-done | bytes 1622048 | tf_op jit(solution)/shard_map/ppermute | solution.py:1010
  97.8 2.8 copy-done.37
  102.0 1.7 norm_two.1
  103.7 1.7 copy-done.63
  105.4 2.0 collective-permute-start.8
  107.4 2.0 collective-permute-start.9
  109.4 22.8 %experts.5 = (bf16[256,1536]{1,0:T(8,128)(2,1)}, bf16[256,1536]{1,0:T(8,128)(2,1)}, bf16[256,1536]{1,0:T(8,128)(2,1)}, bf16[288,1536]{1,0:T(8,128)(2,1)}, bf16[4...) custom-call(s32[1]{0:T(128)} %bitcast.13.base_ref, ...), custom_call_target="tpu_custom_call" | custom-call | flops 26518999040 | bytes 1000000 | tf_op jit(solution)/shard_map/experts/pallas_call | solution.py:597
  132.2 18.3 %collective-permute-done.8.refs_0_ = bf16[256,1536]{1,0:T(8,128)(2,1)} collective-permute-done((bf16[256,1536]{1,0:T(8,128)(2,1)S(1)}, bf16[256,1536]{1,0:T(8,128)(2,1)}, u32[]{:S(2)}, u32[]{:S(2)}) %collective-permute-start.8) | collective-permute-done | bytes 786464 | tf_op jit(solution)/shard_map/ppermute | solution.py:1056
  150.8 14.9 %collective-permute-done.9.refs_1_ = bf16[256,1536]{1,0:T(8,128)(2,1)} collective-permute-done((bf16[256,1536]{1,0:T(8,128)(2,1)S(1)}, bf16[256,1536]{1,0:T(8,128)(2,1)}, u32[]{:S(2)}, u32[]{:S(2)}) %collective-permute-start.9) | collective-permute-done | bytes 786464 | tf_op jit(solution)/shard_map/ppermute | solution.py:1056
  169.4 34.3 %experts.6 = (bf16[256,1536]{1,0:T(8,128)(2,1)}, bf16[256,1536]{1,0:T(8,128)(2,1)}, bf16[256,1536]{1,0:T(8,128)(2,1)}, bf16[256,1536]{1,0:T(8,128)(2,1)}, bf16[2...) custom-call(s32[1]{0:T(128)} %bitcast.13.base_ref, ...), custom_call_target="tpu_custom_call", output_to_operand_aliasing={{8}: (11, {}), {9}: (12, {}), {10}: (13, {}), {11}: (14, {}... | custom-call | flops 39202000896 | bytes 1000000 | tf_op jit(solution)/shard_map/experts/pallas_call | solution.py:597
  204.2 1.7 slice.181
  208.1 16.4 %collective-permute-done.15.refs_3_ = bf16[256,1536]{1,0:T(8,128)(2,1)} collective-permute-done((bf16[256,1536]{1,0:T(8,128)(2,1)}, bf16[256,1536]{1,0:T(8,128)(2,1)}, u32[]{:S(2)}, u32[]{:S(2)}) %collective-permute-start.15) | collective-permute-done | bytes 786464 | tf_op jit(solution)/shard_map/ppermute | solution.py:1056
  228.6 34.6 %experts.7 = (bf16[256,1536]{1,0:T(8,128)(2,1)}, bf16[256,1536]{1,0:T(8,128)(2,1)}, bf16[256,1536]{1,0:T(8,128)(2,1)}, bf16[256,1536]{1,0:T(8,128)(2,1)}, bf16[2...) custom-call(s32[1]{0:T(128)} %bitcast.13.base_ref, ...), custom_call_target="tpu_custom_call", output_to_operand_aliasing={{8}: (11, {}), {9}: (12, {}), {10}: (13, {}), {11}: (14, {}... | custom-call | flops 39202000896 | bytes 1000000 | tf_op jit(solution)/shard_map/experts/pallas_call | solution.py:597
  264.5 8.2 %collective-permute-done.19.refs_3_ = bf16[256,1536]{1,0:T(8,128)(2,1)} collective-permute-done((bf16[256,1536]{1,0:T(8,128)(2,1)}, bf16[256,1536]{1,0:T(8,128)(2,1)}, u32[]{:S(2)}, u32[]{:S(2)}) %collective-permute-start.19) | collective-permute-done | bytes 786464 | tf_op jit(solution)/shard_map/ppermute | solution.py:1056
  274.8 34.8 %experts.8 = (bf16[256,1536]{1,0:T(8,128)(2,1)}, bf16[256,1536]{1,0:T(8,128)(2,1)}, bf16[256,1536]{1,0:T(8,128)(2,1)}, bf16[256,1536]{1,0:T(8,128)(2,1)}, bf16[2...) custom-call(s32[1]{0:T(128)S(6)} %add.305.base_ref, ...), custom_call_target="tpu_custom_call", output_to_operand_aliasing={{8}: (11, {}), {9}: (12, {}), {10}: (13, {}), {11}: (14, {}... | custom-call | flops 39202000896 | bytes 1000000 | tf_op jit(solution)/shard_map/experts/pallas_call | solution.py:597
  312.8 22.5 %experts.9 = (bf16[256,1536]{1,0:T(8,128)(2,1)}, bf16[256,1536]{1,0:T(8,128)(2,1)}, bf16[256,1536]{1,0:T(8,128)(2,1)}, bf16[288,1536]{1,0:T(8,128)(2,1)}, bf16[4...) custom-call(s32[1]{0:T(128)} %bitcast.13.base_ref, ...), custom_call_target="tpu_custom_call", output_to_operand_aliasing={{4}: (8, {}), {5}: (9, {}), {6}: (10, {}), {7}: (11, {}), {... | custom-call | flops 26518999040 | bytes 1000000 | tf_op jit(solution)/shard_map/experts/pallas_call | solution.py:597
  342.1 5.5 copy-done.68
  347.6 2.5 copy-done.80
  350.1 14.3 %weight_grad.3 = (bf16[2,4,384,512]{3,2,1,0:T(8,128)(2,1)S(1)}, bf16[2,4,384,512]{3,2,1,0:T(8,128)(2,1)S(1)}) custom-call(s32[4]{0:T(128)S(1)} %get-tuple-element.302.order_ref, bf16[4,1280,1536]{2,1,0:T(8,128)(2,1)S(1)} %copy-done.68, bf16[4,1280,512]{2,1,0:T(8,128)(2,1)S(1)} %copy-done.80), custom_call_target="tpu_custom_call" | custom-call | flops 20753999872 | bytes 1000000 | tf_op jit(solution)/shard_map/weight_grad/pallas_call | solution.py:647
  370.9 2.0 collective-permute-done.32
  376.5 15.2 %weight_grad.4 = (bf16[2,4,384,512]{3,2,1,0:T(8,128)(2,1)}, bf16[2,4,384,512]{3,2,1,0:T(8,128)(2,1)S(1)}) custom-call(s32[4]{0:T(128)S(1)} %broadcast_add_fusion.1.order_ref, bf16[4,1280,1536]{2,1,0:T(8,128)(2,1)S(1)} %copy-done.68, bf16[4,1280,512]{2,1,0:T(8,128)(2,1)S(1)} %bitcast.92), custom_call_target="tpu_custom_call" | custom-call | flops 20753999872 | bytes 1000000 | tf_op jit(solution)/shard_map/weight_grad/pallas_call | solution.py:647
  393.4 2.5 add_convert_fusion.12
  397.4 11.8 %collective-permute-done.34 = bf16[288,1536]{1,0:T(8,128)(2,1)S(1)} collective-permute-done((bf16[288,1536]{1,0:T(8,128)(2,1)}, bf16[288,1536]{1,0:T(8,128)(2,1)S(1)}, u32[]{:S(2)}, u32[]{:S(2)}) %collective-permute-start.34) | collective-permute-done | bytes 884768 | tf_op jit(solution)/shard_map/ppermute | solution.py:935
  411.9 5.5 copy-done.69
  417.4 18.3 %weight_grad.5 = (bf16[2,4,512,384]{3,2,1,0:T(8,128)(2,1)}, bf16[2,4,512,384]{3,2,1,0:T(8,128)(2,1)S(1)}) custom-call(s32[4]{0:T(128)S(1)} %add_add_fusion.3.order_ref, bf16[4,1280,512]{2,1,0:T(8,128)(2,1)S(1)} %bitcast.90, bf16[4,1280,1536]{2,1,0:T(8,128)(2,1)S(1)} %copy-done.69), custom_call_target="tpu_custom_call" | custom-call | flops 20753999872 | bytes 1000000 | tf_op jit(solution)/shard_map/weight_grad/pallas_call | solution.py:647
  441.1 6.2 collective-permute-done.41
  449.4 7.9 %collective-permute-done.36.refs_1_ = bf16[256,1536]{1,0:T(8,128)(2,1)S(1)} collective-permute-done((bf16[256,1536]{1,0:T(8,128)(2,1)S(1)}, bf16[256,1536]{1,0:T(8,128)(2,1)S(1)}, u32[]{:S(2)}, u32[]{:S(2)}) %collective-permute-start.36) | collective-permute-done | bytes 786464 | tf_op jit(solution)/shard_map/ppermute | solution.py:935
  457.4 3.8 collective-permute-done.40.refs_5_.refs_8_
  461.2 3.9 middle_back.1
  465.1 1.7 copy-done.66
  469.2 1.8 collective-permute-start.44
  472.1 14.8 %collective-permute-done.42.a_ref = bf16[256,1536]{1,0:T(8,128)(2,1)S(1)} collective-permute-done((bf16[256,1536]{1,0:T(8,128)(2,1)S(1)}, bf16[256,1536]{1,0:T(8,128)(2,1)S(1)}, u32[]{:S(2)}, u32[]{:S(2)}) %collective-permute-start.42) | collective-permute-done | bytes 786464 | tf_op jit(solution)/shard_map/ppermute | solution.py:1144
  488.3 3.5 two_sums.3
  493.8 1.7 collective-permute-start.49
  496.9 15.1 %attend_back.2 = (bf16[2048,384]{1,0:T(8,128)(2,1)S(1)}, f32[2,2048,64]{2,1,0:T(8,128)S(1)}, f32[2,2048,64]{2,1,0:T(8,128)S(1)}) custom-call(s32[4]{0:T(128)S(1)} %fusion.10.order_ref, bf16[6,2048,64]{2,1,0:T(8,128)(2,1)S(1)} %copy-done, bf16[2,2048,64]{2,1,0:T(8,128)(2,1)S(1)} %copy-done.6, bf16[2,2048,64]{2,1,0:T(8,128)(2,1)S(1)} %copy-done.9, ...), custom_call_target="tpu_custom_call" | custom-call | flops 31131000832 | bytes 1000000 | tf_op jit(solution)/shard_map/attend_back/pallas_call | solution.py:353
  519.6 8.1 %collective-permute-done.46.a_ref = bf16[512,1536]{1,0:T(8,128)(2,1)} collective-permute-done((bf16[512,1536]{1,0:T(8,128)(2,1)}, bf16[512,1536]{1,0:T(8,128)(2,1)}, u32[]{:S(2)}, u32[]{:S(2)}) %collective-permute-start.46) | collective-permute-done | bytes 1572896 | tf_op jit(solution)/shard_map/ppermute | solution.py:1149
  532.8 8.2 %two_sums.4 = (bf16[512,1536]{1,0:T(8,128)(2,1)}, bf16[512,1536]{1,0:T(8,128)(2,1)}) custom-call(s32[1]{0:T(128)} %bitcast.37.wait_ref, bf16[512,1536]{1,0:T(8,128)(2,1)} %collective-permute-done.46.a_ref, bf16[512,1536]{1,0:T(8,128)(2,1)} %collective-permute-done.47.b_ref, bf16[256,1536]{1,0:T(8,128)(2,1)S(1)} %copy-done.78, ...), custom_call_target="tpu_custom_call" | custom-call | flops 4611999744 | bytes 1000000 | tf_op jit(solution)/shard_map/two_sums/pallas_call | solution.py:816
  543.2 3.1 add_convert_fusion.3
  548.5 1.8 collective-permute-start.55
  550.5 39.9 %attend_back.3 = (bf16[2048,384]{1,0:T(8,128)(2,1)S(1)}, bf16[2048,256]{1,0:T(8,128)(2,1)S(1)}) custom-call(s32[4]{0:T(128)S(1)} %fusion.9.order_ref, bf16[6,2048,64]{2,1,0:T(8,128)(2,1)} %get-tuple-element.140.q_ref, bf16[2,2048,64]{2,1,0:T(8,128)(2,1)S(1)} %copy-done.7, bf16[2,2048,64]{2,1,0:T(8,128)(2,1)S(1)} %copy-done.10, ...), custom_call_target="tpu_custom_call", output_to_operand_aliasing={{0}: (18, {})} | custom-call | flops 31131000832 | bytes 1000000 | tf_op jit(solution)/shard_map/attend_back/pallas_call | solution.py:353
  593.8 2.7 fusion.1
  598.3 8.0 %two_sums.5 = (bf16[512,1536]{1,0:T(8,128)(2,1)}, bf16[512,1536]{1,0:T(8,128)(2,1)}) custom-call(s32[1]{0:T(128)} %bitcast.41.wait_ref, bf16[512,1536]{1,0:T(8,128)(2,1)} %collective-permute-done.51.a_ref, bf16[512,1536]{1,0:T(8,128)(2,1)} %collective-permute-done.52.b_ref, bf16[256,1536]{1,0:T(8,128)(2,1)S(1)} %copy-done.74, ...), custom_call_target="tpu_custom_call" | custom-call | flops 4611999744 | bytes 1000000 | tf_op jit(solution)/shard_map/two_sums/pallas_call | solution.py:816
  606.5 13.2 %dense_grad.1 = bf16[1536,1152]{1,0:T(8,128)(2,1)} custom-call(s32[4]{0:T(128)S(1)} %fusion.11.order_ref, bf16[2048,1536]{1,0:T(8,128)(2,1)} %get-tuple-element.255.n_ref, bf16[2048,384]{1,0:T(8,128)(2,1)S(1)} %copy-done.52, bf16[2048,256]{1,0:T(8,128)(2,1)S(1)} %copy-done.55, bf16[512,1536]{1,0:T(8,128)(2,1)S(1)} %copy-done.17, ...), custom_call_target="tpu_custom_call" | custom-call | flops 14988999680 | bytes 1000000 | tf_op jit(solution)/shard_map/dense_grad/pallas_call | solution.py:454
  625.3 9.0 %qkv_back.1 = (bf16[1024,1536]{1,0:T(8,128)(2,1)S(1)}, bf16[1024,1536]{1,0:T(8,128)(2,1)S(1)}) custom-call(s32[8]{0:T(128)S(1)} %broadcast_add_fusion.order_ref, bf16[2048,384]{1,0:T(8,128)(2,1)S(1)} %copy-done.53, bf16[2048,256]{1,0:T(8,128)(2,1)S(1)} %copy-done.56, bf16[1536,384]{1,0:T(8,128)(2,1)S(1)} %copy-done.43, bf16[1536,128]{1,0:T(8,128)(2,1)S(1)} %copy-done.45, ...), custom_call_target="tpu_custom_call" | custom-call | flops 10376999936 | bytes 1000000 | tf_op jit(solution)/shard_map/qkv_back/pallas_call | solution.py:392
  638.3 3.1 fusion.3
  641.4 1.8 add_convert_fusion.1
  643.6 2.0 collective-permute-start.57
  645.6 40.8 %collective-permute-done.53.a_ref = bf16[512,1536]{1,0:T(8,128)(2,1)} collective-permute-done((bf16[512,1536]{1,0:T(8,128)(2,1)}, bf16[512,1536]{1,0:T(8,128)(2,1)}, u32[]{:S(2)}, u32[]{:S(2)}) %collective-permute-start.53) | collective-permute-done | bytes 1572896 | tf_op jit(solution)/shard_map/ppermute | solution.py:1149
  686.4 2.3 collective-permute-done.54.b_ref
  688.7 1.9 copy-done.65
  692.8 6.3 layer_out.1
  700.9 4.3 fusion
  705.3 6.3 collective-permute-done.57.far_ref
  711.6 2.8 copy-done.38
  714.4 6.6 input_back.1
  730.0 2.0 collective-permute-done.59
  (423 shorter events, 105.2 us)
Async XLA Ops:
  7.2 717.3 %reduce-scatter.2.cloned.1.call-start = ((), (), s32[]{:S(2)}) async-start(), calls=%async_computation.1 | async-start | bytes 3981312 | tf_op jit(solution)/shard_map/reduce_scatter | solution.py:1196
  10.4 44.0 %collective-permute-start = (bf16[528,1536]{1,0:T(8,128)(2,1)S(1)}, bf16[528,1536]{1,0:T(8,128)(2,1)}, u32[]{:S(2)}, u32[]{:S(2)}) collective-permute-start(bf16[528,1536]{1,0:T(8,128)(2,1)S(1)} %maximum_maximum_fusion.refs_2_), channel_id=1, source_target_pairs={{0,8},{8,16},{16,24},{24,28},{28,20},{20,12},{12,4},{4,0},{1,9},{9... | collective-permute-start | bytes 4866056 | tf_op jit(solution)/shard_map/ppermute | solution.py:1010
  13.5 40.9 %collective-permute-start.2 = (bf16[528,1536]{1,0:T(8,128)(2,1)S(1)}, bf16[528,1536]{1,0:T(8,128)(2,1)}, u32[]{:S(2)}, u32[]{:S(2)}) collective-permute-start(bf16[528,1536]{1,0:T(8,128)(2,1)S(1)} %maximum_maximum_fusion.refs_2_), channel_id=1, source_target_pairs={{8,0},{16,8},{24,16},{28,24},{20,28},{12,20},{4,12},{0,4},{9,1},{1... | collective-permute-start | bytes 4866056 | tf_op jit(solution)/shard_map/ppermute | solution.py:1010
  54.4 3.7 collective-permute-start.4
  55.1 38.4 %collective-permute-start.1 = (bf16[528,1536]{1,0:T(8,128)(2,1)}, bf16[528,1536]{1,0:T(8,128)(2,1)}, u32[]{:S(2)}, u32[]{:S(2)}) collective-permute-start(bf16[528,1536]{1,0:T(8,128)(2,1)} %collective-permute-done.refs_4_), channel_id=1, source_target_pairs={{0,8},{8,16},{16,24},{24,28},{28,20},{20,12},{12,4},{4,0},{1,9},{9... | collective-permute-start | bytes 4866056 | tf_op jit(solution)/shard_map/ppermute | solution.py:1010
  57.1 37.9 %collective-permute-start.3 = (bf16[528,1536]{1,0:T(8,128)(2,1)}, bf16[528,1536]{1,0:T(8,128)(2,1)}, u32[]{:S(2)}, u32[]{:S(2)}) collective-permute-start(bf16[528,1536]{1,0:T(8,128)(2,1)} %collective-permute-done.2.refs_5_), channel_id=1, source_target_pairs={{8,0},{16,8},{24,16},{28,24},{20,28},{12,20},{4,12},{0,4},{9,1},{1... | collective-permute-start | bytes 4866056 | tf_op jit(solution)/shard_map/ppermute | solution.py:1010
  61.1 36.7 %collective-permute-start.7 = (bf16[512,1536]{1,0:T(8,128)(2,1)}, bf16[512,1536]{1,0:T(8,128)(2,1)S(1)}, u32[]{:S(2)}, u32[]{:S(2)}) collective-permute-start(bf16[512,1536]{1,0:T(8,128)(2,1)} %add_convert_fusion.5), channel_id=1, source_target_pairs={{0,2},{2,0},{1,3},{3,1},{4,6},{6,4},{5,7},{7,5},{8,10},{10,8},{9,1... | collective-permute-start | bytes 4718600 | tf_op jit(solution)/shard_map/ppermute | solution.py:952
  79.6 16.9 %collective-permute-start.6 = (bf16[256,1536]{1,0:T(8,128)(2,1)}, bf16[256,1536]{1,0:T(8,128)(2,1)S(1)}, u32[]{:S(2)}, u32[]{:S(2)}) collective-permute-start(bf16[256,1536]{1,0:T(8,128)(2,1)} %get-tuple-element.307), channel_id=1, source_target_pairs={{0,1},{1,0},{2,3},{3,2},{4,5},{5,4},{6,7},{7,6},{8,9},{9,8},{10,11... | collective-permute-start | bytes 2359304 | tf_op jit(solution)/shard_map/ppermute | solution.py:948
  79.8 16.8 %collective-permute-start.5 = (bf16[256,1536]{1,0:T(8,128)(2,1)S(1)}, bf16[256,1536]{1,0:T(8,128)(2,1)}, u32[]{:S(2)}, u32[]{:S(2)}) collective-permute-start(bf16[256,1536]{1,0:T(8,128)(2,1)S(1)} %get-tuple-element.306), channel_id=1, source_target_pairs={{0,1},{1,0},{2,3},{3,2},{4,5},{5,4},{6,7},{7,6},{8,9},{9,8},{10,11... | collective-permute-start | bytes 2359304 | tf_op jit(solution)/shard_map/ppermute | solution.py:948
  95.0 108.7 %collective-permute-start.22 = (bf16[528,1536]{1,0:T(8,128)(2,1)}, bf16[528,1536]{1,0:T(8,128)(2,1)}, u32[]{:S(2)}, u32[]{:S(2)}) collective-permute-start(bf16[528,1536]{1,0:T(8,128)(2,1)} %collective-permute-done.1.refs_4_), channel_id=1, source_target_pairs={{0,8},{8,16},{16,24},{24,28},{28,20},{20,12},{12,4},{4,0},{1,9},{9... | collective-permute-start | bytes 4866056 | tf_op jit(solution)/shard_map/ppermute | solution.py:1010
  105.4 45.2 %collective-permute-start.8 = (bf16[256,1536]{1,0:T(8,128)(2,1)S(1)}, bf16[256,1536]{1,0:T(8,128)(2,1)}, u32[]{:S(2)}, u32[]{:S(2)}) collective-permute-start(bf16[256,1536]{1,0:T(8,128)(2,1)S(1)} %get-tuple-element.227.refs_0_.first_ref), channel_id=1, source_target_pairs={{0,8},{8,16},{16,24},{24,28},{28,20},{20,12},{12,4},{4,0},{1,9},{9... | collective-permute-start | bytes 2359304 | tf_op jit(solution)/shard_map/ppermute | solution.py:1056
  107.3 58.4 %collective-permute-start.10 = (bf16[256,1536]{1,0:T(8,128)(2,1)S(1)}, bf16[256,1536]{1,0:T(8,128)(2,1)}, u32[]{:S(2)}, u32[]{:S(2)}) collective-permute-start(bf16[256,1536]{1,0:T(8,128)(2,1)S(1)} %get-tuple-element.227.refs_0_.first_ref), channel_id=1, source_target_pairs={{8,0},{16,8},{24,16},{28,24},{20,28},{12,20},{4,12},{0,4},{9,1},{1... | collective-permute-start | bytes 2359304 | tf_op jit(solution)/shard_map/ppermute | solution.py:1056
  107.4 58.3 %collective-permute-start.9 = (bf16[256,1536]{1,0:T(8,128)(2,1)S(1)}, bf16[256,1536]{1,0:T(8,128)(2,1)}, u32[]{:S(2)}, u32[]{:S(2)}) collective-permute-start(bf16[256,1536]{1,0:T(8,128)(2,1)S(1)} %get-tuple-element.228.refs_1_.second_ref), channel_id=1, source_target_pairs={{0,8},{8,16},{16,24},{24,28},{28,20},{20,12},{12,4},{4,0},{1,9},{9... | collective-permute-start | bytes 2359304 | tf_op jit(solution)/shard_map/ppermute | solution.py:1056
  109.3 56.4 %collective-permute-start.11 = (bf16[256,1536]{1,0:T(8,128)(2,1)S(1)}, bf16[256,1536]{1,0:T(8,128)(2,1)S(1)}, u32[]{:S(2)}, u32[]{:S(2)}) collective-permute-start(bf16[256,1536]{1,0:T(8,128)(2,1)S(1)} %get-tuple-element.228.refs_1_.second_ref), channel_id=1, source_target_pairs={{8,0},{16,8},{24,16},{28,24},{20,28},{12,20},{4,12},{0,4},{9,1},{1... | collective-permute-start | bytes 2359304 | tf_op jit(solution)/shard_map/ppermute | solution.py:1056
  150.5 53.7 %collective-permute-start.23 = (bf16[528,1536]{1,0:T(8,128)(2,1)}, bf16[528,1536]{1,0:T(8,128)(2,1)S(1)}, u32[]{:S(2)}, u32[]{:S(2)}) collective-permute-start(bf16[528,1536]{1,0:T(8,128)(2,1)} %collective-permute-done.3.refs_5_), channel_id=1, source_target_pairs={{8,0},{16,8},{24,16},{28,24},{20,28},{12,20},{4,12},{0,4},{9,1},{1... | collective-permute-start | bytes 4866056 | tf_op jit(solution)/shard_map/ppermute | solution.py:1010
  165.7 41.9 %collective-permute-start.12 = (bf16[256,1536]{1,0:T(8,128)(2,1)}, bf16[256,1536]{1,0:T(8,128)(2,1)}, u32[]{:S(2)}, u32[]{:S(2)}) collective-permute-start(bf16[256,1536]{1,0:T(8,128)(2,1)} %collective-permute-done.8.refs_0_), channel_id=1, source_target_pairs={{0,8},{8,16},{16,24},{24,28},{28,20},{20,12},{12,4},{4,0},{1,9},{9... | collective-permute-start | bytes 2359304 | tf_op jit(solution)/shard_map/ppermute | solution.py:1056
  167.4 40.8 %collective-permute-start.13 = (bf16[256,1536]{1,0:T(8,128)(2,1)}, bf16[256,1536]{1,0:T(8,128)(2,1)}, u32[]{:S(2)}, u32[]{:S(2)}) collective-permute-start(bf16[256,1536]{1,0:T(8,128)(2,1)} %collective-permute-done.9.refs_1_), channel_id=1, source_target_pairs={{0,8},{8,16},{16,24},{24,28},{28,20},{20,12},{12,4},{4,0},{1,9},{9... | collective-permute-start | bytes 2359304 | tf_op jit(solution)/shard_map/ppermute | solution.py:1056
  168.9 39.2 %collective-permute-start.14 = (bf16[256,1536]{1,0:T(8,128)(2,1)}, bf16[256,1536]{1,0:T(8,128)(2,1)}, u32[]{:S(2)}, u32[]{:S(2)}) collective-permute-start(bf16[256,1536]{1,0:T(8,128)(2,1)} %collective-permute-done.10.refs_2_), channel_id=1, source_target_pairs={{8,0},{16,8},{24,16},{28,24},{20,28},{12,20},{4,12},{0,4},{9,1},{1... | collective-permute-start | bytes 2359304 | tf_op jit(solution)/shard_map/ppermute | solution.py:1056
  203.7 20.8 %collective-permute-start.15 = (bf16[256,1536]{1,0:T(8,128)(2,1)}, bf16[256,1536]{1,0:T(8,128)(2,1)}, u32[]{:S(2)}, u32[]{:S(2)}) collective-permute-start(bf16[256,1536]{1,0:T(8,128)(2,1)} %copy-done.120), channel_id=1, source_target_pairs={{8,0},{16,8},{24,16},{28,24},{20,28},{12,20},{4,12},{0,4},{9,1},{1... | collective-permute-start | bytes 2359304 | tf_op jit(solution)/shard_map/ppermute | solution.py:1056
  204.2 59.0 %copy-start.109 = (bf16[528,1536]{1,0:T(8,128)(2,1)}, bf16[528,1536]{1,0:T(8,128)(2,1)S(1)}, u32[]{:S(2)}) copy-start(bf16[528,1536]{1,0:T(8,128)(2,1)S(1)} %collective-permute-done.23.refs_5_) | copy-start | bytes 4866052
  205.9 22.2 %collective-permute-start.24 = (bf16[256,1536]{1,0:T(8,128)(2,1)S(1)}, bf16[256,1536]{1,0:T(8,128)(2,1)S(1)}, u32[]{:S(2)}, u32[]{:S(2)}) collective-permute-start(bf16[256,1536]{1,0:T(8,128)(2,1)S(1)} %slice.181), channel_id=1, source_target_pairs={{0,8},{8,16},{16,24},{24,28},{28,20},{20,12},{12,4},{4,0},{1,9},{9... | collective-permute-start | bytes 2359304 | tf_op jit(solution)/shard_map/ppermute | solution.py:1075
  207.6 55.6 %collective-permute-start.25 = (bf16[272,1536]{1,0:T(8,128)(2,1)S(1)}, bf16[272,1536]{1,0:T(8,128)(2,1)S(1)}, u32[]{:S(2)}, u32[]{:S(2)}) collective-permute-start(bf16[272,1536]{1,0:T(8,128)(2,1)S(1)} %slice.182), channel_id=1, source_target_pairs={{8,0},{16,8},{24,16},{28,24},{20,28},{12,20},{4,12},{0,4},{9,1},{1... | collective-permute-start | bytes 2506760 | tf_op jit(solution)/shard_map/ppermute | solution.py:1075
  224.6 40.0 %collective-permute-start.16 = (bf16[256,1536]{1,0:T(8,128)(2,1)}, bf16[256,1536]{1,0:T(8,128)(2,1)}, u32[]{:S(2)}, u32[]{:S(2)}) collective-permute-start(bf16[256,1536]{1,0:T(8,128)(2,1)} %collective-permute-done.12.refs_0_), channel_id=1, source_target_pairs={{0,8},{8,16},{16,24},{24,28},{28,20},{20,12},{12,4},{4,0},{1,9},{9... | collective-permute-start | bytes 2359304 | tf_op jit(solution)/shard_map/ppermute | solution.py:1056
  226.1 38.4 %collective-permute-start.17 = (bf16[256,1536]{1,0:T(8,128)(2,1)}, bf16[256,1536]{1,0:T(8,128)(2,1)}, u32[]{:S(2)}, u32[]{:S(2)}) collective-permute-start(bf16[256,1536]{1,0:T(8,128)(2,1)} %collective-permute-done.13.refs_1_), channel_id=1, source_target_pairs={{0,8},{8,16},{16,24},{24,28},{28,20},{20,12},{12,4},{4,0},{1,9},{9... | collective-permute-start | bytes 2359304 | tf_op jit(solution)/shard_map/ppermute | solution.py:1056
  227.7 36.9 %collective-permute-start.18 = (bf16[256,1536]{1,0:T(8,128)(2,1)}, bf16[256,1536]{1,0:T(8,128)(2,1)}, u32[]{:S(2)}, u32[]{:S(2)}) collective-permute-start(bf16[256,1536]{1,0:T(8,128)(2,1)} %collective-permute-done.14.refs_2_), channel_id=1, source_target_pairs={{8,0},{16,8},{24,16},{28,24},{20,28},{12,20},{4,12},{0,4},{9,1},{1... | collective-permute-start | bytes 2359304 | tf_op jit(solution)/shard_map/ppermute | solution.py:1056
  228.2 44.6 %collective-permute-start.19 = (bf16[256,1536]{1,0:T(8,128)(2,1)}, bf16[256,1536]{1,0:T(8,128)(2,1)}, u32[]{:S(2)}, u32[]{:S(2)}) collective-permute-start(bf16[256,1536]{1,0:T(8,128)(2,1)} %collective-permute-done.15.refs_3_), channel_id=1, source_target_pairs={{8,0},{16,8},{24,16},{28,24},{20,28},{12,20},{4,12},{0,4},{9,1},{1... | collective-permute-start | bytes 2359304 | tf_op jit(solution)/shard_map/ppermute | solution.py:1056
  272.8 38.9 %collective-permute-start.20 = (bf16[256,1536]{1,0:T(8,128)(2,1)}, bf16[256,1536]{1,0:T(8,128)(2,1)S(1)}, u32[]{:S(2)}, u32[]{:S(2)}) collective-permute-start(bf16[256,1536]{1,0:T(8,128)(2,1)} %collective-permute-done.16.refs_0_), channel_id=1, source_target_pairs={{0,8},{8,16},{16,24},{24,28},{28,20},{20,12},{12,4},{4,0},{1,9},{9... | collective-permute-start | bytes 2359304 | tf_op jit(solution)/shard_map/ppermute | solution.py:1056
  274.3 37.3 %collective-permute-start.21 = (bf16[256,1536]{1,0:T(8,128)(2,1)}, bf16[256,1536]{1,0:T(8,128)(2,1)S(1)}, u32[]{:S(2)}, u32[]{:S(2)}) collective-permute-start(bf16[256,1536]{1,0:T(8,128)(2,1)} %collective-permute-done.19.refs_3_), channel_id=1, source_target_pairs={{8,0},{16,8},{24,16},{28,24},{20,28},{12,20},{4,12},{0,4},{9,1},{1... | collective-permute-start | bytes 2359304 | tf_op jit(solution)/shard_map/ppermute | solution.py:1056
  309.6 30.6 %collective-permute-start.27 = (bf16[288,1536]{1,0:T(8,128)(2,1)}, bf16[288,1536]{1,0:T(8,128)(2,1)S(1)}, u32[]{:S(2)}, u32[]{:S(2)}) collective-permute-start(bf16[288,1536]{1,0:T(8,128)(2,1)} %get-tuple-element.202), channel_id=1, source_target_pairs={{0,8},{8,16},{16,24},{24,28},{28,20},{20,12},{12,4},{4,0},{1,9},{9... | collective-permute-start | bytes 2654216 | tf_op jit(solution)/shard_map/ppermute | solution.py:935
  311.2 27.7 %collective-permute-start.28 = (bf16[256,1536]{1,0:T(8,128)(2,1)}, bf16[256,1536]{1,0:T(8,128)(2,1)S(1)}, u32[]{:S(2)}, u32[]{:S(2)}) collective-permute-start(bf16[256,1536]{1,0:T(8,128)(2,1)} %get-tuple-element.204), channel_id=1, source_target_pairs={{8,0},{16,8},{24,16},{28,24},{20,28},{12,20},{4,12},{0,4},{9,1},{1... | collective-permute-start | bytes 2359304 | tf_op jit(solution)/shard_map/ppermute | solution.py:935
  336.7 29.9 %collective-permute-start.26 = (bf16[256,1536]{1,0:T(8,128)(2,1)}, bf16[256,1536]{1,0:T(8,128)(2,1)S(1)}, u32[]{:S(2)}, u32[]{:S(2)}) collective-permute-start(bf16[256,1536]{1,0:T(8,128)(2,1)} %get-tuple-element.200), channel_id=1, source_target_pairs={{0,8},{8,16},{16,24},{24,28},{28,20},{20,12},{12,4},{4,0},{1,9},{9... | collective-permute-start | bytes 2359304 | tf_op jit(solution)/shard_map/ppermute | solution.py:935
  339.2 30.1 %collective-permute-start.31 = (bf16[256,1536]{1,0:T(8,128)(2,1)S(1)}, bf16[256,1536]{1,0:T(8,128)(2,1)S(1)}, u32[]{:S(2)}, u32[]{:S(2)}) collective-permute-start(bf16[256,1536]{1,0:T(8,128)(2,1)S(1)} %add_convert_fusion.15), channel_id=1, source_target_pairs={{8,0},{16,8},{24,16},{28,24},{20,28},{12,20},{4,12},{0,4},{9,1},{1... | collective-permute-start | bytes 2359304 | tf_op jit(solution)/shard_map/ppermute | solution.py:935
  339.7 33.2 %collective-permute-start.32 = (bf16[288,1536]{1,0:T(8,128)(2,1)S(1)}, bf16[288,1536]{1,0:T(8,128)(2,1)S(1)}, u32[]{:S(2)}, u32[]{:S(2)}) collective-permute-start(bf16[288,1536]{1,0:T(8,128)(2,1)S(1)} %copy-done.117), channel_id=1, source_target_pairs={{8,0},{16,8},{24,16},{28,24},{20,28},{12,20},{4,12},{0,4},{9,1},{1... | collective-permute-start | bytes 2654216 | tf_op jit(solution)/shard_map/ppermute | solution.py:935
  340.4 34.2 %collective-permute-start.30 = (bf16[288,1536]{1,0:T(8,128)(2,1)S(1)}, bf16[288,1536]{1,0:T(8,128)(2,1)S(1)}, u32[]{:S(2)}, u32[]{:S(2)}) collective-permute-start(bf16[288,1536]{1,0:T(8,128)(2,1)S(1)} %add_convert_fusion.10), channel_id=1, source_target_pairs={{0,8},{8,16},{16,24},{24,28},{28,20},{20,12},{12,4},{4,0},{1,9},{9... | collective-permute-start | bytes 2654216 | tf_op jit(solution)/shard_map/ppermute | solution.py:935
  365.6 44.5 %collective-permute-start.35 = (bf16[2,4,384,512]{3,2,1,0:T(8,128)(2,1)S(1)}, bf16[2,4,384,512]{3,2,1,0:T(8,128)(2,1)S(1)}, u32[]{:S(2)}, u32[]{:S(2)}) collective-permute-start(bf16[2,4,384,512]{3,2,1,0:T(8,128)(2,1)S(1)} %get-tuple-element.221), channel_id=1, source_target_pairs={{0,1},{1,0},{2,3},{3,2},{4,5},{5,4},{6,7},{7,6},{8,9},{9,8},{10,11... | collective-permute-start | bytes 9437192 | tf_op jit(solution)/shard_map/ppermute | solution.py:948
  367.7 25.7 %collective-permute-start.29 = (bf16[256,1536]{1,0:T(8,128)(2,1)}, bf16[256,1536]{1,0:T(8,128)(2,1)}, u32[]{:S(2)}, u32[]{:S(2)}) collective-permute-start(bf16[256,1536]{1,0:T(8,128)(2,1)} %add_convert_fusion.14), channel_id=1, source_target_pairs={{0,8},{8,16},{16,24},{24,28},{28,20},{20,12},{12,4},{4,0},{1,9},{9... | collective-permute-start | bytes 2359304 | tf_op jit(solution)/shard_map/ppermute | solution.py:935
  370.4 79.0 %collective-permute-start.37 = (bf16[256,1536]{1,0:T(8,128)(2,1)}, bf16[256,1536]{1,0:T(8,128)(2,1)S(1)}, u32[]{:S(2)}, u32[]{:S(2)}) collective-permute-start(bf16[256,1536]{1,0:T(8,128)(2,1)} %add_convert_fusion.13), channel_id=1, source_target_pairs={{8,0},{16,8},{24,16},{28,24},{20,28},{12,20},{4,12},{0,4},{9,1},{1... | collective-permute-start | bytes 2359304 | tf_op jit(solution)/shard_map/ppermute | solution.py:935
  374.1 35.1 %collective-permute-start.34 = (bf16[288,1536]{1,0:T(8,128)(2,1)}, bf16[288,1536]{1,0:T(8,128)(2,1)S(1)}, u32[]{:S(2)}, u32[]{:S(2)}) collective-permute-start(bf16[288,1536]{1,0:T(8,128)(2,1)} %add_convert_fusion.8), channel_id=1, source_target_pairs={{8,0},{16,8},{24,16},{28,24},{20,28},{12,20},{4,12},{0,4},{9,1},{1... | collective-permute-start | bytes 2654216 | tf_op jit(solution)/shard_map/ppermute | solution.py:935
  374.9 74.5 %collective-permute-start.38 = (bf16[288,1536]{1,0:T(8,128)(2,1)S(1)}, bf16[288,1536]{1,0:T(8,128)(2,1)S(1)}, u32[]{:S(2)}, u32[]{:S(2)}) collective-permute-start(bf16[288,1536]{1,0:T(8,128)(2,1)S(1)} %add_convert_fusion.9), channel_id=1, source_target_pairs={{0,8},{8,16},{16,24},{24,28},{28,20},{20,12},{12,4},{4,0},{1,9},{9... | collective-permute-start | bytes 2654216 | tf_op jit(solution)/shard_map/ppermute | solution.py:935
  395.9 41.4 %collective-permute-start.33 = (bf16[256,1536]{1,0:T(8,128)(2,1)}, bf16[256,1536]{1,0:T(8,128)(2,1)}, u32[]{:S(2)}, u32[]{:S(2)}) collective-permute-start(bf16[256,1536]{1,0:T(8,128)(2,1)} %add_convert_fusion.12), channel_id=1, source_target_pairs={{0,8},{8,16},{16,24},{24,28},{28,20},{20,12},{12,4},{4,0},{1,9},{9... | collective-permute-start | bytes 2359304 | tf_op jit(solution)/shard_map/ppermute | solution.py:935
  409.6 30.7 %collective-permute-start.39 = (bf16[288,1536]{1,0:T(8,128)(2,1)S(1)}, bf16[288,1536]{1,0:T(8,128)(2,1)S(1)}, u32[]{:S(2)}, u32[]{:S(2)}) collective-permute-start(bf16[288,1536]{1,0:T(8,128)(2,1)S(1)} %add_convert_fusion.7), channel_id=1, source_target_pairs={{8,0},{16,8},{24,16},{28,24},{20,28},{12,20},{4,12},{0,4},{9,1},{1... | collective-permute-start | bytes 2654216 | tf_op jit(solution)/shard_map/ppermute | solution.py:935
  411.8 35.6 %collective-permute-start.41 = (bf16[4,384,512]{2,1,0:T(8,128)(2,1)S(1)}, bf16[4,384,512]{2,1,0:T(8,128)(2,1)S(1)}, u32[]{:S(2)}, u32[]{:S(2)}) collective-permute-start(bf16[4,384,512]{2,1,0:T(8,128)(2,1)S(1)} %bitcast.93), channel_id=1, source_target_pairs={{0,2},{2,0},{1,3},{3,1},{4,6},{6,4},{5,7},{7,5},{8,10},{10,8},{9,1... | collective-permute-start | bytes 4718600 | tf_op jit(solution)/shard_map/ppermute | solution.py:952
  438.7 18.7 %collective-permute-start.36 = (bf16[256,1536]{1,0:T(8,128)(2,1)S(1)}, bf16[256,1536]{1,0:T(8,128)(2,1)S(1)}, u32[]{:S(2)}, u32[]{:S(2)}) collective-permute-start(bf16[256,1536]{1,0:T(8,128)(2,1)S(1)} %add_convert_fusion.11), channel_id=1, source_target_pairs={{0,8},{8,16},{16,24},{24,28},{28,20},{20,12},{12,4},{4,0},{1,9},{9... | collective-permute-start | bytes 2359304 | tf_op jit(solution)/shard_map/ppermute | solution.py:935
  440.6 20.5 %collective-permute-start.40 = (bf16[288,1536]{1,0:T(8,128)(2,1)S(1)}, bf16[288,1536]{1,0:T(8,128)(2,1)S(1)}, u32[]{:S(2)}, u32[]{:S(2)}) collective-permute-start(bf16[288,1536]{1,0:T(8,128)(2,1)S(1)} %add_convert_fusion.6), channel_id=1, source_target_pairs={{8,0},{16,8},{24,16},{28,24},{20,28},{12,20},{4,12},{0,4},{9,1},{1... | collective-permute-start | bytes 2654216 | tf_op jit(solution)/shard_map/ppermute | solution.py:935
  466.9 29.9 %collective-permute-start.45 = (bf16[512,1536]{1,0:T(8,128)(2,1)S(1)}, bf16[512,1536]{1,0:T(8,128)(2,1)S(1)}, u32[]{:S(2)}, u32[]{:S(2)}) collective-permute-start(bf16[512,1536]{1,0:T(8,128)(2,1)S(1)} %get-tuple-element.229.dba_ref.db0_ref), channel_id=1, source_target_pairs={{0,1},{1,0},{2,3},{3,2},{4,5},{5,4},{6,7},{7,6},{8,9},{9,8},{10,11... | collective-permute-start | bytes 4718600 | tf_op jit(solution)/shard_map/ppermute | solution.py:948
  467.0 19.9 %collective-permute-start.42 = (bf16[256,1536]{1,0:T(8,128)(2,1)S(1)}, bf16[256,1536]{1,0:T(8,128)(2,1)S(1)}, u32[]{:S(2)}, u32[]{:S(2)}) collective-permute-start(bf16[256,1536]{1,0:T(8,128)(2,1)S(1)} %copy-done.119), channel_id=1, source_target_pairs={{0,8},{8,16},{16,24},{24,28},{28,20},{20,12},{12,4},{4,0},{1,9},{9... | collective-permute-start | bytes 2359304 | tf_op jit(solution)/shard_map/ppermute | solution.py:1144
  468.6 19.6 %collective-permute-start.43 = (bf16[256,1536]{1,0:T(8,128)(2,1)S(1)}, bf16[256,1536]{1,0:T(8,128)(2,1)S(1)}, u32[]{:S(2)}, u32[]{:S(2)}) collective-permute-start(bf16[256,1536]{1,0:T(8,128)(2,1)S(1)} %copy-done.118), channel_id=1, source_target_pairs={{8,0},{16,8},{24,16},{28,24},{20,28},{12,20},{4,12},{0,4},{9,1},{1... | collective-permute-start | bytes 2359304 | tf_op jit(solution)/shard_map/ppermute | solution.py:1144
  469.2 24.7 %collective-permute-start.44 = (bf16[256,1536]{1,0:T(8,128)(2,1)S(1)}, bf16[256,1536]{1,0:T(8,128)(2,1)S(1)}, u32[]{:S(2)}, u32[]{:S(2)}) collective-permute-start(bf16[256,1536]{1,0:T(8,128)(2,1)S(1)} %get-tuple-element.305), channel_id=1, source_target_pairs={{0,2},{2,0},{1,3},{3,1},{4,6},{6,4},{5,7},{7,5},{8,10},{10,8},{9,1... | collective-permute-start | bytes 2359304 | tf_op jit(solution)/shard_map/ppermute | solution.py:952
  470.9 72.2 %collective-permute-start.48 = (bf16[2,4,384,512]{3,2,1,0:T(8,128)(2,1)}, bf16[2,4,384,512]{3,2,1,0:T(8,128)(2,1)}, u32[]{:S(2)}, u32[]{:S(2)}) collective-permute-start(bf16[2,4,384,512]{3,2,1,0:T(8,128)(2,1)} %get-tuple-element.248), channel_id=1, source_target_pairs={{0,1},{1,0},{2,3},{3,2},{4,5},{5,4},{6,7},{7,6},{8,9},{9,8},{10,11... | collective-permute-start | bytes 9437192 | tf_op jit(solution)/shard_map/ppermute | solution.py:948
  491.8 35.9 %collective-permute-start.46 = (bf16[512,1536]{1,0:T(8,128)(2,1)}, bf16[512,1536]{1,0:T(8,128)(2,1)}, u32[]{:S(2)}, u32[]{:S(2)}) collective-permute-start(bf16[512,1536]{1,0:T(8,128)(2,1)} %get-tuple-element.238), channel_id=1, source_target_pairs={{0,8},{8,16},{16,24},{24,28},{28,20},{20,12},{12,4},{4,0},{1,9},{9... | collective-permute-start | bytes 4718600 | tf_op jit(solution)/shard_map/ppermute | solution.py:1149
  492.6 35.7 %collective-permute-start.47 = (bf16[512,1536]{1,0:T(8,128)(2,1)}, bf16[512,1536]{1,0:T(8,128)(2,1)}, u32[]{:S(2)}, u32[]{:S(2)}) collective-permute-start(bf16[512,1536]{1,0:T(8,128)(2,1)} %get-tuple-element.239), channel_id=1, source_target_pairs={{8,0},{16,8},{24,16},{28,24},{20,28},{12,20},{4,12},{0,4},{9,1},{1... | collective-permute-start | bytes 4718600 | tf_op jit(solution)/shard_map/ppermute | solution.py:1149
  493.8 23.2 %collective-permute-start.49 = (bf16[256,1536]{1,0:T(8,128)(2,1)S(1)}, bf16[256,1536]{1,0:T(8,128)(2,1)S(1)}, u32[]{:S(2)}, u32[]{:S(2)}) collective-permute-start(bf16[256,1536]{1,0:T(8,128)(2,1)S(1)} %get-tuple-element.304), channel_id=1, source_target_pairs={{0,2},{2,0},{1,3},{3,1},{4,6},{6,4},{5,7},{7,5},{8,10},{10,8},{9,1... | collective-permute-start | bytes 2359304 | tf_op jit(solution)/shard_map/ppermute | solution.py:952
  518.5 31.9 %collective-permute-start.50 = (bf16[512,1536]{1,0:T(8,128)(2,1)}, bf16[512,1536]{1,0:T(8,128)(2,1)}, u32[]{:S(2)}, u32[]{:S(2)}) collective-permute-start(bf16[512,1536]{1,0:T(8,128)(2,1)} %add_convert_fusion.2.dba_ref.db2_ref), channel_id=1, source_target_pairs={{0,1},{1,0},{2,3},{3,2},{4,5},{5,4},{6,7},{7,6},{8,9},{9,8},{10,11... | collective-permute-start | bytes 4718600 | tf_op jit(solution)/shard_map/ppermute | solution.py:948
  519.1 119.2 %collective-permute-start.60 = (bf16[2,4,512,384]{3,2,1,0:T(8,128)(2,1)}, bf16[2,4,512,384]{3,2,1,0:T(8,128)(2,1)}, u32[]{:S(2)}, u32[]{:S(2)}) collective-permute-start(bf16[2,4,512,384]{3,2,1,0:T(8,128)(2,1)} %get-tuple-element.263), channel_id=1, source_target_pairs={{0,1},{1,0},{2,3},{3,2},{4,5},{5,4},{6,7},{7,6},{8,9},{9,8},{10,11... | collective-permute-start | bytes 9437192 | tf_op jit(solution)/shard_map/ppermute | solution.py:948
  541.1 56.8 %collective-permute-start.51 = (bf16[512,1536]{1,0:T(8,128)(2,1)}, bf16[512,1536]{1,0:T(8,128)(2,1)}, u32[]{:S(2)}, u32[]{:S(2)}) collective-permute-start(bf16[512,1536]{1,0:T(8,128)(2,1)} %get-tuple-element.245), channel_id=1, source_target_pairs={{0,8},{8,16},{16,24},{24,28},{28,20},{20,12},{12,4},{4,0},{1,9},{9... | collective-permute-start | bytes 4718600 | tf_op jit(solution)/shard_map/ppermute | solution.py:1149
  541.7 56.2 %collective-permute-start.52 = (bf16[512,1536]{1,0:T(8,128)(2,1)}, bf16[512,1536]{1,0:T(8,128)(2,1)}, u32[]{:S(2)}, u32[]{:S(2)}) collective-permute-start(bf16[512,1536]{1,0:T(8,128)(2,1)} %get-tuple-element.246), channel_id=1, source_target_pairs={{8,0},{16,8},{24,16},{28,24},{20,28},{12,20},{4,12},{0,4},{9,1},{1... | collective-permute-start | bytes 4718600 | tf_op jit(solution)/shard_map/ppermute | solution.py:1149
  548.5 45.3 %collective-permute-start.55 = (bf16[4,384,512]{2,1,0:T(8,128)(2,1)}, bf16[4,384,512]{2,1,0:T(8,128)(2,1)}, u32[]{:S(2)}, u32[]{:S(2)}) collective-permute-start(bf16[4,384,512]{2,1,0:T(8,128)(2,1)} %bitcast.43), channel_id=1, source_target_pairs={{0,2},{2,0},{1,3},{3,1},{4,6},{6,4},{5,7},{7,5},{8,10},{10,8},{9,1... | collective-permute-start | bytes 4718600 | tf_op jit(solution)/shard_map/ppermute | solution.py:952
  634.3 7.1 collective-permute-start.56
  634.4 52.0 %collective-permute-start.53 = (bf16[512,1536]{1,0:T(8,128)(2,1)}, bf16[512,1536]{1,0:T(8,128)(2,1)}, u32[]{:S(2)}, u32[]{:S(2)}) collective-permute-start(bf16[512,1536]{1,0:T(8,128)(2,1)} %get-tuple-element.252), channel_id=1, source_target_pairs={{0,8},{8,16},{16,24},{24,28},{28,20},{20,12},{12,4},{4,0},{1,9},{9... | collective-permute-start | bytes 4718600 | tf_op jit(solution)/shard_map/ppermute | solution.py:1149
  634.9 53.7 %collective-permute-start.54 = (bf16[512,1536]{1,0:T(8,128)(2,1)}, bf16[512,1536]{1,0:T(8,128)(2,1)}, u32[]{:S(2)}, u32[]{:S(2)}) collective-permute-start(bf16[512,1536]{1,0:T(8,128)(2,1)} %get-tuple-element.253), channel_id=1, source_target_pairs={{8,0},{16,8},{24,16},{28,24},{20,28},{12,20},{4,12},{0,4},{9,1},{1... | collective-permute-start | bytes 4718600 | tf_op jit(solution)/shard_map/ppermute | solution.py:1149
  641.4 59.6 %collective-permute-start.61 = (bf16[4,512,384]{2,1,0:T(8,128)(2,1)}, bf16[4,512,384]{2,1,0:T(8,128)(2,1)}, u32[]{:S(2)}, u32[]{:S(2)}) collective-permute-start(bf16[4,512,384]{2,1,0:T(8,128)(2,1)} %fusion.3), channel_id=1, source_target_pairs={{0,2},{2,0},{1,3},{3,1},{4,6},{6,4},{5,7},{7,5},{8,10},{10,8},{9,1... | collective-permute-start | bytes 4718600 | tf_op jit(solution)/shard_map/ppermute | solution.py:952
  643.6 68.0 %collective-permute-start.57 = (bf16[512,1536]{1,0:T(8,128)(2,1)}, bf16[512,1536]{1,0:T(8,128)(2,1)}, u32[]{:S(2)}, u32[]{:S(2)}) collective-permute-start(bf16[512,1536]{1,0:T(8,128)(2,1)} %add_convert_fusion.1), channel_id=1, source_target_pairs={{0,2},{2,0},{1,3},{3,1},{4,6},{6,4},{5,7},{7,5},{8,10},{10,8},{9,1... | collective-permute-start | bytes 4718600 | tf_op jit(solution)/shard_map/ppermute | solution.py:952
  725.6 1.4 collective-permute-start.58
  727.0 4.9 collective-permute-start.59
  (126 other events, 1093.6 us)
Sparse Core Ops, SparseCore 0:
  619.9 104.5 reduce-scatter.1

commit v3 on v2

--- a/solution.py
+++ b/solution.py
@@ -411,7 +411,7 @@
 
 
 def dense_grad_kernel(order_ref, n_ref, dq_ref, dkv_ref, db0_ref, db1_ref, db2_ref, db3_ref,
-                      heads_ref, first_ref, second_ref, dlog_ref, gain2_ref, gain_ref,
+                      heads_ref, normed2_ref, dlog_ref, gain2_ref, gain_ref,
                       wq_ref, wk_ref, wv_ref, out_ref):
     qc, kvc = dq_ref.shape[1], dkv_ref.shape[1]
     quarter = db0_ref.shape[0]
@@ -430,10 +430,7 @@
         part = mm(db_ref[...], heads_ref[pl.ds(at, quarter), :], TN)
         wo = part if wo is None else wo + part
     out_ref[:, qc + kvc:2 * qc + kvc] = wo.astype(bf16)
-    half = first_ref.shape[0]
-    router = (
-        mm(first_ref[...], dlog_ref[:half, :], TN) + mm(second_ref[...], dlog_ref[half:, :], TN)
-    )
+    router = mm(normed2_ref[...], dlog_ref[...], TN)
     cols = router.shape[0]
     column = lambda row: jnp.transpose(jnp.broadcast_to(row.astype(f32), (8, cols)))[:, :1]
     pad = out_ref.shape[1] - (2 * qc + kvc) - router.shape[1] - 2
@@ -457,7 +454,7 @@
             num_scalar_prefetch=1,
             grid=(6,),
             in_specs=[block(normed1), whole(dq), whole(dkv), *map(block, dbs), whole(heads),
-                      *map(block, normed2), whole(d_logits), block(gain2), block(gain),
+                      block(normed2), whole(d_logits), block(gain2), block(gain),
                       *map(lines, ws)],
             out_specs=pl.BlockSpec((cols, lanes), lambda s, o: (s, 0)),
         ),
@@ -465,12 +462,19 @@
         compiler_params=params(36),
         cost_estimate=takes(13),
         name="dense_grad",
-    )(order, normed1, dq, dkv, *dbs, heads, *normed2, d_logits, gain2, gain, *ws)
-
-
-def expert_kernel(sources, cap, experts, base_ref, *refs):
-    x_refs, refs = refs[:2 * sources], refs[2 * sources:]
-    c_refs, refs = refs[:sources], refs[sources:]
+    )(order, normed1, dq, dkv, *dbs, heads, normed2, d_logits, gain2, gain, *ws)
+
+
+def expert_kernel(pieces, cap, experts, base_ref, *refs):
+    sources = len(pieces)
+    x_refs = []
+    for n in pieces:
+        x_refs.append(refs[:n])
+        refs = refs[n:]
+    c_refs = []
+    for n in pieces:
+        c_refs.append(refs[:n])
+        refs = refs[n:]
     router_ref, wg_ref, wu_ref, wd_ref = refs[:4]
     refs = refs[-(4 * sources + 5 + 5):]
     out_refs, refs = refs[:2 * sources], refs[2 * sources:]
@@ -479,23 +483,24 @@
      mix_ref, rank_ref, dmix_ref, so_ref, sd_ref) = refs
     e = pl.program_id(0)
     local = pl.num_programs(0)
-    half = x_refs[0].shape[0]
-    quarter = 2 * half
-    extra = c_refs[0].shape[0] - quarter
+    quarter = sum(x_ref.shape[0] for x_ref in x_refs[0])
+    half = quarter // 2
+    extra = sum(c_ref.shape[0] for c_ref in c_refs[0]) - quarter
     slots = so_ref.shape[1]
     base = base_ref[0]
 
     @pl.when(e == 0)
     def _():
         for s in range(sources):
-            tail = c_refs[s][quarter:, :].astype(f32)
+            end = c_refs[s][-1]
+            tail = end[end.shape[0] - extra:, :].astype(f32)
             rank = jnp.concatenate(
                 [tail[:, j * quarter:(j + 1) * quarter] for j in range(-(-experts // extra))],
                 axis=0,
             )[:experts].astype(i32)
             rank_ref[s] = rank
             logits = jnp.concatenate(
-                [mm(router_ref[...], x_refs[2 * s + j][...], NT) for j in range(2)], axis=1
+                [mm(router_ref[...], x_ref[...], NT) for x_ref in x_refs[s]], axis=1
             )
             chosen = rank >= 0
             logits = jnp.where(chosen, logits, NEG)
@@ -511,10 +516,13 @@
         picks.append(pick)
         mixes.append(jnp.sum(pick * mix_ref[s, pl.ds(base + e, 1), :], axis=1, keepdims=True))
         pick = pick.astype(bf16)
-        xs_ref[0, s * cap:(s + 1) * cap, :] = (
-            mm(pick[:, :half], x_refs[2 * s][...]) + mm(pick[:, half:], x_refs[2 * s + 1][...])
+        n = quarter // pieces[s]
+        xs_ref[0, s * cap:(s + 1) * cap, :] = sum(
+            mm(pick[:, j * n:(j + 1) * n], x_ref[...]) for j, x_ref in enumerate(x_refs[s])
         ).astype(bf16)
-        cs_ref[0, s * cap:(s + 1) * cap, :] = mm(pick, c_refs[s][:quarter, :]).astype(bf16)
+        cs_ref[0, s * cap:(s + 1) * cap, :] = sum(
+            mm(pick[:, j * n:(j + 1) * n], c_ref[:n, :]) for j, c_ref in enumerate(c_refs[s])
+        ).astype(bf16)
     mix = jnp.concatenate(mixes, axis=0)
     xs, cs = xs_ref[0], cs_ref[0]
     gate, up = mm(xs, wg_ref[0]), mm(xs, wu_ref[0])
@@ -558,7 +566,7 @@
                 out_refs[2 * s + j][...] = mm(part, so_ref[s]).astype(bf16)
                 back_refs[2 * s + j][:half, :] = mm(part, sd_ref[s]).astype(bf16)
             row = lax.broadcasted_iota(i32, (extra, quarter), 0)
-            sums = [jnp.zeros((extra, quarter), f32) for _ in range(x_refs[0].shape[1] // quarter)]
+            sums = [jnp.zeros((extra, quarter), f32) for _ in range(x_refs[0][0].shape[1] // quarter)]
             for j in range(count):
                 line = dmix_ref[s, j:j + 1, :]
                 for piece in range(len(sums)):
@@ -570,13 +578,16 @@
 
 
 def expert_call(base, xs, cs, router_t, wg, wu, wd, cap, at, of, held=None):
-    sources = len(cs)
+    sources = len(xs)
     experts = router_t.shape[0]
     local, width, hidden = wg.shape
-    half = xs[0][0].shape[0]
-    quarter = 2 * half
-    xs = [part for halves in xs for part in halves]
-    rows = [half] * (2 * sources) + [half, half + 2 * (cs[0].shape[0] - quarter)] * sources
+    quarter = sum(part.shape[0] for part in xs[0])
+    half = quarter // 2
+    pieces = tuple(len(parts) for parts in xs)
+    extra = sum(part.shape[0] for part in cs[0]) - quarter
+    xs = [part for parts in xs for part in parts]
+    cs = [part for parts in cs for part in parts]
+    rows = [half] * (2 * sources) + [half, half + 2 * extra] * sources
     sizes = (width, width, hidden, hidden, hidden)
     whole = lambda shape: pl.BlockSpec(shape, lambda e, b: (0,) * len(shape))
     slot_spec = lambda n: pl.BlockSpec((1, sources * cap, n), lambda e, b: (e, at, 0))
@@ -595,7 +606,7 @@
         args += list(held)
         in_specs += [pl.BlockSpec(memory_space=pl.ANY)] * 5
     outs = pl.pallas_call(
-        functools.partial(expert_kernel, sources, cap, experts),
+        functools.partial(expert_kernel, pieces, cap, experts),
         grid_spec=pltpu.PrefetchScalarGridSpec(
             num_scalar_prefetch=1,
             grid=(local,),
@@ -668,22 +679,12 @@
     )(order, a, b)
 
 
-def norm_two_kernel(at_ref, x_ref, keep_ref, came_ref, far_ref, gain_ref,
-                    middle_ref, first_ref, second_ref):
-    step = pl.program_id(0)
+def norm_two_kernel(at_ref, x_ref, keep_ref, came_ref, far_ref, gain_ref, middle_ref, out_ref):
     branch = keep_ref[...].astype(f32) + came_ref[...].astype(f32) + far_ref[...].astype(f32)
     middle = x_ref[...].astype(f32) + branch
     middle_ref[...] = middle
     inv = lax.rsqrt(jnp.mean(middle * middle, axis=-1, keepdims=True) + EPS)
-    normed = (middle * inv * gain_ref[...].astype(f32)).astype(bf16)
-
-    @pl.when(step < pl.num_programs(0) // 2)
-    def _():
-        first_ref[...] = normed
-
-    @pl.when(step >= pl.num_programs(0) // 2)
-    def _():
-        second_ref[...] = normed
+    out_ref[...] = (middle * inv * gain_ref[...].astype(f32)).astype(bf16)
 
 
 def norm_two_call(t_rank, x, keep, came, far, gain):
@@ -699,16 +700,11 @@
                 pl.BlockSpec((rb, width), lambda s, t: (4 * t[0] + s, 0)), row, row, row,
                 pl.BlockSpec((1, width), lambda s, t: (0, 0)),
             ],
-            out_specs=[
-                row,
-                pl.BlockSpec((rb, width), lambda s, t: (jnp.minimum(s, 1), 0)),
-                pl.BlockSpec((rb, width), lambda s, t: (jnp.maximum(s - 2, 0), 0)),
-            ],
+            out_specs=[row, row],
         ),
         out_shape=[
             jax.ShapeDtypeStruct((quarter, width), f32),
-            jax.ShapeDtypeStruct((quarter // 2, width), bf16),
-            jax.ShapeDtypeStruct((quarter // 2, width), bf16),
+            jax.ShapeDtypeStruct((quarter, width), bf16),
         ],
         compiler_params=params(12),
         cost_estimate=takes(3),
@@ -1008,7 +1004,7 @@
         grads_from = []
         for _ in range(n_dp // 2 - 1):
             a, b = lax.ppermute(a, "dp", ahead), lax.ppermute(b, "dp", behind)
-            grads_from.append((a, b))
+            grads_from.append(((a,), (b,)))
         stage = [after(g, zero) for g in grads_from]
     else:
         stage = [zero] * 3
@@ -1028,7 +1024,7 @@
         q, k, v, seg_col, seg_row, w_output, held=(heads, lse),
     )
     came_b = jnp.concatenate([to_core(send_b[:QB]), to_core(send_b[QB:])], axis=0)
-    middle, *normed2 = norm_two_call(
+    middle, normed2 = norm_two_call(
         own_at + stage[1], layer_input, keep_b, came_b, far, norm2_gain[None, :]
     )
 
@@ -1038,8 +1034,7 @@
     )
 
     def own_mixing(rows):
-        logits = jnp.concatenate([mm(router_t, r, NT) for r in rows], axis=1)
-        return jax.nn.softmax(jnp.where(hot_t, logits, -jnp.inf), axis=0)
+        return jax.nn.softmax(jnp.where(hot_t, mm(router_t, rows, NT), -jnp.inf), axis=0)
 
     def core_sum(parts, wait):
         send, keep = parts
@@ -1052,36 +1047,34 @@
         return keep.astype(f32) + came.astype(f32) + to_chip(away).astype(f32) + wait
 
     if ringed:
-        own = tuple(normed2)
-        step = lambda rows, way: tuple(lax.ppermute(r, "dp", way) for r in rows)
-        xs = [step(own, ahead), step(own, behind)]
-        (out_own,), (back_own,), held = run(base, [own], [payload], n_dp - 1, n_dp, None)
+        step = lambda rows, way: (lax.ppermute(rows, "dp", way),)
+        xs = [step(normed2, ahead), step(normed2, behind)]
+        (out_own,), (back_own,), held = run(base, [(normed2,)], [(payload,)], n_dp - 1, n_dp, None)
         outs, backs, last = [], [], out_own
         cut = payload.shape[0] // 32 * 16
         for j in range(n_dp // 2):
             cs = grads_from[j]
             if j < n_dp // 2 - 1:
                 at = j
-                a, b = after(last, xs)
+                (a,), (b,) = after(last, xs)
                 if j < n_dp // 2 - 2:
                     later = [step(a, ahead), step(b, behind)]
                 else:
-                    later = [step(a[:1], ahead) + step(b[1:], behind)]
+                    later = [step(a[:quarter // 2], ahead) + step(b[quarter // 2:], behind)]
             else:
                 at = n_dp - 2
-            wait = after(grads_from[-1], zero) if j == n_dp // 2 - 2 else zero
-            if j == max(n_dp // 2 - 3, 0):
-                a, b = after(last, grads_from[-1])
+            if j == n_dp // 2 - 2:
+                (a,), (b,) = after(last, grads_from[-1])
                 a, b = lax.ppermute(a[:cut], "dp", ahead), lax.ppermute(b[cut:], "dp", behind)
-                grads_from.append((jnp.concatenate([a, b], axis=0),))
-            o, b, held = run(base + wait, xs, cs, at, n_dp, held)
+                grads_from.append(((a, b),))
+            o, b, held = run(base, xs, cs, at, n_dp, held)
             outs.append(o)
             backs.append(b)
             last, xs = o, later
         back = RingSum(back_own, backs, n_dp)
         back.round()
         sums = back.round(mark(backs[-1][0][0]))
-        mix_t = own_mixing(after(sums, own))
+        mix_t = own_mixing(after(sums, normed2))
         grad_of = lambda i, j: weight_grad_call(
             quarters + after(sums, zero), held[i], held[j]
         )
@@ -1101,12 +1094,12 @@
         routed = back.terms()
     else:
         grads_all = lax.all_gather(payload, "dp", axis=0)
-        rows_all = lax.all_gather(jnp.concatenate(normed2, axis=0), "dp", axis=0)
+        rows_all = lax.all_gather(normed2, "dp", axis=0)
         halves = lambda a: (a[:quarter // 2], a[quarter // 2:])
 
         def two(sums, pair_rows):
             x, c = pair_rows
-            o, b, held = run(base, [halves(x[0]), halves(x[1])], [c[0], c[1]], 0, 2, None)
+            o, b, held = run(base, [(x[0],), (x[1],)], [(c[0],), (c[1],)], 0, 2, None)
             grads = [
                 list(weight_grad_call(quarters, held[i], held[j], i == 2))
                 for i, j in ((0, 3), (0, 4), (2, 1))
@@ -1169,23 +1162,25 @@
         *common, db_other, db_cross, w_output,
         cos, sin, held=(dq, dk, dv),
     )
-    sums = zero
-    for j in steps[2:]:
-        out_a, out_b, sums = out_step(out_a, out_b, j, zero_of(dkv))
     up_grad = chip_sum(up_sum, zero_of(dkv))
     packed_dense = dense_grad_call(
-        jnp.stack([t_rank, mate, other, cross]).astype(i32) + after(sums, zero)
-        + zero_of(up_grad).astype(i32),
+        jnp.stack([t_rank, mate, other, cross]).astype(i32)
+        + (zero_of(out_a) + zero_of(out_b)).astype(i32),
         normed1, dq, dkv, (db_own, db_mate, db_other, db_cross), heads, normed2, d_logits,
         second_gain_part, norm1_gain[None, :], (w_query, w_key, w_value),
     )
     down_sum = core_sum(down_parts, zero_of(packed_dense))
     send, keep = qkv_back_call(
-        pairs_of(cross, mate, other, t_rank) + after(packed_dense, zero),
+        pairs_of(cross, mate, other, t_rank) + after(packed_dense, zero)
+        + zero_of(up_grad).astype(i32),
         dq, dkv, w_query, w_key, w_value,
     )
     came = to_core(send)
-    sum_in = add_low(keep[:quarter], came[:quarter])
+    for j in steps[2:]:
+        out_a, out_b, sums = out_step(out_a, out_b, j, mark(keep))
+    sum_in = add_low(
+        keep[:quarter], came[:quarter], zero_of(sums[0]) if ringed else 0.0
+    )
     far = to_chip(sum_in)
     down_grad = chip_sum(down_sum, zero_of(sum_in))
 

time: 745 us -> 720 us (0.966)
  waiting for transfers between devices: 184 us -> 163 us
    ppermute x14 -> x8, waiting for transfers between devices: 57.9 us -> 36.9 us  [per_device(): step = lambda rows, way: (lax.ppermute(rows, 'dp', way),)]
    ppermute x8, waiting for transfers between devices: 14.5 us -> 23.4 us  [to_chip(): return lax.ppermute(a, 'tensor', CHIP)]
    unnamed x256 -> x251, local copies, waits for them, and re-layouts: 51.4 us -> 52.9 us
  transfers between devices with their start and end apart: 63 -> 57, of which waited for: 22 -> 18; matrix products, arithmetic and copies ran while one was open for 7% -> 8% of each run, Pallas kernels for 49% -> 49%
where the time goes in v3:
time: 720 us; the launch traced here: 715 us
  Pallas kernels  358 us (50%)
  waiting for transfers between devices  163 us (23%)
  local copies, waits for them, and re-layouts  79.3 us (11%)
  starting transfers between devices  49.4 us (7%)
  other arithmetic  35.5 us (5%)
  between operations  29.3 us (4%)
    pallas_call x5, Pallas kernels, expert_call(): pl.pallas_call(functools.partial(expert_kernel, pieces, cap, experts), gr...  149 us
    pallas_call x2, Pallas kernels, attend_back_call(): pl.pallas_call(functools.partial(attend_back_kernel, last), grid_spec=plt...  54.8 us
    unnamed x251, local copies, waits for them, and re-layouts  52.9 us
    pallas_call x3, Pallas kernels, weight_grad_call(): pl.pallas_call(weight_grad_kernel, grid_spec=pltpu.PrefetchScalarGridSpec...  48 us
    ppermute x6, waiting for transfers between devices, out_step(): return (lax.ppermute(a, 'dp', ahead), lax.ppermute(b, 'dp', behind), (a, b))  45 us
    pallas_call x2, Pallas kernels, attend_call(): pl.pallas_call(attend_kernel, grid_spec=pltpu.PrefetchScalarGridSpec(num_...  39.2 us
    ppermute x8, waiting for transfers between devices, per_device(): step = lambda rows, way: (lax.ppermute(rows, 'dp', way),)  36.9 us
    ppermute x14, waiting for transfers between devices, round(): held[way] = lax.ppermute(t, 'dp', self.ways[way])  24.9 us
  transfers between devices with their start and end apart: 57, of which 18 were waited for; matrix products, arithmetic and copies ran while one was open for 8% of the time, Pallas kernels for 49%

profile of v3, /device:TPU:0, one launch (start us, length us, event | category | flops | bytes accessed | tf_op | source)
XLA Modules:
  0.0 714.7 jit_solution(5595141747502746069)
XLA Ops:
  8.3 1.7 maximum_maximum_fusion.refs_1_
  10.0 3.1 collective-permute-start
  13.2 12.9 %norm_qkv.1 = (bf16[2048,1536]{1,0:T(8,128)(2,1)}, bf16[6,2048,64]{2,1,0:T(8,128)(2,1)}, bf16[2,2048,64]{2,1,0:T(8,128)(2,1)S(1)}, bf16[2,2048,64]{2,1,0:T(8,128)(2,1)S(1)}, bf16[2,64,2048]{2,1,0:T(8,128)(2,1)S(1)}) custom-call(bf16[2048,1536]{1,0:T(8,128)(2,1)} %x_ref.5, bf16[1,1536]{1,0:T(2,128)(2,1)S(1)} %broadcast_in_dim.48.gain_ref, ...), custom_call_target="tpu_custom_call" | custom-call | flops 114147000320 | bytes 1000000 | tf_op jit(solution)/shard_map/norm_qkv/pallas_call | solution.py:98
  30.8 23.0 %attend.2 = (bf16[2048,384]{1,0:T(8,128)(2,1)}, f32[8,2048]{1,0:T(8,128)}, bf16[512,1536]{1,0:T(8,128)(2,1)}, bf16[512,1536]{1,0:T(8,128)(2,1)}) custom-call(s32[4]{0:T(128)} %pad_add_fusion.1.order_ref, bf16[6,2048,64]{2,1,0:T(8,128)(2,1)} %get-tuple-element.132.q_ref, bf16[2,2048,64]{2,1,0:T(8,128)(2,1)} %copy-done.5, bf16[2,2048,64]{2,1,0:T(8,128)(2,1)} %copy-done.8, ...), custom_call_target="tpu_custom_call" | custom-call | flops 1152999936 | bytes 1000000 | tf_op jit(solution)/shard_map/attend/pallas_call | solution.py:212
  54.6 2.0 collective-permute-start.1
  57.5 3.0 add_convert_fusion.5
  60.5 16.1 %attend.3 = (bf16[2048,384]{1,0:T(8,128)(2,1)}, f32[8,2048]{1,0:T(8,128)}, bf16[512,1536]{1,0:T(8,128)(2,1)}, bf16[512,1536]{1,0:T(8,128)(2,1)}) custom-call(s32[4]{0:T(128)} %pad_add_fusion.order_ref, bf16[6,2048,64]{2,1,0:T(8,128)(2,1)} %get-tuple-element.132.q_ref, bf16[2,2048,64]{2,1,0:T(8,128)(2,1)} %copy-done.5, ...), custom_call_target="tpu_custom_call", output_to_operand_aliasing={{0}: (7, {}), {1}: (8, {})} | custom-call | flops 1152999936 | bytes 1000000 | tf_op jit(solution)/shard_map/attend/pallas_call | solution.py:212
  76.7 2.4 fusion.12
  79.6 13.4 %collective-permute-done.1.refs_2_ = bf16[528,1536]{1,0:T(8,128)(2,1)} collective-permute-done((bf16[528,1536]{1,0:T(8,128)(2,1)}, bf16[528,1536]{1,0:T(8,128)(2,1)}, u32[]{:S(2)}, u32[]{:S(2)}) %collective-permute-start.1) | collective-permute-done | bytes 1622048 | tf_op jit(solution)/shard_map/ppermute | solution.py:1006
  97.8 2.8 copy-done.34
  103.6 1.7 copy-done.66
  107.3 22.3 %experts.5 = (bf16[256,1536]{1,0:T(8,128)(2,1)}, bf16[256,1536]{1,0:T(8,128)(2,1)}, bf16[256,1536]{1,0:T(8,128)(2,1)}, bf16[288,1536]{1,0:T(8,128)(2,1)}, bf16[4...) custom-call(s32[1]{0:T(128)} %bitcast.13.base_ref, ...), custom_call_target="tpu_custom_call" | custom-call | flops 26518999040 | bytes 1000000 | tf_op jit(solution)/shard_map/experts/pallas_call | solution.py:608
  129.6 35.6 %collective-permute-done.8.refs_0_ = bf16[512,1536]{1,0:T(8,128)(2,1)} collective-permute-done((bf16[512,1536]{1,0:T(8,128)(2,1)S(1)}, bf16[512,1536]{1,0:T(8,128)(2,1)}, u32[]{:S(2)}, u32[]{:S(2)}) %collective-permute-start.8) | collective-permute-done | bytes 1572896 | tf_op jit(solution)/shard_map/ppermute | solution.py:1050
  169.6 34.2 %experts.6 = (bf16[256,1536]{1,0:T(8,128)(2,1)}, bf16[256,1536]{1,0:T(8,128)(2,1)}, bf16[256,1536]{1,0:T(8,128)(2,1)}, bf16[256,1536]{1,0:T(8,128)(2,1)}, bf16[2...) custom-call(s32[1]{0:T(128)} %bitcast.13.base_ref, ...), custom_call_target="tpu_custom_call", output_to_operand_aliasing={{8}: (9, {}), {9}: (10, {}), {10}: (11, {}), {11}: (12, {})... | custom-call | flops 39202000896 | bytes 1000000 | tf_op jit(solution)/shard_map/experts/pallas_call | solution.py:608
  203.8 1.6 collective-permute-start.12
  205.9 34.5 %experts.7 = (bf16[256,1536]{1,0:T(8,128)(2,1)}, bf16[256,1536]{1,0:T(8,128)(2,1)}, bf16[256,1536]{1,0:T(8,128)(2,1)}, bf16[256,1536]{1,0:T(8,128)(2,1)}, bf16[2...) custom-call(s32[1]{0:T(128)} %bitcast.13.base_ref, ...), custom_call_target="tpu_custom_call", output_to_operand_aliasing={{8}: (9, {}), {9}: (10, {}), {10}: (11, {}), {11}: (12, {})... | custom-call | flops 39202000896 | bytes 1000000 | tf_op jit(solution)/shard_map/experts/pallas_call | solution.py:608
  241.5 1.6 collective-permute-start.18
  246.1 1.6 collective-permute-start.14
  249.4 34.6 %experts.8 = (bf16[256,1536]{1,0:T(8,128)(2,1)}, bf16[256,1536]{1,0:T(8,128)(2,1)}, bf16[256,1536]{1,0:T(8,128)(2,1)}, bf16[256,1536]{1,0:T(8,128)(2,1)}, bf16[2...) custom-call(s32[1]{0:T(128)} %bitcast.13.base_ref, ...), custom_call_target="tpu_custom_call", output_to_operand_aliasing={{8}: (9, {}), {9}: (10, {}), {10}: (11, {}), {11}: (12, {})... | custom-call | flops 39202000896 | bytes 1000000 | tf_op jit(solution)/shard_map/experts/pallas_call | solution.py:608
  284.0 1.6 collective-permute-start.21
  286.1 23.4 %experts.9 = (bf16[256,1536]{1,0:T(8,128)(2,1)}, bf16[256,1536]{1,0:T(8,128)(2,1)}, bf16[256,1536]{1,0:T(8,128)(2,1)}, bf16[288,1536]{1,0:T(8,128)(2,1)}, bf16[4...) custom-call(s32[1]{0:T(128)} %bitcast.13.base_ref, ...), custom_call_target="tpu_custom_call", output_to_operand_aliasing={{4}: (9, {}), {5}: (10, {}), {6}: (11, {}), {7}: (12, {}), ... | custom-call | flops 26518999040 | bytes 1000000 | tf_op jit(solution)/shard_map/experts/pallas_call | solution.py:608
  316.3 5.5 copy-done.71
  321.8 2.5 copy-done.83
  324.3 14.4 %weight_grad.3 = (bf16[2,4,384,512]{3,2,1,0:T(8,128)(2,1)S(1)}, bf16[2,4,384,512]{3,2,1,0:T(8,128)(2,1)S(1)}) custom-call(s32[4]{0:T(128)S(1)} %get-tuple-element.286.order_ref, bf16[4,1280,1536]{2,1,0:T(8,128)(2,1)S(1)} %copy-done.71, bf16[4,1280,512]{2,1,0:T(8,128)(2,1)S(1)} %copy-done.83), custom_call_target="tpu_custom_call" | custom-call | flops 20753999872 | bytes 1000000 | tf_op jit(solution)/shard_map/weight_grad/pallas_call | solution.py:658
  345.0 2.0 collective-permute-done.26
  348.2 1.6 collective-permute-start.32
  349.8 15.3 %weight_grad.4 = (bf16[2,4,384,512]{3,2,1,0:T(8,128)(2,1)}, bf16[2,4,384,512]{3,2,1,0:T(8,128)(2,1)S(1)}) custom-call(s32[4]{0:T(128)S(1)} %broadcast_add_fusion.order_ref, bf16[4,1280,1536]{2,1,0:T(8,128)(2,1)S(1)} %copy-done.71, bf16[4,1280,512]{2,1,0:T(8,128)(2,1)S(1)} %bitcast.91), custom_call_target="tpu_custom_call" | custom-call | flops 20753999872 | bytes 1000000 | tf_op jit(solution)/shard_map/weight_grad/pallas_call | solution.py:658
  369.7 13.7 %collective-permute-done.28 = bf16[288,1536]{1,0:T(8,128)(2,1)S(1)} collective-permute-done((bf16[288,1536]{1,0:T(8,128)(2,1)S(1)}, bf16[288,1536]{1,0:T(8,128)(2,1)S(1)}, u32[]{:S(2)}, u32[]{:S(2)}) %collective-permute-start.28) | collective-permute-done | bytes 884768 | tf_op jit(solution)/shard_map/ppermute | solution.py:931
  384.2 1.9 add_convert_fusion.4
  387.4 5.5 copy-done.72
  392.9 18.2 %weight_grad.5 = (bf16[2,4,512,384]{3,2,1,0:T(8,128)(2,1)}, bf16[2,4,512,384]{3,2,1,0:T(8,128)(2,1)S(1)}) custom-call(s32[4]{0:T(128)S(1)} %add_add_fusion.4.order_ref, bf16[4,1280,512]{2,1,0:T(8,128)(2,1)S(1)} %bitcast.89, bf16[4,1280,1536]{2,1,0:T(8,128)(2,1)S(1)} %copy-done.72), custom_call_target="tpu_custom_call" | custom-call | flops 20753999872 | bytes 1000000 | tf_op jit(solution)/shard_map/weight_grad/pallas_call | solution.py:658
  413.0 1.7 collective-permute-start.30
  415.4 7.3 %collective-permute-done.35 = bf16[4,384,512]{2,1,0:T(8,128)(2,1)S(1)} collective-permute-done((bf16[4,384,512]{2,1,0:T(8,128)(2,1)S(1)}, bf16[4,384,512]{2,1,0:T(8,128)(2,1)S(1)}, u32[]{:S(2)}, u32[]{:S(2)}) %collective-permute-start.35) | collective-permute-done | bytes 1572896 | tf_op jit(solution)/shard_map/ppermute | solution.py:948
  422.7 2.0 fusion.2
  426.2 5.4 collective-permute-done.30.refs_1_
  431.5 3.8 collective-permute-done.34.refs_5_.refs_8_
  435.4 3.9 middle_back.1
  439.3 1.7 copy-done.69
  443.3 1.8 collective-permute-start.38
  446.3 14.8 %collective-permute-done.36.a_ref = bf16[256,1536]{1,0:T(8,128)(2,1)S(1)} collective-permute-done((bf16[256,1536]{1,0:T(8,128)(2,1)S(1)}, bf16[256,1536]{1,0:T(8,128)(2,1)S(1)}, u32[]{:S(2)}, u32[]{:S(2)}) %collective-permute-start.36) | collective-permute-done | bytes 786464 | tf_op jit(solution)/shard_map/ppermute | solution.py:1137
  462.4 3.2 two_sums.3
  467.7 1.7 collective-permute-start.45
  470.8 14.9 %attend_back.2 = (bf16[2048,384]{1,0:T(8,128)(2,1)S(1)}, f32[2,2048,64]{2,1,0:T(8,128)S(1)}, f32[2,2048,64]{2,1,0:T(8,128)S(1)}) custom-call(s32[4]{0:T(128)S(1)} %fusion.9.order_ref, bf16[6,2048,64]{2,1,0:T(8,128)(2,1)S(1)} %copy-done, bf16[2,2048,64]{2,1,0:T(8,128)(2,1)S(1)} %copy-done.6, bf16[2,2048,64]{2,1,0:T(8,128)(2,1)S(1)} %copy-done.9, ...), custom_call_target="tpu_custom_call" | custom-call | flops 31131000832 | bytes 1000000 | tf_op jit(solution)/shard_map/attend_back/pallas_call | solution.py:353
  492.7 8.8 %collective-permute-done.40.a_ref = bf16[512,1536]{1,0:T(8,128)(2,1)S(1)} collective-permute-done((bf16[512,1536]{1,0:T(8,128)(2,1)}, bf16[512,1536]{1,0:T(8,128)(2,1)S(1)}, u32[]{:S(2)}, u32[]{:S(2)}) %collective-permute-start.40) | collective-permute-done | bytes 1572896 | tf_op jit(solution)/shard_map/ppermute | solution.py:1142
  508.6 7.8 %two_sums.4 = (bf16[512,1536]{1,0:T(8,128)(2,1)}, bf16[512,1536]{1,0:T(8,128)(2,1)}) custom-call(s32[1]{0:T(128)} %bitcast.35.wait_ref, bf16[512,1536]{1,0:T(8,128)(2,1)S(1)} %copy-done.43, bf16[512,1536]{1,0:T(8,128)(2,1)} %collective-permute-done.41.b_ref, bf16[256,1536]{1,0:T(8,128)(2,1)S(1)} %copy-done.81, bf16[256,1536]{1,0:T(8,128)(2,1)S(1)} %copy-done.82, ...), custom_call_target="tpu_custom_call" | custom-call | flops 4611999744 | bytes 1000000 | tf_op jit(solution)/shard_map/two_sums/pallas_call | solution.py:812
  518.5 3.1 add_convert_fusion.3
  521.6 1.7 collective-permute-start.47
  525.8 39.9 %attend_back.3 = (bf16[2048,384]{1,0:T(8,128)(2,1)S(1)}, bf16[2048,256]{1,0:T(8,128)(2,1)S(1)}) custom-call(s32[4]{0:T(128)S(1)} %fusion.10.order_ref, bf16[6,2048,64]{2,1,0:T(8,128)(2,1)} %get-tuple-element.132.q_ref, bf16[2,2048,64]{2,1,0:T(8,128)(2,1)S(1)} %copy-done.7, bf16[2,2048,64]{2,1,0:T(8,128)(2,1)S(1)} %copy-done.10, ...), custom_call_target="tpu_custom_call", output_to_operand_aliasing={{0}: (18, {})} | custom-call | flops 31131000832 | bytes 1000000 | tf_op jit(solution)/shard_map/attend_back/pallas_call | solution.py:353
  574.5 12.1 %dense_grad.1 = bf16[1536,1152]{1,0:T(8,128)(2,1)S(1)} custom-call(s32[4]{0:T(128)S(1)} %add_add_fusion.order_ref, bf16[2048,1536]{1,0:T(8,128)(2,1)} %get-tuple-element.232.n_ref, bf16[2048,384]{1,0:T(8,128)(2,1)S(1)} %get-tuple-element.237.dq_ref, bf16[2048,256]{1,0:T(8,128)(2,1)S(1)} %copy-done.58, bf16[512,1536]{1,0:T(8,128)(2,1)S(1)} %copy-done.18, ...), custom_call_target="tpu_custom_call" | custom-call | flops 14988999680 | bytes 1000000 | tf_op jit(solution)/shard_map/dense_grad/pallas_call | solution.py:451
  586.6 1.8 copy-done.15
  590.3 2.7 fusion.1
  594.8 9.0 %qkv_back.1 = (bf16[1024,1536]{1,0:T(8,128)(2,1)S(1)}, bf16[1024,1536]{1,0:T(8,128)(2,1)S(1)}) custom-call(s32[8]{0:T(128)S(1)} %add_add_fusion.3.order_ref, bf16[2048,384]{1,0:T(8,128)(2,1)S(1)} %copy-done.56, bf16[2048,256]{1,0:T(8,128)(2,1)S(1)} %copy-done.59, bf16[1536,384]{1,0:T(8,128)(2,1)S(1)} %copy-done.46, bf16[1536,128]{1,0:T(8,128)(2,1)S(1)} %copy-done.49, ...), custom_call_target="tpu_custom_call" | custom-call | flops 10376999936 | bytes 1000000 | tf_op jit(solution)/shard_map/qkv_back/pallas_call | solution.py:392
  605.2 3.3 two_sums.5
  614.3 3.0 fusion.3
  617.4 2.0 add_convert_fusion.1
  619.5 2.1 collective-permute-start.51
  621.6 36.0 %collective-permute-done.48.a_ref = bf16[512,1536]{1,0:T(8,128)(2,1)} collective-permute-done((bf16[512,1536]{1,0:T(8,128)(2,1)}, bf16[512,1536]{1,0:T(8,128)(2,1)}, u32[]{:S(2)}, u32[]{:S(2)}) %collective-permute-start.48) | collective-permute-done | bytes 1572896 | tf_op jit(solution)/shard_map/ppermute | solution.py:1142
  657.8 1.9 copy-done.68
  662.0 6.3 layer_out.1
  670.2 4.3 fusion
  674.5 13.0 %collective-permute-done.51.far_ref = bf16[512,1536]{1,0:T(8,128)(2,1)} collective-permute-done((bf16[512,1536]{1,0:T(8,128)(2,1)}, bf16[512,1536]{1,0:T(8,128)(2,1)}, u32[]{:S(2)}, u32[]{:S(2)}) %collective-permute-start.51) | collective-permute-done | bytes 1572896 | tf_op jit(solution)/shard_map/ppermute | solution.py:948
  687.5 2.8 copy-done.35
  690.3 6.6 input_back.1
  703.1 3.1 collective-permute-done.53
  (409 shorter events, 97.9 us)
Async XLA Ops:
  7.2 691.6 %reduce-scatter.2.cloned.1.call-start = ((), (), s32[]{:S(2)}) async-start(), calls=%async_computation.1 | async-start | bytes 3981312 | tf_op jit(solution)/shard_map/reduce_scatter | solution.py:1191
  10.0 43.8 %collective-permute-start = (bf16[528,1536]{1,0:T(8,128)(2,1)S(1)}, bf16[528,1536]{1,0:T(8,128)(2,1)}, u32[]{:S(2)}, u32[]{:S(2)}) collective-permute-start(bf16[528,1536]{1,0:T(8,128)(2,1)S(1)} %maximum_maximum_fusion.refs_1_), channel_id=1, source_target_pairs={{0,8},{8,16},{16,24},{24,28},{28,20},{20,12},{12,4},{4,0},{1,9},{9... | collective-permute-start | bytes 4866056 | tf_op jit(solution)/shard_map/ppermute | solution.py:1006
  13.1 40.8 %collective-permute-start.2 = (bf16[528,1536]{1,0:T(8,128)(2,1)S(1)}, bf16[528,1536]{1,0:T(8,128)(2,1)}, u32[]{:S(2)}, u32[]{:S(2)}) collective-permute-start(bf16[528,1536]{1,0:T(8,128)(2,1)S(1)} %maximum_maximum_fusion.refs_1_), channel_id=1, source_target_pairs={{8,0},{16,8},{24,16},{28,24},{20,28},{12,20},{4,12},{0,4},{9,1},{1... | collective-permute-start | bytes 4866056 | tf_op jit(solution)/shard_map/ppermute | solution.py:1006
  53.8 3.7 collective-permute-start.4
  54.6 38.4 %collective-permute-start.1 = (bf16[528,1536]{1,0:T(8,128)(2,1)}, bf16[528,1536]{1,0:T(8,128)(2,1)}, u32[]{:S(2)}, u32[]{:S(2)}) collective-permute-start(bf16[528,1536]{1,0:T(8,128)(2,1)} %collective-permute-done.refs_2_), channel_id=1, source_target_pairs={{0,8},{8,16},{16,24},{24,28},{28,20},{20,12},{12,4},{4,0},{1,9},{9... | collective-permute-start | bytes 4866056 | tf_op jit(solution)/shard_map/ppermute | solution.py:1006
  56.6 37.9 %collective-permute-start.3 = (bf16[528,1536]{1,0:T(8,128)(2,1)}, bf16[528,1536]{1,0:T(8,128)(2,1)}, u32[]{:S(2)}, u32[]{:S(2)}) collective-permute-start(bf16[528,1536]{1,0:T(8,128)(2,1)} %collective-permute-done.2.refs_3_), channel_id=1, source_target_pairs={{8,0},{16,8},{24,16},{28,24},{20,28},{12,20},{4,12},{0,4},{9,1},{1... | collective-permute-start | bytes 4866056 | tf_op jit(solution)/shard_map/ppermute | solution.py:1006
  60.5 37.2 %collective-permute-start.7 = (bf16[512,1536]{1,0:T(8,128)(2,1)}, bf16[512,1536]{1,0:T(8,128)(2,1)S(1)}, u32[]{:S(2)}, u32[]{:S(2)}) collective-permute-start(bf16[512,1536]{1,0:T(8,128)(2,1)} %add_convert_fusion.5), channel_id=1, source_target_pairs={{0,2},{2,0},{1,3},{3,1},{4,6},{6,4},{5,7},{7,5},{8,10},{10,8},{9,1... | collective-permute-start | bytes 4718600 | tf_op jit(solution)/shard_map/ppermute | solution.py:948
  79.0 17.5 %collective-permute-start.6 = (bf16[256,1536]{1,0:T(8,128)(2,1)}, bf16[256,1536]{1,0:T(8,128)(2,1)S(1)}, u32[]{:S(2)}, u32[]{:S(2)}) collective-permute-start(bf16[256,1536]{1,0:T(8,128)(2,1)} %get-tuple-element.291), channel_id=1, source_target_pairs={{0,1},{1,0},{2,3},{3,2},{4,5},{5,4},{6,7},{7,6},{8,9},{9,8},{10,11... | collective-permute-start | bytes 2359304 | tf_op jit(solution)/shard_map/ppermute | solution.py:944
  79.2 17.3 %collective-permute-start.5 = (bf16[256,1536]{1,0:T(8,128)(2,1)S(1)}, bf16[256,1536]{1,0:T(8,128)(2,1)}, u32[]{:S(2)}, u32[]{:S(2)}) collective-permute-start(bf16[256,1536]{1,0:T(8,128)(2,1)S(1)} %get-tuple-element.290), channel_id=1, source_target_pairs={{0,1},{1,0},{2,3},{3,2},{4,5},{5,4},{6,7},{7,6},{8,9},{9,8},{10,11... | collective-permute-start | bytes 2359304 | tf_op jit(solution)/shard_map/ppermute | solution.py:944
  94.5 145.9 %collective-permute-start.16 = (bf16[528,1536]{1,0:T(8,128)(2,1)}, bf16[528,1536]{1,0:T(8,128)(2,1)}, u32[]{:S(2)}, u32[]{:S(2)}) collective-permute-start(bf16[528,1536]{1,0:T(8,128)(2,1)} %collective-permute-done.1.refs_2_), channel_id=1, source_target_pairs={{0,8},{8,16},{16,24},{24,28},{28,20},{20,12},{12,4},{4,0},{1,9},{9... | collective-permute-start | bytes 4866056 | tf_op jit(solution)/shard_map/ppermute | solution.py:1006
  96.0 144.3 %collective-permute-start.17 = (bf16[528,1536]{1,0:T(8,128)(2,1)}, bf16[528,1536]{1,0:T(8,128)(2,1)}, u32[]{:S(2)}, u32[]{:S(2)}) collective-permute-start(bf16[528,1536]{1,0:T(8,128)(2,1)} %collective-permute-done.3.refs_3_), channel_id=1, source_target_pairs={{8,0},{16,8},{24,16},{28,24},{20,28},{12,20},{4,12},{0,4},{9,1},{1... | collective-permute-start | bytes 4866056 | tf_op jit(solution)/shard_map/ppermute | solution.py:1006
  105.2 60.0 %collective-permute-start.8 = (bf16[512,1536]{1,0:T(8,128)(2,1)S(1)}, bf16[512,1536]{1,0:T(8,128)(2,1)}, u32[]{:S(2)}, u32[]{:S(2)}) collective-permute-start(bf16[512,1536]{1,0:T(8,128)(2,1)S(1)} %get-tuple-element.213.refs_0_.normed2_ref), channel_id=1, source_target_pairs={{0,8},{8,16},{16,24},{24,28},{28,20},{20,12},{12,4},{4,0},{1,9},{9... | collective-permute-start | bytes 4718600 | tf_op jit(solution)/shard_map/ppermute | solution.py:1050
  106.8 59.6 %collective-permute-start.9 = (bf16[512,1536]{1,0:T(8,128)(2,1)S(1)}, bf16[512,1536]{1,0:T(8,128)(2,1)S(1)}, u32[]{:S(2)}, u32[]{:S(2)}) collective-permute-start(bf16[512,1536]{1,0:T(8,128)(2,1)S(1)} %get-tuple-element.213.refs_0_.normed2_ref), channel_id=1, source_target_pairs={{8,0},{16,8},{24,16},{28,24},{20,28},{12,20},{4,12},{0,4},{9,1},{1... | collective-permute-start | bytes 4718600 | tf_op jit(solution)/shard_map/ppermute | solution.py:1050
  167.6 36.2 %collective-permute-start.10 = (bf16[512,1536]{1,0:T(8,128)(2,1)}, bf16[512,1536]{1,0:T(8,128)(2,1)S(1)}, u32[]{:S(2)}, u32[]{:S(2)}) collective-permute-start(bf16[512,1536]{1,0:T(8,128)(2,1)} %collective-permute-done.8.refs_0_), channel_id=1, source_target_pairs={{0,8},{8,16},{16,24},{24,28},{28,20},{20,12},{12,4},{4,0},{1,9},{9... | collective-permute-start | bytes 4718600 | tf_op jit(solution)/shard_map/ppermute | solution.py:1050
  169.1 34.6 %collective-permute-start.11 = (bf16[512,1536]{1,0:T(8,128)(2,1)}, bf16[512,1536]{1,0:T(8,128)(2,1)}, u32[]{:S(2)}, u32[]{:S(2)}) collective-permute-start(bf16[512,1536]{1,0:T(8,128)(2,1)} %copy-done.117), channel_id=1, source_target_pairs={{8,0},{16,8},{24,16},{28,24},{20,28},{12,20},{4,12},{0,4},{9,1},{1... | collective-permute-start | bytes 4718600 | tf_op jit(solution)/shard_map/ppermute | solution.py:1050
  203.8 41.1 %collective-permute-start.12 = (bf16[512,1536]{1,0:T(8,128)(2,1)S(1)}, bf16[512,1536]{1,0:T(8,128)(2,1)}, u32[]{:S(2)}, u32[]{:S(2)}) collective-permute-start(bf16[512,1536]{1,0:T(8,128)(2,1)S(1)} %collective-permute-done.10.refs_0_), channel_id=1, source_target_pairs={{0,8},{8,16},{16,24},{24,28},{28,20},{20,12},{12,4},{4,0},{1,9},{9... | collective-permute-start | bytes 4718600 | tf_op jit(solution)/shard_map/ppermute | solution.py:1050
  205.4 39.5 %collective-permute-start.13 = (bf16[512,1536]{1,0:T(8,128)(2,1)}, bf16[512,1536]{1,0:T(8,128)(2,1)}, u32[]{:S(2)}, u32[]{:S(2)}) collective-permute-start(bf16[512,1536]{1,0:T(8,128)(2,1)} %collective-permute-done.11.refs_1_), channel_id=1, source_target_pairs={{8,0},{16,8},{24,16},{28,24},{20,28},{12,20},{4,12},{0,4},{9,1},{1... | collective-permute-start | bytes 4718600 | tf_op jit(solution)/shard_map/ppermute | solution.py:1050
  241.5 44.1 %collective-permute-start.18 = (bf16[256,1536]{1,0:T(8,128)(2,1)S(1)}, bf16[256,1536]{1,0:T(8,128)(2,1)}, u32[]{:S(2)}, u32[]{:S(2)}) collective-permute-start(bf16[256,1536]{1,0:T(8,128)(2,1)S(1)} %slice.200), channel_id=1, source_target_pairs={{0,8},{8,16},{16,24},{24,28},{28,20},{20,12},{12,4},{4,0},{1,9},{9... | collective-permute-start | bytes 2359304 | tf_op jit(solution)/shard_map/ppermute | solution.py:1068
  244.4 41.7 %collective-permute-start.19 = (bf16[272,1536]{1,0:T(8,128)(2,1)S(1)}, bf16[272,1536]{1,0:T(8,128)(2,1)}, u32[]{:S(2)}, u32[]{:S(2)}) collective-permute-start(bf16[272,1536]{1,0:T(8,128)(2,1)S(1)} %slice.201), channel_id=1, source_target_pairs={{8,0},{16,8},{24,16},{28,24},{20,28},{12,20},{4,12},{0,4},{9,1},{1... | collective-permute-start | bytes 2506760 | tf_op jit(solution)/shard_map/ppermute | solution.py:1068
  246.1 40.0 %collective-permute-start.14 = (bf16[256,1536]{1,0:T(8,128)(2,1)S(1)}, bf16[256,1536]{1,0:T(8,128)(2,1)}, u32[]{:S(2)}, u32[]{:S(2)}) collective-permute-start(bf16[256,1536]{1,0:T(8,128)(2,1)S(1)} %slice.198), channel_id=1, source_target_pairs={{0,8},{8,16},{16,24},{24,28},{28,20},{20,12},{12,4},{4,0},{1,9},{9... | collective-permute-start | bytes 2359304 | tf_op jit(solution)/shard_map/ppermute | solution.py:1050
  248.9 37.2 %collective-permute-start.15 = (bf16[256,1536]{1,0:T(8,128)(2,1)S(1)}, bf16[256,1536]{1,0:T(8,128)(2,1)}, u32[]{:S(2)}, u32[]{:S(2)}) collective-permute-start(bf16[256,1536]{1,0:T(8,128)(2,1)S(1)} %slice.199), channel_id=1, source_target_pairs={{8,0},{16,8},{24,16},{28,24},{20,28},{12,20},{4,12},{0,4},{9,1},{1... | collective-permute-start | bytes 2359304 | tf_op jit(solution)/shard_map/ppermute | solution.py:1050
  284.0 30.4 %collective-permute-start.21 = (bf16[288,1536]{1,0:T(8,128)(2,1)}, bf16[288,1536]{1,0:T(8,128)(2,1)S(1)}, u32[]{:S(2)}, u32[]{:S(2)}) collective-permute-start(bf16[288,1536]{1,0:T(8,128)(2,1)} %get-tuple-element.188), channel_id=1, source_target_pairs={{0,8},{8,16},{16,24},{24,28},{28,20},{20,12},{12,4},{4,0},{1,9},{9... | collective-permute-start | bytes 2654216 | tf_op jit(solution)/shard_map/ppermute | solution.py:931
  285.7 27.5 %collective-permute-start.22 = (bf16[256,1536]{1,0:T(8,128)(2,1)}, bf16[256,1536]{1,0:T(8,128)(2,1)S(1)}, u32[]{:S(2)}, u32[]{:S(2)}) collective-permute-start(bf16[256,1536]{1,0:T(8,128)(2,1)} %get-tuple-element.190), channel_id=1, source_target_pairs={{8,0},{16,8},{24,16},{28,24},{20,28},{12,20},{4,12},{0,4},{9,1},{1... | collective-permute-start | bytes 2359304 | tf_op jit(solution)/shard_map/ppermute | solution.py:931
  310.9 29.8 %collective-permute-start.20 = (bf16[256,1536]{1,0:T(8,128)(2,1)}, bf16[256,1536]{1,0:T(8,128)(2,1)S(1)}, u32[]{:S(2)}, u32[]{:S(2)}) collective-permute-start(bf16[256,1536]{1,0:T(8,128)(2,1)} %get-tuple-element.186), channel_id=1, source_target_pairs={{0,8},{8,16},{16,24},{24,28},{28,20},{20,12},{12,4},{4,0},{1,9},{9... | collective-permute-start | bytes 2359304 | tf_op jit(solution)/shard_map/ppermute | solution.py:931
  313.4 30.1 %collective-permute-start.25 = (bf16[256,1536]{1,0:T(8,128)(2,1)S(1)}, bf16[256,1536]{1,0:T(8,128)(2,1)S(1)}, u32[]{:S(2)}, u32[]{:S(2)}) collective-permute-start(bf16[256,1536]{1,0:T(8,128)(2,1)S(1)} %add_convert_fusion.15), channel_id=1, source_target_pairs={{8,0},{16,8},{24,16},{28,24},{20,28},{12,20},{4,12},{0,4},{9,1},{1... | collective-permute-start | bytes 2359304 | tf_op jit(solution)/shard_map/ppermute | solution.py:931
  313.9 33.2 %collective-permute-start.26 = (bf16[288,1536]{1,0:T(8,128)(2,1)S(1)}, bf16[288,1536]{1,0:T(8,128)(2,1)S(1)}, u32[]{:S(2)}, u32[]{:S(2)}) collective-permute-start(bf16[288,1536]{1,0:T(8,128)(2,1)S(1)} %copy-done.118), channel_id=1, source_target_pairs={{8,0},{16,8},{24,16},{28,24},{20,28},{12,20},{4,12},{0,4},{9,1},{1... | collective-permute-start | bytes 2654216 | tf_op jit(solution)/shard_map/ppermute | solution.py:931
  314.7 33.2 %collective-permute-start.24 = (bf16[288,1536]{1,0:T(8,128)(2,1)S(1)}, bf16[288,1536]{1,0:T(8,128)(2,1)S(1)}, u32[]{:S(2)}, u32[]{:S(2)}) collective-permute-start(bf16[288,1536]{1,0:T(8,128)(2,1)S(1)} %add_convert_fusion.10), channel_id=1, source_target_pairs={{0,8},{8,16},{16,24},{24,28},{28,20},{20,12},{12,4},{4,0},{1,9},{9... | collective-permute-start | bytes 2654216 | tf_op jit(solution)/shard_map/ppermute | solution.py:931
  339.9 44.2 %collective-permute-start.29 = (bf16[2,4,384,512]{3,2,1,0:T(8,128)(2,1)S(1)}, bf16[2,4,384,512]{3,2,1,0:T(8,128)(2,1)}, u32[]{:S(2)}, u32[]{:S(2)}) collective-permute-start(bf16[2,4,384,512]{3,2,1,0:T(8,128)(2,1)S(1)} %get-tuple-element.207), channel_id=1, source_target_pairs={{0,1},{1,0},{2,3},{3,2},{4,5},{5,4},{6,7},{7,6},{8,9},{9,8},{10,11... | collective-permute-start | bytes 9437192 | tf_op jit(solution)/shard_map/ppermute | solution.py:944
  341.9 24.9 %collective-permute-start.23 = (bf16[256,1536]{1,0:T(8,128)(2,1)}, bf16[256,1536]{1,0:T(8,128)(2,1)}, u32[]{:S(2)}, u32[]{:S(2)}) collective-permute-start(bf16[256,1536]{1,0:T(8,128)(2,1)} %add_convert_fusion.14), channel_id=1, source_target_pairs={{0,8},{8,16},{16,24},{24,28},{28,20},{20,12},{12,4},{4,0},{1,9},{9... | collective-permute-start | bytes 2359304 | tf_op jit(solution)/shard_map/ppermute | solution.py:931
  344.6 81.6 %collective-permute-start.31 = (bf16[256,1536]{1,0:T(8,128)(2,1)}, bf16[256,1536]{1,0:T(8,128)(2,1)S(1)}, u32[]{:S(2)}, u32[]{:S(2)}) collective-permute-start(bf16[256,1536]{1,0:T(8,128)(2,1)} %add_convert_fusion.13), channel_id=1, source_target_pairs={{8,0},{16,8},{24,16},{28,24},{20,28},{12,20},{4,12},{0,4},{9,1},{1... | collective-permute-start | bytes 2359304 | tf_op jit(solution)/shard_map/ppermute | solution.py:931
  347.3 36.1 %collective-permute-start.28 = (bf16[288,1536]{1,0:T(8,128)(2,1)S(1)}, bf16[288,1536]{1,0:T(8,128)(2,1)S(1)}, u32[]{:S(2)}, u32[]{:S(2)}) collective-permute-start(bf16[288,1536]{1,0:T(8,128)(2,1)S(1)} %add_convert_fusion.8), channel_id=1, source_target_pairs={{8,0},{16,8},{24,16},{28,24},{20,28},{12,20},{4,12},{0,4},{9,1},{1... | collective-permute-start | bytes 2654216 | tf_op jit(solution)/shard_map/ppermute | solution.py:931
  347.8 39.5 %slice-start = ((s8[5242880]{0:T(1024)(128)(4,1)}), s8[4194304]{0:T(1024)(128)(4,1)S(1)}, s32[]{:S(2)}) async-start(s8[5242880]{0:T(1024)(128)(4,1)} %bitcast.88), calls=%async_computation.2 | async-start | bytes 8388608
  348.2 78.0 %collective-permute-start.32 = (bf16[288,1536]{1,0:T(8,128)(2,1)S(1)}, bf16[288,1536]{1,0:T(8,128)(2,1)S(1)}, u32[]{:S(2)}, u32[]{:S(2)}) collective-permute-start(bf16[288,1536]{1,0:T(8,128)(2,1)S(1)} %add_convert_fusion.9), channel_id=1, source_target_pairs={{0,8},{8,16},{16,24},{24,28},{28,20},{20,12},{12,4},{4,0},{1,9},{9... | collective-permute-start | bytes 2654216 | tf_op jit(solution)/shard_map/ppermute | solution.py:931
  368.2 44.5 %collective-permute-start.27 = (bf16[256,1536]{1,0:T(8,128)(2,1)S(1)}, bf16[256,1536]{1,0:T(8,128)(2,1)S(1)}, u32[]{:S(2)}, u32[]{:S(2)}) collective-permute-start(bf16[256,1536]{1,0:T(8,128)(2,1)S(1)} %add_convert_fusion.12), channel_id=1, source_target_pairs={{0,8},{8,16},{16,24},{24,28},{28,20},{20,12},{12,4},{4,0},{1,9},{9... | collective-permute-start | bytes 2359304 | tf_op jit(solution)/shard_map/ppermute | solution.py:931
  383.7 30.9 %collective-permute-start.33 = (bf16[288,1536]{1,0:T(8,128)(2,1)S(1)}, bf16[288,1536]{1,0:T(8,128)(2,1)S(1)}, u32[]{:S(2)}, u32[]{:S(2)}) collective-permute-start(bf16[288,1536]{1,0:T(8,128)(2,1)S(1)} %add_convert_fusion.7), channel_id=1, source_target_pairs={{8,0},{16,8},{24,16},{28,24},{20,28},{12,20},{4,12},{0,4},{9,1},{1... | collective-permute-start | bytes 2654216 | tf_op jit(solution)/shard_map/ppermute | solution.py:931
  387.3 35.4 %collective-permute-start.35 = (bf16[4,384,512]{2,1,0:T(8,128)(2,1)S(1)}, bf16[4,384,512]{2,1,0:T(8,128)(2,1)S(1)}, u32[]{:S(2)}, u32[]{:S(2)}) collective-permute-start(bf16[4,384,512]{2,1,0:T(8,128)(2,1)S(1)} %bitcast.92), channel_id=1, source_target_pairs={{0,2},{2,0},{1,3},{3,1},{4,6},{6,4},{5,7},{7,5},{8,10},{10,8},{9,1... | collective-permute-start | bytes 4718600 | tf_op jit(solution)/shard_map/ppermute | solution.py:948
  413.0 18.6 %collective-permute-start.30 = (bf16[256,1536]{1,0:T(8,128)(2,1)S(1)}, bf16[256,1536]{1,0:T(8,128)(2,1)S(1)}, u32[]{:S(2)}, u32[]{:S(2)}) collective-permute-start(bf16[256,1536]{1,0:T(8,128)(2,1)S(1)} %add_convert_fusion.11), channel_id=1, source_target_pairs={{0,8},{8,16},{16,24},{24,28},{28,20},{20,12},{12,4},{4,0},{1,9},{9... | collective-permute-start | bytes 2359304 | tf_op jit(solution)/shard_map/ppermute | solution.py:931
  415.0 20.4 %collective-permute-start.34 = (bf16[288,1536]{1,0:T(8,128)(2,1)S(1)}, bf16[288,1536]{1,0:T(8,128)(2,1)S(1)}, u32[]{:S(2)}, u32[]{:S(2)}) collective-permute-start(bf16[288,1536]{1,0:T(8,128)(2,1)S(1)} %add_convert_fusion.6), channel_id=1, source_target_pairs={{8,0},{16,8},{24,16},{28,24},{20,28},{12,20},{4,12},{0,4},{9,1},{1... | collective-permute-start | bytes 2654216 | tf_op jit(solution)/shard_map/ppermute | solution.py:931
  441.0 29.6 %collective-permute-start.39 = (bf16[512,1536]{1,0:T(8,128)(2,1)S(1)}, bf16[512,1536]{1,0:T(8,128)(2,1)S(1)}, u32[]{:S(2)}, u32[]{:S(2)}) collective-permute-start(bf16[512,1536]{1,0:T(8,128)(2,1)S(1)} %get-tuple-element.214.dba_ref.db0_ref), channel_id=1, source_target_pairs={{0,1},{1,0},{2,3},{3,2},{4,5},{5,4},{6,7},{7,6},{8,9},{9,8},{10,11... | collective-permute-start | bytes 4718600 | tf_op jit(solution)/shard_map/ppermute | solution.py:944
  441.1 19.9 %collective-permute-start.36 = (bf16[256,1536]{1,0:T(8,128)(2,1)S(1)}, bf16[256,1536]{1,0:T(8,128)(2,1)S(1)}, u32[]{:S(2)}, u32[]{:S(2)}) collective-permute-start(bf16[256,1536]{1,0:T(8,128)(2,1)S(1)} %copy-done.120), channel_id=1, source_target_pairs={{0,8},{8,16},{16,24},{24,28},{28,20},{20,12},{12,4},{4,0},{1,9},{9... | collective-permute-start | bytes 2359304 | tf_op jit(solution)/shard_map/ppermute | solution.py:1137
  442.7 19.6 %collective-permute-start.37 = (bf16[256,1536]{1,0:T(8,128)(2,1)S(1)}, bf16[256,1536]{1,0:T(8,128)(2,1)S(1)}, u32[]{:S(2)}, u32[]{:S(2)}) collective-permute-start(bf16[256,1536]{1,0:T(8,128)(2,1)S(1)} %copy-done.119), channel_id=1, source_target_pairs={{8,0},{16,8},{24,16},{28,24},{20,28},{12,20},{4,12},{0,4},{9,1},{1... | collective-permute-start | bytes 2359304 | tf_op jit(solution)/shard_map/ppermute | solution.py:1137
  443.3 24.4 %collective-permute-start.38 = (bf16[256,1536]{1,0:T(8,128)(2,1)S(1)}, bf16[256,1536]{1,0:T(8,128)(2,1)S(1)}, u32[]{:S(2)}, u32[]{:S(2)}) collective-permute-start(bf16[256,1536]{1,0:T(8,128)(2,1)S(1)} %get-tuple-element.289), channel_id=1, source_target_pairs={{0,2},{2,0},{1,3},{3,1},{4,6},{6,4},{5,7},{7,5},{8,10},{10,8},{9,1... | collective-permute-start | bytes 2359304 | tf_op jit(solution)/shard_map/ppermute | solution.py:948
  445.1 73.4 %collective-permute-start.44 = (bf16[2,4,384,512]{3,2,1,0:T(8,128)(2,1)}, bf16[2,4,384,512]{3,2,1,0:T(8,128)(2,1)}, u32[]{:S(2)}, u32[]{:S(2)}) collective-permute-start(bf16[2,4,384,512]{3,2,1,0:T(8,128)(2,1)} %get-tuple-element.234), channel_id=1, source_target_pairs={{0,1},{1,0},{2,3},{3,2},{4,5},{5,4},{6,7},{7,6},{8,9},{9,8},{10,11... | collective-permute-start | bytes 9437192 | tf_op jit(solution)/shard_map/ppermute | solution.py:944
  465.6 35.8 %collective-permute-start.40 = (bf16[512,1536]{1,0:T(8,128)(2,1)}, bf16[512,1536]{1,0:T(8,128)(2,1)S(1)}, u32[]{:S(2)}, u32[]{:S(2)}) collective-permute-start(bf16[512,1536]{1,0:T(8,128)(2,1)} %get-tuple-element.223), channel_id=1, source_target_pairs={{0,8},{8,16},{16,24},{24,28},{28,20},{20,12},{12,4},{4,0},{1,9},{9... | collective-permute-start | bytes 4718600 | tf_op jit(solution)/shard_map/ppermute | solution.py:1142
  466.3 36.4 %collective-permute-start.41 = (bf16[512,1536]{1,0:T(8,128)(2,1)S(1)}, bf16[512,1536]{1,0:T(8,128)(2,1)}, u32[]{:S(2)}, u32[]{:S(2)}) collective-permute-start(bf16[512,1536]{1,0:T(8,128)(2,1)S(1)} %get-tuple-element.224), channel_id=1, source_target_pairs={{8,0},{16,8},{24,16},{28,24},{20,28},{12,20},{4,12},{0,4},{9,1},{1... | collective-permute-start | bytes 4718600 | tf_op jit(solution)/shard_map/ppermute | solution.py:1142
  467.7 23.0 %collective-permute-start.45 = (bf16[256,1536]{1,0:T(8,128)(2,1)S(1)}, bf16[256,1536]{1,0:T(8,128)(2,1)S(1)}, u32[]{:S(2)}, u32[]{:S(2)}) collective-permute-start(bf16[256,1536]{1,0:T(8,128)(2,1)S(1)} %get-tuple-element.288), channel_id=1, source_target_pairs={{0,2},{2,0},{1,3},{3,1},{4,6},{6,4},{5,7},{7,5},{8,10},{10,8},{9,1... | collective-permute-start | bytes 2359304 | tf_op jit(solution)/shard_map/ppermute | solution.py:948
  492.1 33.6 %collective-permute-start.46 = (bf16[512,1536]{1,0:T(8,128)(2,1)}, bf16[512,1536]{1,0:T(8,128)(2,1)}, u32[]{:S(2)}, u32[]{:S(2)}) collective-permute-start(bf16[512,1536]{1,0:T(8,128)(2,1)} %add_convert_fusion.2.dba_ref.db2_ref), channel_id=1, source_target_pairs={{0,1},{1,0},{2,3},{3,2},{4,5},{5,4},{6,7},{7,6},{8,9},{9,8},{10,11... | collective-permute-start | bytes 4718600 | tf_op jit(solution)/shard_map/ppermute | solution.py:944
  492.2 122.1 %collective-permute-start.54 = (bf16[2,4,512,384]{3,2,1,0:T(8,128)(2,1)}, bf16[2,4,512,384]{3,2,1,0:T(8,128)(2,1)}, u32[]{:S(2)}, u32[]{:S(2)}) collective-permute-start(bf16[2,4,512,384]{3,2,1,0:T(8,128)(2,1)} %get-tuple-element.247), channel_id=1, source_target_pairs={{0,1},{1,0},{2,3},{3,2},{4,5},{5,4},{6,7},{7,6},{8,9},{9,8},{10,11... | collective-permute-start | bytes 9437192 | tf_op jit(solution)/shard_map/ppermute | solution.py:944
  516.4 50.8 %collective-permute-start.42 = (bf16[512,1536]{1,0:T(8,128)(2,1)}, bf16[512,1536]{1,0:T(8,128)(2,1)S(1)}, u32[]{:S(2)}, u32[]{:S(2)}) collective-permute-start(bf16[512,1536]{1,0:T(8,128)(2,1)} %get-tuple-element.230), channel_id=1, source_target_pairs={{0,8},{8,16},{16,24},{24,28},{28,20},{20,12},{12,4},{4,0},{1,9},{9... | collective-permute-start | bytes 4718600 | tf_op jit(solution)/shard_map/ppermute | solution.py:1142
  517.0 52.5 %collective-permute-start.43 = (bf16[512,1536]{1,0:T(8,128)(2,1)}, bf16[512,1536]{1,0:T(8,128)(2,1)S(1)}, u32[]{:S(2)}, u32[]{:S(2)}) collective-permute-start(bf16[512,1536]{1,0:T(8,128)(2,1)} %get-tuple-element.231), channel_id=1, source_target_pairs={{8,0},{16,8},{24,16},{28,24},{20,28},{12,20},{4,12},{0,4},{9,1},{1... | collective-permute-start | bytes 4718600 | tf_op jit(solution)/shard_map/ppermute | solution.py:1142
  521.6 68.6 %collective-permute-start.47 = (bf16[4,384,512]{2,1,0:T(8,128)(2,1)}, bf16[4,384,512]{2,1,0:T(8,128)(2,1)}, u32[]{:S(2)}, u32[]{:S(2)}) collective-permute-start(bf16[4,384,512]{2,1,0:T(8,128)(2,1)} %bitcast.40), channel_id=1, source_target_pairs={{0,2},{2,0},{1,3},{3,1},{4,6},{6,4},{5,7},{7,5},{8,10},{10,8},{9,1... | collective-permute-start | bytes 4718600 | tf_op jit(solution)/shard_map/ppermute | solution.py:948
  525.8 46.2 %copy-start.18 = (bf16[512,1536]{1,0:T(8,128)(2,1)S(1)}, bf16[512,1536]{1,0:T(8,128)(2,1)}, u32[]{:S(2)}) copy-start(bf16[512,1536]{1,0:T(8,128)(2,1)} %copy-done.17) | copy-start | bytes 4718596
  525.8 46.2 %copy-start.21 = (bf16[512,1536]{1,0:T(8,128)(2,1)S(1)}, bf16[512,1536]{1,0:T(8,128)(2,1)}, u32[]{:S(2)}) copy-start(bf16[512,1536]{1,0:T(8,128)(2,1)} %copy-done.19) | copy-start | bytes 4718596
  525.8 46.1 %copy-start.33 = (bf16[1,1536]{1,0:T(2,128)(2,1)S(1)}, bf16[1,1536]{1,0:T(2,128)(2,1)}, u32[]{:S(2)}) copy-start(bf16[1,1536]{1,0:T(2,128)(2,1)} %copy-done.32) | copy-start | bytes 9220
  525.8 46.1 %copy-start.37 = (bf16[512,1536]{1,0:T(8,128)(2,1)S(1)}, bf16[512,1536]{1,0:T(8,128)(2,1)}, u32[]{:S(2)}) copy-start(bf16[512,1536]{1,0:T(8,128)(2,1)} %copy-done.36) | copy-start | bytes 4718596
  525.8 46.1 %copy-start.48 = (bf16[1536,128]{1,0:T(8,128)(2,1)S(1)}, bf16[1536,128]{1,0:T(8,128)(2,1)}, u32[]{:S(2)}) copy-start(bf16[1536,128]{1,0:T(8,128)(2,1)} %wk_ref.5) | copy-start | bytes 1179652
  525.8 46.1 %copy-start.51 = (bf16[1536,128]{1,0:T(8,128)(2,1)S(1)}, bf16[1536,128]{1,0:T(8,128)(2,1)}, u32[]{:S(2)}) copy-start(bf16[1536,128]{1,0:T(8,128)(2,1)} %wv_ref.5) | copy-start | bytes 1179652
  603.7 13.6 %collective-permute-start.50 = (bf16[1024,1536]{1,0:T(8,128)(2,1)S(1)}, bf16[1024,1536]{1,0:T(8,128)(2,1)S(1)}, u32[]{:S(2)}, u32[]{:S(2)}) collective-permute-start(bf16[1024,1536]{1,0:T(8,128)(2,1)S(1)} %get-tuple-element.245), channel_id=1, source_target_pairs={{0,1},{1,0},{2,3},{3,2},{4,5},{5,4},{6,7},{7,6},{8,9},{9,8},{10,11... | collective-permute-start | bytes 9437192 | tf_op jit(solution)/shard_map/ppermute | solution.py:944
  608.5 49.1 %collective-permute-start.48 = (bf16[512,1536]{1,0:T(8,128)(2,1)}, bf16[512,1536]{1,0:T(8,128)(2,1)}, u32[]{:S(2)}, u32[]{:S(2)}) collective-permute-start(bf16[512,1536]{1,0:T(8,128)(2,1)} %get-tuple-element.243), channel_id=1, source_target_pairs={{0,8},{8,16},{16,24},{24,28},{28,20},{20,12},{12,4},{4,0},{1,9},{9... | collective-permute-start | bytes 4718600 | tf_op jit(solution)/shard_map/ppermute | solution.py:1142
  611.5 46.3 %collective-permute-start.49 = (bf16[512,1536]{1,0:T(8,128)(2,1)}, bf16[512,1536]{1,0:T(8,128)(2,1)}, u32[]{:S(2)}, u32[]{:S(2)}) collective-permute-start(bf16[512,1536]{1,0:T(8,128)(2,1)} %get-tuple-element.244), channel_id=1, source_target_pairs={{8,0},{16,8},{24,16},{28,24},{20,28},{12,20},{4,12},{0,4},{9,1},{1... | collective-permute-start | bytes 4718600 | tf_op jit(solution)/shard_map/ppermute | solution.py:1142
  617.3 52.8 %collective-permute-start.55 = (bf16[4,512,384]{2,1,0:T(8,128)(2,1)}, bf16[4,512,384]{2,1,0:T(8,128)(2,1)}, u32[]{:S(2)}, u32[]{:S(2)}) collective-permute-start(bf16[4,512,384]{2,1,0:T(8,128)(2,1)} %fusion.3), channel_id=1, source_target_pairs={{0,2},{2,0},{1,3},{3,1},{4,6},{6,4},{5,7},{7,5},{8,10},{10,8},{9,1... | collective-permute-start | bytes 4718600 | tf_op jit(solution)/shard_map/ppermute | solution.py:948
  619.5 67.9 %collective-permute-start.51 = (bf16[512,1536]{1,0:T(8,128)(2,1)}, bf16[512,1536]{1,0:T(8,128)(2,1)}, u32[]{:S(2)}, u32[]{:S(2)}) collective-permute-start(bf16[512,1536]{1,0:T(8,128)(2,1)} %add_convert_fusion.1), channel_id=1, source_target_pairs={{0,2},{2,0},{1,3},{3,1},{4,6},{6,4},{5,7},{7,5},{8,10},{10,8},{9,1... | collective-permute-start | bytes 4718600 | tf_op jit(solution)/shard_map/ppermute | solution.py:948
  699.9 1.4 collective-permute-start.52
  701.3 4.9 collective-permute-start.53
  (118 other events, 1035.1 us)
Sparse Core Ops, SparseCore 0:
  589.7 100.3 reduce-scatter.1
